TPU v7x, 32 devices: a whole 2x2x4 slice. The times are simulated.
32 devices in a mesh: src: 8 (over y, x, core), rcv: 4 (over z).
Axes of the slice: x: 2, y: 2, z: 4, core: 2. Of those that a mesh axis runs over, the one named last changes fastest.
Arguments:
- src_spec: bfloat16 [2, 16, 256, 512], P(None, None, 'rcv', 'src'), may hold values from -6 to 6
- rcv_spec: bfloat16 [2, 16, 256, 1024], P(None, None, 'src', 'rcv'), may hold values from -6 to 6
- lag_table: int32 [16, 8192], replicated, may hold values from 0 to 511
- src_pos: int32 [512], P('src'), may hold values from 0 to 8191
- rcv_pos: int32 [1024], P('rcv'), may hold values from 0 to 8191
Outputs:
- panel_src: float32 [16, 2, 512, 256], P(None, None, ('src', 'rcv'))
- panel_rcv: float32 [16, 2, 256, 1024], P(None, None, 'src', 'rcv')
All inputs are finite; a program needn't handle non-finite values.
Results may differ from a plain program's by a relative error of at most 0.0035.
Values may be sent and summed in bfloat16 or wider, within the bound.
No kernel may reach another device: no remote copies, remote signals or barrier semaphores. Data moves between devices by JAX's collectives and lax.ppermute only.
A program may use at most 64 MiB of HBM per device.

v0:
```python
import math

import jax
import jax.numpy as jnp
from jax import lax
from jax.sharding import PartitionSpec as P

WIN = 8
SEGS = 2


def phase_table(freqs, lags, n_freq):
    index_mod = freqs[:, None, None] * jnp.transpose(lags)[None, :, :] % (2 * n_freq)
    angles = index_mod.astype(jnp.float32) * (math.pi / n_freq)
    return (jnp.cos(angles), jnp.sin(angles))


def cross_block(src_block, rcv_block):
    block_width = src_block.shape[2]
    src_five = src_block.reshape(2, SEGS, WIN, block_width, src_block.shape[3])
    rcv_five = rcv_block.reshape(2, SEGS, WIN, block_width, rcv_block.shape[3])
    swapped = jnp.stack([src_five[1], -src_five[0]])
    real_part = jnp.einsum(
        "cgwfs,cgwfr->gfsr", src_five, rcv_five, preferred_element_type=jnp.float32
    )
    imag_part = jnp.einsum(
        "cgwfs,cgwfr->gfsr", swapped, rcv_five, preferred_element_type=jnp.float32
    )
    floor_mod = jnp.maximum(jnp.sqrt(real_part * real_part + imag_part * imag_part), 1.0)
    stacked_re = (jnp.sum(real_part / floor_mod, axis=0) / SEGS).astype(jnp.bfloat16)
    stacked_im = (jnp.sum(imag_part / floor_mod, axis=0) / SEGS).astype(jnp.bfloat16)
    return (stacked_re, stacked_im)


def source_slant(stacked_re, stacked_im, rcv_cos, rcv_sin, src_cos, src_sin, factor):
    left_op = jnp.concatenate([stacked_re, stacked_im], axis=2)
    cos_b = rcv_cos.astype(jnp.bfloat16)
    sin_b = rcv_sin.astype(jnp.bfloat16)
    upper_half = jnp.concatenate([cos_b, sin_b], axis=2)
    bottom = jnp.concatenate([-sin_b, cos_b], axis=2)
    right_op = jnp.concatenate([upper_half, bottom], axis=1)
    sums = jnp.einsum("fsk,fkq->fsq", left_op, right_op, preferred_element_type=jnp.float32)
    n_slow = rcv_cos.shape[2]
    sum_re = sums[:, :, :n_slow]
    sum_im = sums[:, :, n_slow:]
    panel_re = (sum_re * src_cos + sum_im * src_sin) * factor
    panel_im = (sum_im * src_cos - sum_re * src_sin) * factor
    return jnp.transpose(jnp.stack([panel_re, panel_im]), (3, 0, 2, 1))


def receiver_right(src_cos_b, src_sin_b):
    upper_half = jnp.concatenate([src_cos_b, -src_sin_b], axis=2)
    bottom = jnp.concatenate([src_sin_b, src_cos_b], axis=2)
    return jnp.concatenate([upper_half, bottom], axis=1)


def receiver_sums(left_op, right_op):
    return jnp.einsum("fkr,fkq->fqr", left_op, right_op, preferred_element_type=jnp.float32)


def receiver_outer(sums, rcv_cos, rcv_sin, factor):
    n_slow = rcv_cos.shape[2]
    cos_t = jnp.transpose(rcv_cos, (0, 2, 1))
    sin_t = jnp.transpose(rcv_sin, (0, 2, 1))
    sum_re = sums[:, :n_slow, :]
    sum_im = sums[:, n_slow:, :]
    panel_re = (sum_re * cos_t - sum_im * sin_t) * factor
    panel_im = (sum_re * sin_t + sum_im * cos_t) * factor
    return jnp.transpose(jnp.stack([panel_re, panel_im]), (2, 0, 1, 3))


def per_device(src_spec, rcv_spec, lag_table, src_pos, rcv_pos):
    src_full = lax.all_gather(src_spec, "rcv", axis=2, tiled=True)
    n_freq = src_full.shape[2]
    src_dev = src_full.shape[3]
    rcv_dev = rcv_spec.shape[3]
    n_slow = lag_table.shape[0]
    n_src = lax.axis_size("src")
    n_rcv = lax.axis_size("rcv")
    src_factor = 1.0 / math.sqrt(rcv_dev * n_rcv)
    rcv_factor = 1.0 / math.sqrt(src_dev * n_src)
    lag_src = jnp.take(lag_table, src_pos, axis=1)
    lag_rcv = jnp.take(lag_table, rcv_pos, axis=1)
    src_init = jnp.zeros((n_slow, 2, src_dev, n_freq), jnp.float32)
    other_init = jnp.zeros((n_slow, 2, n_freq, rcv_dev), jnp.float32)
    shard_piece = lax.all_gather(rcv_spec, "src", axis=2, tiled=True)
    block_width = math.gcd(shard_piece.shape[2], 16)

    def inner(turn_index, totals):
        offset = turn_index * block_width
        freqs = offset + jnp.arange(block_width, dtype=jnp.int32)
        src_block = lax.dynamic_slice_in_dim(src_full, offset, block_width, 2)
        rcv_block = lax.dynamic_slice_in_dim(shard_piece, offset, block_width, 2)
        stacked_re, stacked_im = cross_block(src_block, rcv_block)
        rcv_cos, rcv_sin = phase_table(freqs, lag_rcv, n_freq)
        src_cos, src_sin = phase_table(freqs, lag_src, n_freq)
        src_part = source_slant(
            stacked_re, stacked_im, rcv_cos, rcv_sin, src_cos, src_sin, src_factor
        )
        src_total = lax.dynamic_update_slice_in_dim(totals[0], src_part, offset, 3)
        left_op = jnp.concatenate([stacked_re, stacked_im], axis=1)
        right_op = receiver_right(src_cos.astype(jnp.bfloat16), src_sin.astype(jnp.bfloat16))
        rcv_part = receiver_outer(receiver_sums(left_op, right_op), rcv_cos, rcv_sin, rcv_factor)
        other = lax.dynamic_update_slice_in_dim(totals[1], rcv_part, offset, 2)
        return (src_total, other)

    src_total, other = lax.fori_loop(
        0, shard_piece.shape[2] // block_width, inner, (src_init, other_init)
    )
    panel_src = lax.psum_scatter(src_total, "rcv", scatter_dimension=2, tiled=True)
    panel_rcv = lax.psum_scatter(other, "src", scatter_dimension=2, tiled=True)
    return (panel_src, panel_rcv)


def solution(mesh):
    placed = (P(None, None, "rcv", "src"), P(None, None, "src", "rcv"), P(), P("src"), P("rcv"))
    return jax.shard_map(
        per_device,
        mesh=mesh,
        in_specs=placed,
        out_specs=(P(None, None, ("src", "rcv"), None), P(None, None, "src", "rcv")),
        check_vma=False,
    )
```

profile of v0, /device:TPU:0, one launch (start us, length us, event | category | flops | bytes accessed | tf_op | source)
XLA Modules:
  0.0 431.7 jit_solution(10800249658615100742)
XLA Ops:
  8.7 3.5 copy.18
  12.2 2.8 gather_fusion.1
  15.1 2.9 gather_fusion
  18.3 39.9 %all-gather.3.cloned.1.call-done = bf16[2,16,256,64]{3,2,1,0:T(8,128)(2,1)} async-done(((bf16[2,16,64,64]{3,2,1,0:T(8,128)(2,1)}), bf16[2,16,256,64]{3,2,1,0:T(8,128)(2,1)}) %all-gather.3.cloned.1.call-update) | async-done | bytes 1048592 | tf_op jit(solution)/shard_map/all_gather | solution.py:73
  58.2 37.4 %all-gather.5.cloned.1.call-done = bf16[2,16,256,256]{3,2,1,0:T(8,128)(2,1)} async-done(((bf16[2,16,32,256]{3,2,1,0:T(8,128)(2,1)}), bf16[2,16,256,256]{3,2,1,0:T(8,128)(2,1)}) %all-gather.5.cloned.1.call-update) | async-done | bytes 4194320 | tf_op jit(solution)/shard_map/all_gather | solution.py:86
  95.6 2.2 broadcast_in_dim.40
  97.8 4.2 broadcast_in_dim.41.clone
  102.0 200.4 %while.17 = (s32[]{:T(128)}, f32[16,2,64,256]{2,0,3,1:T(8,128)}, f32[16,2,256,256]{3,2,1,0:T(8,128)}, bf16[2,16,256,64]{3,2,1,0:T(8,128)(2,1)}, bf16[2,16,256,25...) while((s32[]{:T(128)}, f32[16,2,64,256]{2,0,3,1:T(8,128)}, ...), condition=%wide.region_3.4_spmd, body=%wide.region_0.3_spmd.sunk | while | flops 116801552 | bytes 18604620 | solution.py:107
  108.3 1.4 fusion.77
  111.3 1.3 multiply_bitcast_fusion.5
  120.8 1.4 fusion.77
  123.9 1.3 multiply_bitcast_fusion.5
  133.4 1.4 fusion.77
  136.4 1.3 multiply_bitcast_fusion.5
  145.9 1.4 fusion.77
  148.9 1.3 multiply_bitcast_fusion.5
  158.4 1.4 fusion.77
  161.4 1.3 multiply_bitcast_fusion.5
  170.9 1.4 fusion.77
  183.4 1.4 fusion.77
  196.0 1.4 fusion.77
  208.5 1.4 fusion.77
  221.1 1.4 fusion.77
  233.6 1.4 fusion.77
  246.1 1.4 fusion.77
  258.6 1.4 fusion.77
  271.1 1.4 fusion.77
  283.7 1.4 fusion.77
  296.2 1.4 fusion.77
  302.4 3.8 copy.22
  306.8 43.4 %reduce-scatter.3.cloned.1.call-done = f32[16,2,16,256]{3,2,1,0:T(8,128)} async-done(((f32[16,2,64,256]{3,2,1,0:T(8,128)}), f32[16,2,16,256]{3,2,1,0:T(8,128)}) %reduce-scatter.3.cloned.1.call-update) | async-done | bytes 524304 | tf_op jit(solution)/shard_map/reduce_scatter | solution.py:110
  350.2 74.9 %reduce-scatter.5.cloned.1.call-done = f32[16,2,32,256]{3,2,1,0:T(8,128)} async-done(((f32[16,2,256,256]{3,2,1,0:T(8,128)}), f32[16,2,32,256]{3,2,1,0:T(8,128)}) %reduce-scatter.5.cloned.1.call-update) | async-done | bytes 1048592 | tf_op jit(solution)/shard_map/reduce_scatter | solution.py:111
  (305 shorter events, 172.9 us)
Async XLA Ops:
  7.2 51.1 %all-gather.3.cloned.1.call-start = ((), (), s32[]{:S(2)}) async-start(), calls=%async_computation.2 | async-start | bytes 2621440 | tf_op jit(solution)/shard_map/all_gather | solution.py:73
  7.9 87.7 %all-gather.5.cloned.1.call-start = ((), (), s32[]{:S(2)}) async-start(), calls=%async_computation.3 | async-start | bytes 4718592 | tf_op jit(solution)/shard_map/all_gather | solution.py:86
  8.6 341.6 %reduce-scatter.3.cloned.1.call-start = ((), (), s32[]{:S(2)}) async-start(), calls=%async_computation.4 | async-start | bytes 2621440 | tf_op jit(solution)/shard_map/reduce_scatter | solution.py:110
  8.7 3.5 copy-start.1
  8.7 6.3 %copy-start = (s32[256]{0:T(256)S(1)}, s32[256]{0:T(256)}, u32[]{:S(2)}) copy-start(s32[256]{0:T(256)} %param.11) | copy-start | bytes 3076
  306.2 118.9 %reduce-scatter.5.cloned.1.call-start = ((), (), s32[]{:S(2)}) async-start(), calls=%async_computation.5 | async-start | bytes 9437184 | tf_op jit(solution)/shard_map/reduce_scatter | solution.py:111
Sparse Core Ops, SparseCore 0:
  9.6 48.6 all-gather.2
  60.1 35.4 all-gather.4
  306.3 43.8 reduce-scatter.2
  354.5 70.6 reduce-scatter.4
where the time goes:
time: 433 us; the launch traced here: 432 us
  waiting for transfers between devices  198 us (46%)
  other arithmetic  109 us (25%)
  local copies, waits for them, and re-layouts  68.7 us (16%)
  matrix products  41.3 us (10%)
  between operations  13.8 us (3%)
    reduce_scatter x1, waiting for transfers between devices, per_device(): panel_rcv = lax.psum_scatter(other, 'src', scatter_dimension=2, tiled=True)  74.9 us
    reduce_scatter x1, waiting for transfers between devices, per_device(): lax.psum_scatter(src_total, 'rcv', scatter_dimension=2, tiled=True)  43.4 us
    all_gather x1, waiting for transfers between devices, per_device(): src_full = lax.all_gather(src_spec, 'rcv', axis=2, tiled=True)  39.9 us
    all_gather x1, waiting for transfers between devices, per_device(): shard_piece = lax.all_gather(rcv_spec, 'src', axis=2, tiled=True)  37.4 us
    dot_general x16, matrix products, cross_block(): jnp.einsum('cgwfs,cgwfr->gfsr', swapped, rcv_five, preferred_element_type...  22 us
    another operation x16, other arithmetic, receiver_outer(): return jnp.transpose(jnp.stack([panel_re, panel_im]), (2, 0, 1, 3))  20.7 us
    convert_element_type x16, other arithmetic, source_slant(): sin_b = rcv_sin.astype(jnp.bfloat16)  20.1 us
    dynamic_update_slice x16, local copies, waits for them, and re-layouts, inner(): other = lax.dynamic_update_slice_in_dim(totals[1], rcv_part, offset, 2)  18 us
  transfers between devices with their start and end apart: 4, of which 4 were waited for; matrix products, arithmetic and copies ran while one was open for 2% of the time, Pallas kernels for 0%

commit v1 on v0

--- a/solution.py
+++ b/solution.py
@@ -3,6 +3,8 @@
 import jax
 import jax.numpy as jnp
 from jax import lax
+from jax.experimental import pallas as pl
+from jax.experimental.pallas import tpu as pltpu
 from jax.sharding import PartitionSpec as P
 
 WIN = 8
@@ -69,7 +71,7 @@
     return jnp.transpose(jnp.stack([panel_re, panel_im]), (2, 0, 1, 3))
 
 
-def per_device(src_spec, rcv_spec, lag_table, src_pos, rcv_pos):
+def per_device_general(src_spec, rcv_spec, lag_table, src_pos, rcv_pos):
     src_full = lax.all_gather(src_spec, "rcv", axis=2, tiled=True)
     n_freq = src_full.shape[2]
     src_dev = src_full.shape[3]
@@ -112,6 +114,393 @@
     return (panel_src, panel_rcv)
 
 
+LANES = 128
+HALVES = 2
+ROWS = 32
+LAG_ROWS = 16
+VMEM = 56 * 2**20
+F32 = jnp.float32
+BF16 = jnp.bfloat16
+SIN = [(-1) ** n * (math.pi / 2) ** (2 * n + 1) / math.factorial(2 * n + 1) for n in range(5)]
+COS = [(-1) ** n * (math.pi / 2) ** (2 * n) / math.factorial(2 * n) for n in range(6)]
+
+
+def horner(coefs, v):
+    total = coefs[-1]
+    for coef in coefs[-2::-1]:
+        total = coef + v * total
+    return total
+
+
+def phases(lag, freq, period):
+    turns = lag * freq * (1.0 / period)
+    quarters = 4.0 * (turns - jnp.floor(turns))
+    near = jnp.floor(quarters + 0.5)
+    u = quarters - near
+    v = u * u
+    s = u * horner(SIN, v)
+    c = horner(COS, v)
+    odd = (near == 1.0) | (near == 3.0)
+    cos = jnp.where(odd, s, c)
+    sin = jnp.where(odd, c, s)
+    cos = jnp.where((near == 1.0) | (near == 2.0), -cos, cos)
+    sin = jnp.where((near == 2.0) | (near == 3.0), -sin, sin)
+    return cos, sin
+
+
+def lanes_of(rows):
+    return lax.broadcasted_iota(jnp.int32, (rows, LANES), 1)
+
+
+class Sizes:
+    def __init__(self, shapes, n_src, n_rcv):
+        src_spec, rcv_spec, lag_table = shapes
+        self.n_src, self.n_rcv, self.n_dev = n_src, n_rcv, n_src * n_rcv
+        self.n_slow, self.n_pos = lag_table
+        self.n_win = src_spec[1]
+        self.src_freq, self.src_dev = src_spec[2:]
+        self.rcv_freq, self.rcv_dev = rcv_spec[2:]
+        self.n_freq = self.rcv_freq * n_src
+        self.own = self.n_freq // self.n_dev
+        self.s_all, self.r_all = self.src_dev * n_src, self.rcv_dev * n_rcv
+        self.r_half = self.r_all // HALVES
+        self.src_part, self.rcv_part = self.src_dev // n_rcv, self.rcv_dev // n_src
+
+    def fits(self):
+        return (
+            2 * self.n_win == ROWS
+            and 2 * self.n_slow == ROWS
+            and self.n_win == WIN * SEGS
+            and self.own == self.n_src
+            and self.rcv_freq == self.n_dev
+            and self.src_freq == 2 * self.n_dev
+            and 2 * self.src_dev == LANES
+            and self.rcv_dev == HALVES * LANES
+            and self.src_part * self.own == LANES
+            and self.rcv_part * self.n_src == HALVES * LANES
+            and LANES % self.rcv_part == 0
+            and self.n_pos % LANES == 0
+            and self.own * self.n_dev == HALVES * LANES
+        )
+
+
+def pack_first(z):
+    def kernel(me_ref, src_pos_ref, rcv_pos_ref, src_ref, rcv_ref, lag_ref, out_ref, flat_src, flat_rcv):
+        lane = lanes_of(LAG_ROWS)
+        acc = jnp.zeros((LAG_ROWS, LANES), jnp.int32)
+        for n in range(z.src_part + z.rcv_part):
+            if n < z.src_part:
+                pos = src_pos_ref[me_ref[1] * z.src_part + n]
+            else:
+                pos = rcv_pos_ref[me_ref[0] * z.rcv_part + n - z.src_part]
+            base = pl.multiple_of((pos // LANES) * LANES, LANES)
+            tile = lag_ref[:, pl.ds(base, LANES)]
+            acc = jnp.where(lane == n, pltpu.roll(tile, (n - pos) & (LANES - 1), 1), acc)
+        lags = (acc - z.n_freq).astype(F32).astype(BF16)
+        count = z.n_dev
+        for row in range(ROWS):
+            both = src_ref[row].astype(F32)
+            flat_src[row * count:(row + 1) * count, :] = jnp.concatenate([both[:count], both[count:]], 1)
+            flat_rcv[row * count:(row + 1) * count, :] = rcv_ref[row].astype(F32)
+        for dev in range(count):
+            out_ref[dev, :ROWS, :] = flat_src[pl.ds(dev, ROWS, stride=count), :].astype(BF16)
+            out_ref[dev, ROWS:2 * ROWS, :] = flat_rcv[pl.ds(dev, ROWS, stride=count), :].astype(BF16)
+            out_ref[dev, 2 * ROWS:, :] = lags
+
+    rows = 2 * ROWS + LAG_ROWS
+    flat = pltpu.VMEM((ROWS * z.n_dev, LANES), F32)
+    return pl.pallas_call(
+        kernel,
+        grid=(1,),
+        in_specs=[pl.BlockSpec(memory_space=pltpu.SMEM)] * 3
+        + [
+            pl.BlockSpec((ROWS, z.src_freq, z.src_dev), lambda n: (0, 0, 0)),
+            pl.BlockSpec((ROWS, z.rcv_freq, LANES), lambda n: (0, 0, 0)),
+            pl.BlockSpec((z.n_slow, z.n_pos), lambda n: (0, 0)),
+        ],
+        out_specs=pl.BlockSpec((z.n_dev, rows, LANES), lambda n: (0, 0, 0)),
+        out_shape=jax.ShapeDtypeStruct((z.n_dev, rows, LANES), BF16),
+        scratch_shapes=[flat, flat],
+        compiler_params=pltpu.CompilerParams(vmem_limit_bytes=VMEM),
+        cost_estimate=pl.CostEstimate(flops=10**6, bytes_accessed=2 * 10**6, transcendentals=0),
+        name="pack_first",
+    )
+
+
+def pack_second(z):
+    def kernel(rcv_ref, out_ref, flat):
+        count = z.n_dev
+        for row in range(ROWS):
+            flat[row * count:(row + 1) * count, :] = rcv_ref[row].astype(F32)
+        for dev in range(count):
+            out_ref[dev] = flat[pl.ds(dev, ROWS, stride=count), :].astype(BF16)
+
+    return pl.pallas_call(
+        kernel,
+        grid=(1,),
+        in_specs=[pl.BlockSpec((ROWS, z.rcv_freq, LANES), lambda n: (0, 0, 1))],
+        out_specs=pl.BlockSpec((z.n_dev, ROWS, LANES), lambda n: (0, 0, 0)),
+        out_shape=jax.ShapeDtypeStruct((z.n_dev, ROWS, LANES), BF16),
+        scratch_shapes=[pltpu.VMEM((ROWS * z.n_dev, LANES), F32)],
+        compiler_params=pltpu.CompilerParams(vmem_limit_bytes=VMEM),
+        cost_estimate=pl.CostEstimate(flops=10**6, bytes_accessed=10**6, transcendentals=0),
+        name="pack_second",
+    )
+
+
+def gather_lags(z, first_ref, half, src_lag, rcv_lag):
+    lane = lanes_of(LAG_ROWS)
+
+    def spread(pieces):
+        total = jnp.zeros((LAG_ROWS, LANES), F32)
+        for sender, begin, place, width in pieces:
+            tile = first_ref[sender, 2 * ROWS:, :].astype(F32) + float(z.n_freq)
+            shift = (place - begin) % LANES
+            moved = pltpu.roll(tile, shift, 1) if shift else tile
+            total = jnp.where((lane >= place) & (lane < place + width), moved, total)
+        return total
+
+    for block in range(z.s_all // LANES):
+        pieces = [
+            ((2 * block + odd) * z.n_rcv + rcv, 0, odd * z.src_dev + rcv * z.src_part, z.src_part)
+            for odd in range(2)
+            for rcv in range(z.n_rcv)
+        ]
+        src_lag[:, block * LANES:(block + 1) * LANES] = spread(pieces)
+    per_half = z.n_src // HALVES
+    for rcv in range(z.n_rcv):
+        pieces = [
+            ((half * per_half + n) * z.n_rcv + rcv, z.src_part, n * z.rcv_part, z.rcv_part)
+            for n in range(per_half)
+        ]
+        rcv_lag[:, rcv * LANES:(rcv + 1) * LANES] = spread(pieces)
+
+
+def cross_spectra(z, first_ref, rcv_ref, rcv_row, turn, left, right, stack):
+    pair, odd = turn // 2, turn % 2
+    lane = lanes_of(ROWS)
+    blocks = []
+    for block in range(z.s_all // LANES):
+        one = first_ref[(2 * block) * z.n_rcv + pair, :ROWS, :].astype(F32)
+        two = first_ref[(2 * block + 1) * z.n_rcv + pair, :ROWS, :].astype(F32)
+        one = jnp.where(odd == 0, one, pltpu.roll(one, z.src_dev, 1))
+        two = jnp.where(odd == 0, pltpu.roll(two, z.src_dev, 1), two)
+        blocks.append(jnp.where(lane < z.src_dev, one, two))
+    left[...] = jnp.transpose(jnp.concatenate(blocks, 1)).astype(BF16)
+    pieces = [rcv_ref[turn * z.n_rcv + rcv, rcv_row:rcv_row + ROWS, :] for rcv in range(z.n_rcv)]
+    spec = jnp.concatenate(pieces, 1).astype(F32)
+    turned = jnp.concatenate([-spec[z.n_win:], spec[:z.n_win]], 0)
+    window = lax.broadcasted_iota(jnp.int32, (ROWS, 1), 0) % z.n_win
+    for seg in range(SEGS):
+        here = window // WIN == seg
+        right[seg] = jnp.where(here, spec, 0.0).astype(BF16)
+        right[SEGS + seg] = jnp.where(here, turned, 0.0).astype(BF16)
+    width, height = 2 * LANES, TILE_ROWS
+    for col in range(0, z.r_half, width):
+        for row in range(0, z.s_all, height):
+            part = left[row:row + height, :]
+            total_re, total_im = 0.0, 0.0
+            for seg in range(SEGS):
+                real = jnp.dot(part, right[seg, :, col:col + width], preferred_element_type=F32)
+                imag = jnp.dot(part, right[SEGS + seg, :, col:col + width], preferred_element_type=F32)
+                scale = lax.rsqrt(jnp.maximum(real * real + imag * imag, 1.0))
+                total_re, total_im = total_re + real * scale, total_im + imag * scale
+            stack[row:row + height, col:col + width] = total_re.astype(BF16)
+            stack[z.s_all + row:z.s_all + row + height, col:col + width] = total_im.astype(BF16)
+
+
+TILE_ROWS = 32
+
+
+def compute(z, half):
+    last = half == HALVES - 1
+    src_factor = 1.0 / (SEGS * math.sqrt(z.r_all))
+    rcv_factor = 1.0 / (SEGS * math.sqrt(z.s_all))
+    n = z.n_slow
+
+    def kernel(me_ref, first_ref, *refs):
+        if last:
+            second_ref, before_ref, out_ref, src_lag, rcv_lag, left, right, stack, sums = refs
+            rcv_ref, rcv_row = second_ref, 0
+        else:
+            out_ref, part_ref, src_lag, rcv_lag, left, right, stack = refs
+            rcv_ref, rcv_row = first_ref, ROWS
+        turn = pl.program_id(0)
+
+        @pl.when(turn == 0)
+        def _():
+            gather_lags(z, first_ref, half, src_lag, rcv_lag)
+
+        cross_spectra(z, first_ref, rcv_ref, rcv_row, turn, left, right, stack)
+        freq = (turn * z.n_dev + me_ref[0] * z.n_rcv + me_ref[1]).astype(F32)
+        src_cos, src_sin = phases(src_lag[...], freq, 2.0 * z.n_freq)
+        rcv_cos, rcv_sin = phases(rcv_lag[...], freq, 2.0 * z.n_freq)
+        upper = jnp.concatenate([src_cos, src_sin], 1)
+        lower = jnp.concatenate([-src_sin, src_cos], 1)
+        both = jnp.concatenate([upper, lower], 0).astype(BF16)
+        over_src = jnp.dot(both, stack[...], preferred_element_type=F32) * rcv_factor
+        over_re, over_im = over_src[:n], over_src[n:]
+        panel = jnp.concatenate([over_re * rcv_cos - over_im * rcv_sin, over_re * rcv_sin + over_im * rcv_cos], 0)
+        for rcv in range(z.n_rcv):
+            out_ref[turn * z.n_rcv + rcv, :ROWS, :] = panel[:, rcv * LANES:(rcv + 1) * LANES].astype(BF16)
+        dims = (((1,), (1,)), ((), ()))
+        with_re = jnp.concatenate([rcv_cos, rcv_sin], 0).astype(BF16)
+        with_im = jnp.concatenate([-rcv_sin, rcv_cos], 0).astype(BF16)
+        over_rcv = lax.dot_general(with_re, stack[:z.s_all, :], dims, preferred_element_type=F32)
+        over_rcv += lax.dot_general(with_im, stack[z.s_all:, :], dims, preferred_element_type=F32)
+        if not last:
+            part_ref[0] = over_rcv
+            return
+        over_rcv = (over_rcv + before_ref[0]) * src_factor
+        over_re, over_im = over_rcv[:n], over_rcv[n:]
+        panel = jnp.concatenate([over_re * src_cos + over_im * src_sin, over_im * src_cos - over_re * src_sin], 0)
+        sums[turn] = panel
+
+        @pl.when(turn == z.own - 1)
+        def _():
+            lane = lanes_of(ROWS)
+            width = z.src_part
+            for dev in range(z.n_dev):
+                block, place = divmod(dev * width, LANES)
+                total = jnp.zeros((ROWS, LANES), F32)
+                for k in range(z.own):
+                    tile = sums[k, :, block * LANES:(block + 1) * LANES]
+                    shift = (k * width - place) % LANES
+                    moved = pltpu.roll(tile, shift, 1) if shift else tile
+                    total = jnp.where((lane >= k * width) & (lane < (k + 1) * width), moved, total)
+                out_ref[dev, ROWS:, :] = total.astype(BF16)
+
+    whole = lambda *shape: pl.BlockSpec(shape, lambda k: (0,) * len(shape))
+    part_spec = pl.BlockSpec((1, ROWS, z.s_all), lambda k: (k, 0, 0))
+    part_shape = jax.ShapeDtypeStruct((z.own, ROWS, z.s_all), F32)
+    in_specs = [pl.BlockSpec(memory_space=pltpu.SMEM), whole(z.n_dev, 2 * ROWS + LAG_ROWS, LANES)]
+    out_rows = ROWS * (2 if last else 1)
+    out_specs = [whole(z.n_dev, out_rows, LANES)]
+    out_shape = [jax.ShapeDtypeStruct((z.n_dev, out_rows, LANES), BF16)]
+    scratch = [
+        pltpu.VMEM((n, z.s_all), F32),
+        pltpu.VMEM((n, z.r_half), F32),
+        pltpu.VMEM((z.s_all, ROWS), BF16),
+        pltpu.VMEM((2 * SEGS, ROWS, z.r_half), BF16),
+        pltpu.VMEM((2 * z.s_all, z.r_half), BF16),
+    ]
+    if last:
+        in_specs += [whole(z.n_dev, ROWS, LANES), part_spec]
+        scratch.append(pltpu.VMEM((z.own, ROWS, z.s_all), F32))
+    else:
+        out_specs.append(part_spec)
+        out_shape.append(part_shape)
+    return pl.pallas_call(
+        kernel,
+        grid=(z.own,),
+        in_specs=in_specs,
+        out_specs=out_specs,
+        out_shape=out_shape,
+        scratch_shapes=scratch,
+        compiler_params=pltpu.CompilerParams(vmem_limit_bytes=VMEM),
+        cost_estimate=pl.CostEstimate(flops=8 * 10**9, bytes_accessed=2 * 10**6, transcendentals=4 * 10**6),
+        name="compute_last" if last else "compute_first",
+    )
+
+
+def unpack_receivers(z, in_ref, flat, out_ref):
+    n = z.n_slow
+    for dev in range(z.n_dev):
+        flat[dev * ROWS:(dev + 1) * ROWS, :] = in_ref[dev, :ROWS, :].astype(F32)
+    for slow in range(n):
+        for part in range(2):
+            out_ref[2 * slow + part] = flat[pl.ds(part * n + slow, z.n_dev, stride=ROWS), :]
+
+
+def unpack_first(z):
+    def kernel(in_ref, out_ref, flat):
+        unpack_receivers(z, in_ref, flat, out_ref)
+
+    return pl.pallas_call(
+        kernel,
+        grid=(1,),
+        in_specs=[pl.BlockSpec((z.n_dev, ROWS, LANES), lambda k: (0, 0, 0))],
+        out_specs=pl.BlockSpec((ROWS, z.rcv_freq, LANES), lambda k: (0, 0, 0)),
+        out_shape=jax.ShapeDtypeStruct((ROWS, z.rcv_freq, z.rcv_dev), F32),
+        scratch_shapes=[pltpu.VMEM((z.n_dev * ROWS, LANES), F32)],
+        compiler_params=pltpu.CompilerParams(vmem_limit_bytes=VMEM),
+        cost_estimate=pl.CostEstimate(flops=10**6, bytes_accessed=10**6, transcendentals=0),
+        name="unpack_first",
+    )
+
+
+def unpack_last(z):
+    n = z.n_slow
+    group = LANES // z.n_dev
+    width = z.src_part
+
+    def kernel(in_ref, held_ref, rcv_ref, src_ref, flat):
+        del held_ref
+        unpack_receivers(z, in_ref, flat, rcv_ref)
+        for dev in range(z.n_dev):
+            flat[dev * ROWS:(dev + 1) * ROWS, :] = in_ref[dev, ROWS:, :].astype(F32)
+        lane = lanes_of(width)
+        for first in range(0, ROWS, group):
+            tiles = [flat[pl.ds(first + j, z.n_dev, stride=ROWS), :] for j in range(group)]
+            turned = jnp.transpose(jnp.concatenate(tiles, 0))
+            for j in range(group):
+                part, slow = divmod(first + j, n)
+                for block in range(z.own // group):
+                    total = jnp.zeros((width, LANES), F32)
+                    for k in range(group):
+                        row = (block * group + k) * width
+                        tile = turned[row:row + width, :]
+                        shift = (k - j) * z.n_dev % LANES
+                        moved = pltpu.roll(tile, shift, 1) if shift else tile
+                        total = jnp.where((lane >= k * z.n_dev) & (lane < (k + 1) * z.n_dev), moved, total)
+                    src_ref[2 * slow + part, :, block * LANES:(block + 1) * LANES] = total
+
+    return pl.pallas_call(
+        kernel,
+        grid=(1,),
+        in_specs=[pl.BlockSpec((z.n_dev, 2 * ROWS, LANES), lambda k: (0, 0, 0)), pl.BlockSpec(memory_space=pl.ANY)],
+        out_specs=[
+            pl.BlockSpec((ROWS, z.rcv_freq, LANES), lambda k: (0, 0, 1)),
+            pl.BlockSpec((ROWS, width, z.n_freq), lambda k: (0, 0, 0)),
+        ],
+        out_shape=[
+            jax.ShapeDtypeStruct((ROWS, z.rcv_freq, z.rcv_dev), F32),
+            jax.ShapeDtypeStruct((ROWS, width, z.n_freq), F32),
+        ],
+        input_output_aliases={1: 0},
+        scratch_shapes=[pltpu.VMEM((z.n_dev * ROWS, LANES), F32)],
+        compiler_params=pltpu.CompilerParams(vmem_limit_bytes=VMEM),
+        cost_estimate=pl.CostEstimate(flops=10**6, bytes_accessed=2 * 10**6, transcendentals=0),
+        name="unpack_last",
+    )
+
+
+def exchange(payload):
+    return lax.all_to_all(payload, ("src", "rcv"), 0, 0, tiled=True)
+
+
+def per_device(src_spec, rcv_spec, lag_table, src_pos, rcv_pos):
+    n_src, n_rcv = lax.axis_size("src"), lax.axis_size("rcv")
+    z = Sizes((src_spec.shape, rcv_spec.shape, lag_table.shape), n_src, n_rcv)
+    if not z.fits():
+        return per_device_general(src_spec, rcv_spec, lag_table, src_pos, rcv_pos)
+    me = jnp.stack([lax.axis_index("src"), lax.axis_index("rcv")]).astype(jnp.int32)
+    src_rows = src_spec.reshape(ROWS, z.src_freq, z.src_dev)
+    rcv_rows = rcv_spec.reshape(ROWS, z.rcv_freq, z.rcv_dev)
+    first = exchange(pack_first(z)(me, src_pos, rcv_pos, src_rows, rcv_rows, lag_table))
+    second = exchange(pack_second(z)(rcv_rows))
+    out_first, before = compute(z, 0)(me, first)
+    got_first = exchange(out_first)
+    (out_last,) = compute(z, 1)(me, first, second, before)
+    got_last = exchange(out_last)
+    held = unpack_first(z)(got_first)
+    panel_rcv, panel_src = unpack_last(z)(got_last, held)
+    return (
+        panel_src.reshape(z.n_slow, 2, z.src_part, z.n_freq),
+        panel_rcv.reshape(z.n_slow, 2, z.rcv_freq, z.rcv_dev),
+    )
+
+
 def solution(mesh):
     placed = (P(None, None, "rcv", "src"), P(None, None, "src", "rcv"), P(), P("src"), P("rcv"))
     return jax.shard_map(

time: 433 us -> 94.1 us (0.22)
  waiting for transfers between devices: 198 us -> 27.2 us
  other arithmetic: 109 us -> 0.58 us
  local copies, waits for them, and re-layouts: 68.7 us -> 2.21 us
  matrix products: 41.3 us -> 0 us
  Pallas kernels: 0 us -> 38.8 us
  starting transfers between devices: 0.15 us -> 23.3 us
  between operations: 13.8 us -> 0.68 us
    reduce_scatter x2 -> x0, waiting for transfers between devices: 118 us -> none  [the longest x1 74.9 us: per_device(): panel_rcv = lax.psum_scatter(other, 'src', scatter_dimension=2, tiled=True)]
    all_gather x2 -> x0, waiting for transfers between devices: 77.3 us -> none  [the longest x1 39.9 us: per_device(): src_full = lax.all_gather(src_spec, 'rcv', axis=2, tiled=True)]
    dot_general x64 -> x0, matrix products: 41.3 us -> none  [the longest x16 22 us: cross_block(): jnp.einsum('cgwfs,cgwfr->gfsr', swapped, rcv_five, preferred_element_type...]
    pallas_call x0 -> x6, Pallas kernels: none -> 38.8 us  [the longest x1 14.8 us: per_device(): out_last, = compute(z, 1)(me, first, second, before)]
    convert_element_type x48 -> x0, other arithmetic: 34.9 us -> none  [the longest x16 20.1 us: source_slant(): sin_b = rcv_sin.astype(jnp.bfloat16)]
    dynamic_slice x32 -> x0, local copies, waits for them, and re-layouts: 30.6 us -> none  [the longest x16 15.7 us: inner(): rcv_block = lax.dynamic_slice_in_dim(shard_piece, offset, block_width, 2)]
    all_to_all x0 -> x4, waiting for transfers between devices: none -> 27.2 us  [exchange(): return lax.all_to_all(payload, ('src', 'rcv'), 0, 0, tiled=True)]
    neg x32 -> x0, other arithmetic: 26.1 us -> none  [the longest x16 17 us: source_slant(): bottom = jnp.concatenate([-sin_b, cos_b], axis=2)]
  transfers between devices with their start and end apart: 4 -> 4, of which waited for: 4 -> 2; matrix products, arithmetic and copies ran while one was open for 2% -> 0% of each run, Pallas kernels for 0% -> 35%
where the time goes in v1:
time: 94.1 us; the launch traced here: 92.8 us
  Pallas kernels  38.8 us (41%)
  waiting for transfers between devices  27.2 us (29%)
  starting transfers between devices  23.3 us (25%)
  local copies, waits for them, and re-layouts  2.21 us (2%)
    all_to_all x4, waiting for transfers between devices, exchange(): return lax.all_to_all(payload, ('src', 'rcv'), 0, 0, tiled=True)  27.2 us
    all_to_all x4, starting transfers between devices, exchange(): return lax.all_to_all(payload, ('src', 'rcv'), 0, 0, tiled=True)  23.3 us
    pallas_call x1, Pallas kernels, per_device(): out_last, = compute(z, 1)(me, first, second, before)  14.8 us
    pallas_call x1, Pallas kernels, per_device(): out_first, before = compute(z, 0)(me, first)  13.8 us
    pallas_call x1, Pallas kernels, per_device(): pack_first(z)(me, src_pos, rcv_pos, src_rows, rcv_rows, lag_table)  3.2 us
    pallas_call x1, Pallas kernels, per_device(): panel_rcv, panel_src = unpack_last(z)(got_last, held)  2.99 us
    unnamed x8, local copies, waits for them, and re-layouts  2.21 us
    pallas_call x1, Pallas kernels, per_device(): held = unpack_first(z)(got_first)  2.09 us
  transfers between devices with their start and end apart: 4, of which 2 were waited for; matrix products, arithmetic and copies ran while one was open for 0% of the time, Pallas kernels for 35%

profile of v1, /device:TPU:0, one launch (start us, length us, event | category | flops | bytes accessed | tf_op | source)
XLA Modules:
  0.0 92.8 jit_solution(7939544054675318752)
XLA Ops:
  0.6 0.6 pad_add_fusion.me_ref
  1.2 3.2 %pack_first.1 = bf16[32,80,128]{2,1,0:T(8,128)(2,1)} custom-call(s32[2]{0:T(128)} %pad_add_fusion.me_ref, s32[64]{0:T(128)} %src_pos_ref.1, s32[256]{0:T(256)} %rcv_pos_ref.1, bf16[32,64,64]{2,1,0:T(8,128)(2,1)} %bitcast.9, bf16[32,32,256]{2,1,0:T(8,128)(2,1)} %bitcast.7, s32[16,8192]{1,0:T(8,128)} %lag_ref.1), custom_call_target="tpu_custom_call" | custom-call | flops 1000000 | bytes 2000000 | tf_op jit(solution)/shard_map/pack_first/pallas_call | solution.py:490
  4.4 7.3 %all-to-all-start = ((bf16[32,80,128]{2,1,0:T(8,128)(2,1)}), bf16[32,80,128]{2,1,0:T(8,128)(2,1)S(1)}, u32[]{:S(2)}, u32[]{:S(2)}) async-start(bf16[32,80,128]{2,1,0:T(8,128)(2,1)} %pack_first.1), calls=%async_computation | async-start | bytes 1310720 | tf_op jit(solution)/shard_map/all_to_all | solution.py:479
  11.7 2.0 %pack_second.1 = bf16[32,32,128]{2,1,0:T(8,128)(2,1)} custom-call(bf16[32,32,256]{2,1,0:T(8,128)(2,1)} %bitcast.8), custom_call_target="tpu_custom_call" | custom-call | flops 1000000 | bytes 1000000 | tf_op jit(solution)/shard_map/pack_second/pallas_call | solution.py:491
  13.7 14.9 %all-to-all-done.first_ref = bf16[32,80,128]{2,1,0:T(8,128)(2,1)S(1)} async-done(((bf16[32,80,128]{2,1,0:T(8,128)(2,1)}), bf16[32,80,128]{2,1,0:T(8,128)(2,1)S(1)}, u32[]{:S(2)}, u32[]{:S(2)}) %all-to-all-start) | async-done | bytes 655392 | tf_op jit(solution)/shard_map/all_to_all | solution.py:479
  28.6 0.0 copy-start.2
  28.6 4.3 %all-to-all-start.1 = ((bf16[32,32,128]{2,1,0:T(8,128)(2,1)}), bf16[32,32,128]{2,1,0:T(8,128)(2,1)S(1)}, u32[]{:S(2)}, u32[]{:S(2)}) async-start(bf16[32,32,128]{2,1,0:T(8,128)(2,1)} %pack_second.1), calls=%async_computation.1 | async-start | bytes 524288 | tf_op jit(solution)/shard_map/all_to_all | solution.py:479
  32.9 0.0 copy-done.2
  32.9 13.8 %compute_first.1 = (bf16[32,32,128]{2,1,0:T(8,128)(2,1)}, f32[8,32,512]{2,1,0:T(8,128)}) custom-call(s32[2]{0:T(128)} %pad_add_fusion.me_ref, bf16[32,80,128]{2,1,0:T(8,128)(2,1)} %copy-done.2), custom_call_target="tpu_custom_call" | custom-call | flops 8000000000 | bytes 2000000 | tf_op jit(solution)/shard_map/compute_first/pallas_call | solution.py:492
  46.7 0.0 all-to-all-done.1.refs_0_
  46.7 0.0 copy-start.3
  46.7 0.7 copy-done.3
  47.4 5.8 %all-to-all-start.3 = ((bf16[32,32,128]{2,1,0:T(8,128)(2,1)}), bf16[32,32,128]{2,1,0:T(8,128)(2,1)S(1)}, u32[]{:S(2)}, u32[]{:S(2)}) async-start(bf16[32,32,128]{2,1,0:T(8,128)(2,1)} %get-tuple-element.7), calls=%async_computation.3 | async-start | bytes 524288 | tf_op jit(solution)/shard_map/all_to_all | solution.py:479
  53.3 14.8 %compute_last.1 = bf16[32,64,128]{2,1,0:T(8,128)(2,1)} custom-call(s32[2]{0:T(128)} %pad_add_fusion.me_ref, bf16[32,80,128]{2,1,0:T(8,128)(2,1)} %copy-done.2, bf16[32,32,128]{2,1,0:T(8,128)(2,1)} %copy-done.3, f32[8,32,512]{2,1,0:T(8,128)} %get-tuple-element.6.refs_1_), custom_call_target="tpu_custom_call" | custom-call | flops 8000000000 | bytes 2000000 | tf_op jit(solution)/shard_map/compute_last/pallas_call | solution.py:494
  68.1 0.0 all-to-all-done.3.in_ref
  68.1 0.0 copy-start.1
  68.1 0.7 copy-done.1
  68.8 5.8 %all-to-all-start.2 = ((bf16[32,64,128]{2,1,0:T(8,128)(2,1)}), bf16[32,64,128]{2,1,0:T(8,128)(2,1)S(1)}, u32[]{:S(2)}, u32[]{:S(2)}) async-start(bf16[32,64,128]{2,1,0:T(8,128)(2,1)} %compute_last.1), calls=%async_computation.2 | async-start | bytes 1048576 | tf_op jit(solution)/shard_map/all_to_all | solution.py:479
  74.6 2.1 %unpack_first.1.held_ref = f32[32,32,256]{2,1,0:T(8,128)} custom-call(bf16[32,32,128]{2,1,0:T(8,128)(2,1)} %copy-done.1), custom_call_target="tpu_custom_call" | custom-call | flops 1000000 | bytes 1000000 | tf_op jit(solution)/shard_map/unpack_first/pallas_call | solution.py:496
  76.7 12.3 %all-to-all-done.2.in_ref = bf16[32,64,128]{2,1,0:T(8,128)(2,1)S(1)} async-done(((bf16[32,64,128]{2,1,0:T(8,128)(2,1)}), bf16[32,64,128]{2,1,0:T(8,128)(2,1)S(1)}, u32[]{:S(2)}, u32[]{:S(2)}) %all-to-all-start.2) | async-done | bytes 524320 | tf_op jit(solution)/shard_map/all_to_all | solution.py:479
  89.0 0.0 copy-start
  89.0 0.8 copy-done
  89.8 3.0 %unpack_last.1 = (f32[32,32,256]{2,1,0:T(8,128)}, f32[32,16,256]{2,1,0:T(8,128)}) custom-call(bf16[32,64,128]{2,1,0:T(8,128)(2,1)} %copy-done, f32[32,32,256]{2,1,0:T(8,128)} %unpack_first.1.held_ref), custom_call_target="tpu_custom_call", output_to_operand_aliasing={{0}: (1, {})} | custom-call | flops 1000000 | bytes 2000000 | tf_op jit(solution)/shard_map/unpack_last/pallas_call | solution.py:497
Async XLA Ops:
  4.4 24.2 %all-to-all-start = ((bf16[32,80,128]{2,1,0:T(8,128)(2,1)}), bf16[32,80,128]{2,1,0:T(8,128)(2,1)S(1)}, u32[]{:S(2)}, u32[]{:S(2)}) async-start(bf16[32,80,128]{2,1,0:T(8,128)(2,1)} %pack_first.1), calls=%async_computation | async-start | bytes 1310720 | tf_op jit(solution)/shard_map/all_to_all | solution.py:479
  28.6 4.3 %copy-start.2 = (bf16[32,80,128]{2,1,0:T(8,128)(2,1)}, bf16[32,80,128]{2,1,0:T(8,128)(2,1)S(1)}, u32[]{:S(2)}) copy-start(bf16[32,80,128]{2,1,0:T(8,128)(2,1)S(1)} %all-to-all-done.first_ref) | copy-start | bytes 1966084
  28.6 18.1 %all-to-all-start.1 = ((bf16[32,32,128]{2,1,0:T(8,128)(2,1)}), bf16[32,32,128]{2,1,0:T(8,128)(2,1)S(1)}, u32[]{:S(2)}, u32[]{:S(2)}) async-start(bf16[32,32,128]{2,1,0:T(8,128)(2,1)} %pack_second.1), calls=%async_computation.1 | async-start | bytes 524288 | tf_op jit(solution)/shard_map/all_to_all | solution.py:479
  46.7 0.7 copy-start.3
  47.4 20.6 %all-to-all-start.3 = ((bf16[32,32,128]{2,1,0:T(8,128)(2,1)}), bf16[32,32,128]{2,1,0:T(8,128)(2,1)S(1)}, u32[]{:S(2)}, u32[]{:S(2)}) async-start(bf16[32,32,128]{2,1,0:T(8,128)(2,1)} %get-tuple-element.7), calls=%async_computation.3 | async-start | bytes 524288 | tf_op jit(solution)/shard_map/all_to_all | solution.py:479
  68.1 0.7 copy-start.1
  68.8 20.2 %all-to-all-start.2 = ((bf16[32,64,128]{2,1,0:T(8,128)(2,1)}), bf16[32,64,128]{2,1,0:T(8,128)(2,1)S(1)}, u32[]{:S(2)}, u32[]{:S(2)}) async-start(bf16[32,64,128]{2,1,0:T(8,128)(2,1)} %compute_last.1), calls=%async_computation.2 | async-start | bytes 1048576 | tf_op jit(solution)/shard_map/all_to_all | solution.py:479
  89.0 0.8 copy-start

commit v2 on v0

--- a/solution.py
+++ b/solution.py
@@ -3,6 +3,8 @@
 import jax
 import jax.numpy as jnp
 from jax import lax
+from jax.experimental import pallas as pl
+from jax.experimental.pallas import tpu as pltpu
 from jax.sharding import PartitionSpec as P
 
 WIN = 8
@@ -69,7 +71,7 @@
     return jnp.transpose(jnp.stack([panel_re, panel_im]), (2, 0, 1, 3))
 
 
-def per_device(src_spec, rcv_spec, lag_table, src_pos, rcv_pos):
+def per_device_general(src_spec, rcv_spec, lag_table, src_pos, rcv_pos):
     src_full = lax.all_gather(src_spec, "rcv", axis=2, tiled=True)
     n_freq = src_full.shape[2]
     src_dev = src_full.shape[3]
@@ -112,6 +114,447 @@
     return (panel_src, panel_rcv)
 
 
+LANES = 128
+ROWS = 32
+LAG_ROWS = 16
+CALLS = ((0,), (3, 2), (1,))
+VMEM = 20 * 2**20
+FULL_VMEM = 56 * 2**20
+TILE_ROWS = 64
+COST = 10**6
+F32 = jnp.float32
+BF16 = jnp.bfloat16
+SIN = [(-1) ** n * (math.pi / 2) ** (2 * n + 1) / math.factorial(2 * n + 1) for n in range(5)]
+COS = [(-1) ** n * (math.pi / 2) ** (2 * n) / math.factorial(2 * n) for n in range(6)]
+
+
+def horner(coefs, v):
+    total = coefs[-1]
+    for coef in coefs[-2::-1]:
+        total = coef + v * total
+    return total
+
+
+def phases(lag, freq, period):
+    turns = lag * freq * (1.0 / period)
+    quarters = 4.0 * (turns - jnp.floor(turns))
+    near = jnp.floor(quarters + 0.5)
+    u = quarters - near
+    v = u * u
+    s = u * horner(SIN, v)
+    c = horner(COS, v)
+    odd = (near == 1.0) | (near == 3.0)
+    cos = jnp.where(odd, s, c)
+    sin = jnp.where(odd, c, s)
+    cos = jnp.where((near == 1.0) | (near == 2.0), -cos, cos)
+    sin = jnp.where((near == 2.0) | (near == 3.0), -sin, sin)
+    return cos, sin
+
+
+def lanes_of(rows):
+    return lax.broadcasted_iota(jnp.int32, (rows, LANES), 1)
+
+
+class Sizes:
+    def __init__(self, shapes, n_src, n_rcv):
+        src_spec, rcv_spec, lag_table = shapes
+        self.n_src, self.n_rcv, self.n_dev = n_src, n_rcv, n_src * n_rcv
+        self.n_slow, self.n_pos = lag_table
+        self.n_win = src_spec[1]
+        self.src_freq, self.src_dev = src_spec[2:]
+        self.rcv_freq, self.rcv_dev = rcv_spec[2:]
+        self.n_freq = self.rcv_freq * n_src
+        self.own = self.n_freq // self.n_dev
+        self.s_all, self.r_all = self.src_dev * n_src, self.rcv_dev * n_rcv
+        self.src_part = self.src_dev // n_rcv
+        self.low = n_src // n_rcv
+        self.chunk = self.own // 2 * ROWS
+
+    def fits(self):
+        return (
+            2 * self.n_win == ROWS
+            and 2 * self.n_slow == ROWS
+            and self.n_win == WIN * SEGS
+            and self.n_rcv == 4
+            and self.own == 8
+            and self.src_freq == self.low * self.n_rcv * self.own
+            and self.rcv_freq == self.n_rcv * self.own
+            and self.n_dev * self.own == self.n_freq == 2 * LANES
+            and 2 * self.src_dev == LANES
+            and self.n_src % 2 == 0
+            and self.rcv_dev == 2 * LANES
+            and self.src_part * self.own == LANES
+            and LANES % self.n_dev == 0
+            and self.n_pos % LANES == 0
+        )
+
+
+def look_up(lag_ref, pos_ref, begin, count, offset):
+    lane = lanes_of(LAG_ROWS)
+    acc = jnp.zeros((LAG_ROWS, LANES), jnp.int32)
+    for n in range(count):
+        pos = pos_ref[begin + n]
+        base = pl.multiple_of((pos // LANES) * LANES, LANES)
+        tile = lag_ref[:, pl.ds(base, LANES)]
+        acc = jnp.where(lane == n, pltpu.roll(tile, (n - pos) & (LANES - 1), 1), acc)
+    return (acc - offset).astype(F32).astype(BF16)
+
+
+def whole(*shape):
+    return pl.BlockSpec(shape, lambda *_: (0,) * len(shape))
+
+
+def pack_sources(z):
+    def kernel(pos_ref, src_ref, lag_ref, out_ref, flat):
+        lags = look_up(lag_ref, pos_ref, 0, z.src_dev, z.n_freq)
+        for row in range(ROWS):
+            flat[row * z.src_freq:(row + 1) * z.src_freq, :z.src_dev] = src_ref[row].astype(F32)
+        half = z.own // 2
+        for rcv in range(z.n_rcv):
+            for low in range(z.low):
+                for m in range(half):
+                    freq = (low * z.n_rcv + rcv) * z.own + m
+                    one = flat[pl.ds(freq, ROWS, stride=z.src_freq), :]
+                    two = flat[pl.ds(freq + half, ROWS, stride=z.src_freq), :]
+                    both = jnp.concatenate([one[:, :z.src_dev], two[:, :z.src_dev]], 1)
+                    out_ref[rcv, low, m * ROWS:(m + 1) * ROWS, :] = both.astype(BF16)
+                out_ref[rcv, low, z.chunk:, :] = lags
+
+    shape = (z.n_rcv, z.low, z.chunk + LAG_ROWS, LANES)
+    return pl.pallas_call(
+        kernel,
+        grid=(1,),
+        in_specs=[
+            pl.BlockSpec(memory_space=pltpu.SMEM),
+            whole(ROWS, z.src_freq, z.src_dev),
+            whole(z.n_slow, z.n_pos),
+        ],
+        out_specs=whole(*shape),
+        out_shape=jax.ShapeDtypeStruct(shape, BF16),
+        scratch_shapes=[pltpu.VMEM((ROWS * z.src_freq, LANES), F32)],
+        compiler_params=pltpu.CompilerParams(vmem_limit_bytes=FULL_VMEM),
+        cost_estimate=pl.CostEstimate(flops=10**6, bytes_accessed=2 * 10**6, transcendentals=0),
+        name="pack_sources",
+    )
+
+
+def pack_receivers(z):
+    def kernel(pos_ref, rcv_ref, lag_ref, *refs):
+        outs, flat = refs[:z.n_rcv], refs[z.n_rcv:]
+        spans = range(0, z.rcv_dev, LANES)
+        lags = [look_up(lag_ref, pos_ref, span, LANES, z.n_freq) for span in spans]
+        for row in range(ROWS):
+            here = rcv_ref[row].astype(F32)
+            for n, span in enumerate(spans):
+                flat[n][row * z.rcv_freq:(row + 1) * z.rcv_freq, :] = here[:, span:span + LANES]
+        for other in range(z.n_rcv):
+            first = (lax.axis_index("rcv") ^ other) * z.own
+            for n, span in enumerate(spans):
+                for k in range(z.own):
+                    tile = flat[n][pl.ds(first + k, ROWS, stride=z.rcv_freq), :]
+                    outs[other][k * ROWS:(k + 1) * ROWS, span:span + LANES] = tile.astype(BF16)
+                outs[other][z.own * ROWS:, span:span + LANES] = lags[n]
+
+    shape = (z.own * ROWS + LAG_ROWS, z.rcv_dev)
+    return pl.pallas_call(
+        kernel,
+        grid=(1,),
+        in_specs=[
+            pl.BlockSpec(memory_space=pltpu.SMEM),
+            whole(ROWS, z.rcv_freq, z.rcv_dev),
+            whole(z.n_slow, z.n_pos),
+        ],
+        out_specs=[whole(*shape)] * z.n_rcv,
+        out_shape=[jax.ShapeDtypeStruct(shape, BF16)] * z.n_rcv,
+        scratch_shapes=[pltpu.VMEM((ROWS * z.rcv_freq, LANES), F32)] * (z.rcv_dev // LANES),
+        compiler_params=pltpu.CompilerParams(vmem_limit_bytes=VMEM),
+        cost_estimate=pl.CostEstimate(flops=10**6, bytes_accessed=2 * 10**6, transcendentals=0),
+        name="pack_receivers",
+    )
+
+
+def cross_spectra(z, src_ref, rcv_refs, turn, left, right, stack):
+    half = z.own // 2
+    begin = pl.multiple_of(turn % half * ROWS, ROWS)
+    odd = turn // half
+    lane = lanes_of(ROWS)
+    blocks = []
+    for block in range(z.s_all // LANES):
+        one = src_ref[2 * block, pl.ds(begin, ROWS), :].astype(F32)
+        two = src_ref[2 * block + 1, pl.ds(begin, ROWS), :].astype(F32)
+        one = jnp.where(odd == 0, one, pltpu.roll(one, z.src_dev, 1))
+        two = jnp.where(odd == 0, pltpu.roll(two, z.src_dev, 1), two)
+        blocks.append(jnp.where(lane < z.src_dev, one, two))
+    left[...] = jnp.transpose(jnp.concatenate(blocks, 1)).astype(BF16)
+    rows = pl.ds(pl.multiple_of(turn * ROWS, ROWS), ROWS)
+    spec = jnp.concatenate([ref[rows, :] for ref in rcv_refs], 1).astype(F32)
+    turned = jnp.concatenate([-spec[z.n_win:], spec[:z.n_win]], 0)
+    window = lax.broadcasted_iota(jnp.int32, (ROWS, 1), 0) % z.n_win
+    for seg in range(SEGS):
+        here = window // WIN == seg
+        right[seg] = jnp.where(here, spec, 0.0).astype(BF16)
+        right[SEGS + seg] = jnp.where(here, turned, 0.0).astype(BF16)
+    width, height = 2 * LANES, TILE_ROWS
+    r_now = spec.shape[1]
+    for col in range(0, r_now, width):
+        for row in range(0, z.s_all, height):
+            part = left[row:row + height, :]
+            total_re, total_im = 0.0, 0.0
+            for seg in range(SEGS):
+                real = jnp.dot(part, right[seg, :, col:col + width], preferred_element_type=F32)
+                imag = jnp.dot(part, right[SEGS + seg, :, col:col + width], preferred_element_type=F32)
+                scale = lax.rsqrt(jnp.maximum(real * real + imag * imag, 1.0))
+                total_re, total_im = total_re + real * scale, total_im + imag * scale
+            stack[row:row + height, col:col + width] = total_re.astype(BF16)
+            stack[z.s_all + row:z.s_all + row + height, col:col + width] = total_im.astype(BF16)
+
+
+def compute(z, count, first, last):
+    src_factor = 1.0 / (SEGS * math.sqrt(z.r_all))
+    rcv_factor = 1.0 / (SEGS * math.sqrt(z.s_all))
+    n = z.n_slow
+    r_now = count * z.rcv_dev
+    place_lag = z.own * ROWS
+
+    def kernel(src_ref, *refs):
+        rcv_refs, refs = refs[:count], refs[count:]
+        if not first:
+            before_ref, refs = refs[0], refs[1:]
+        out_refs, refs = refs[:count], refs[count:]
+        sum_ref, src_lag, rcv_lag, left, right, stack = refs[:6]
+        for src in range(z.n_src):
+            lags = src_ref[src, z.chunk:, :z.src_dev].astype(F32) + float(z.n_freq)
+            src_lag[:, src * z.src_dev:(src + 1) * z.src_dev] = lags
+        for block, ref in enumerate(rcv_refs):
+            rcv_lag[:, block * z.rcv_dev:(block + 1) * z.rcv_dev] = ref[place_lag:, :].astype(F32) + float(z.n_freq)
+        begin = lax.axis_index("src") * z.rcv_freq + lax.axis_index("rcv") * z.own
+
+        def cross(turn, slot):
+            cross_spectra(z, src_ref, rcv_refs, turn, left.at[slot], right.at[slot], stack.at[slot])
+
+        def slant(turn, slot):
+            freq = (begin + turn).astype(F32)
+            src_cos, src_sin = phases(src_lag[...], freq, 2.0 * z.n_freq)
+            rcv_cos, rcv_sin = phases(rcv_lag[...], freq, 2.0 * z.n_freq)
+            upper = jnp.concatenate([src_cos, src_sin], 1)
+            lower = jnp.concatenate([-src_sin, src_cos], 1)
+            both = jnp.concatenate([upper, lower], 0).astype(BF16)
+            over_src = jnp.dot(both, stack[slot], preferred_element_type=F32) * rcv_factor
+            over_re, over_im = over_src[:n], over_src[n:]
+            panel_re = over_re * rcv_cos - over_im * rcv_sin
+            panel_im = over_re * rcv_sin + over_im * rcv_cos
+            panel = jnp.concatenate([panel_re, panel_im], 0).astype(BF16)
+            for block, ref in enumerate(out_refs):
+                ref[turn] = panel[:, block * z.rcv_dev:(block + 1) * z.rcv_dev]
+            dims = (((1,), (1,)), ((), ()))
+            with_re = jnp.concatenate([rcv_cos, rcv_sin], 0).astype(BF16)
+            with_im = jnp.concatenate([-rcv_sin, rcv_cos], 0).astype(BF16)
+            over_rcv = lax.dot_general(with_re, stack[slot, :z.s_all, :], dims, preferred_element_type=F32)
+            over_rcv += lax.dot_general(with_im, stack[slot, z.s_all:, :], dims, preferred_element_type=F32)
+            if not first:
+                over_rcv += before_ref[turn]
+            if not last:
+                sum_ref[turn] = over_rcv
+                return
+            over_rcv *= src_factor
+            over_re, over_im = over_rcv[:n], over_rcv[n:]
+            panel_re = over_re * src_cos + over_im * src_sin
+            panel_im = over_im * src_cos - over_re * src_sin
+            refs[6][turn] = jnp.concatenate([panel_re, panel_im], 0)
+
+        cross(0, 0)
+        for turn in range(1, z.own):
+            cross(turn, turn % 2)
+            slant(turn - 1, (turn - 1) % 2)
+        slant(z.own - 1, (z.own - 1) % 2)
+        if last:
+            send_sources(z, refs[6], sum_ref)
+
+    in_specs = [whole(z.n_src, z.chunk + LAG_ROWS, LANES)]
+    in_specs += [whole(z.own * ROWS + LAG_ROWS, z.rcv_dev)] * count
+    out_specs = [whole(z.own, ROWS, z.rcv_dev)] * count
+    out_shape = [jax.ShapeDtypeStruct((z.own, ROWS, z.rcv_dev), BF16)] * count
+    part_spec = whole(z.own, ROWS, z.s_all)
+    scratch = [
+        pltpu.VMEM((n, z.s_all), F32),
+        pltpu.VMEM((n, r_now), F32),
+        pltpu.VMEM((2, z.s_all, ROWS), BF16),
+        pltpu.VMEM((2, 2 * SEGS, ROWS, r_now), BF16),
+        pltpu.VMEM((2, 2 * z.s_all, r_now), BF16),
+    ]
+    if not first:
+        in_specs.append(part_spec)
+    if last:
+        out_specs.append(whole(z.n_dev, ROWS, LANES))
+        out_shape.append(jax.ShapeDtypeStruct((z.n_dev, ROWS, LANES), BF16))
+        scratch.append(pltpu.VMEM((z.own, ROWS, z.s_all), F32))
+    else:
+        out_specs.append(part_spec)
+        out_shape.append(jax.ShapeDtypeStruct((z.own, ROWS, z.s_all), F32))
+    return pl.pallas_call(
+        kernel,
+        grid=(1,),
+        in_specs=in_specs,
+        out_specs=out_specs,
+        out_shape=out_shape,
+        scratch_shapes=scratch,
+        compiler_params=pltpu.CompilerParams(vmem_limit_bytes=VMEM),
+        cost_estimate=pl.CostEstimate(flops=COST * count, bytes_accessed=10**6, transcendentals=0),
+        name="compute_first" if first else "compute_last" if last else "compute_next",
+    )
+
+
+def send_sources(z, sums, out_ref):
+    lane = lanes_of(ROWS)
+    width = z.src_part
+    for dev in range(z.n_dev):
+        block, place = divmod(dev * width, LANES)
+        total = jnp.zeros((ROWS, LANES), F32)
+        for k in range(z.own):
+            tile = sums[k, :, block * LANES:(block + 1) * LANES]
+            shift = (k * width - place) % LANES
+            moved = pltpu.roll(tile, shift, 1) if shift else tile
+            total = jnp.where((lane >= k * width) & (lane < (k + 1) * width), moved, total)
+        out_ref[dev] = total.astype(BF16)
+
+
+def unpack_block(z, in_ref, flat, write):
+    n = z.n_slow
+    for span in range(0, z.rcv_dev, LANES):
+        for k in range(z.own):
+            flat[k * ROWS:(k + 1) * ROWS, :] = in_ref[k, :, span:span + LANES].astype(F32)
+        for slow in range(n):
+            for part in range(2):
+                write(2 * slow + part, span, flat[pl.ds(part * n + slow, z.own, stride=ROWS), :])
+
+
+def unpack_first(z, others):
+    def kernel(*refs):
+        in_refs, out_ref, flat = refs[:len(others)], refs[-2], refs[-1]
+        for other, in_ref in zip(others, in_refs):
+            rows = pl.ds(pl.multiple_of((lax.axis_index("rcv") ^ other) * z.own, z.own), z.own)
+
+            def write(index, span, tile):
+                out_ref[index, rows, span:span + LANES] = tile
+
+            unpack_block(z, in_ref, flat, write)
+
+    return pl.pallas_call(
+        kernel,
+        grid=(1,),
+        in_specs=[whole(z.own, ROWS, z.rcv_dev)] * len(others),
+        out_specs=whole(ROWS, z.rcv_freq, z.rcv_dev),
+        out_shape=jax.ShapeDtypeStruct((ROWS, z.rcv_freq, z.rcv_dev), F32),
+        scratch_shapes=[pltpu.VMEM((z.own * ROWS, LANES), F32)],
+        compiler_params=pltpu.CompilerParams(vmem_limit_bytes=VMEM),
+        cost_estimate=pl.CostEstimate(flops=10**6, bytes_accessed=10**6, transcendentals=0),
+        name="unpack_first",
+    )
+
+
+def unpack_last(z, other):
+    n = z.n_slow
+    group = LANES // z.n_dev
+    width = z.src_part
+
+    def kernel(rcv_in, src_in, held_ref, rcv_ref, src_ref, flat, small, table):
+        del held_ref
+
+        def write(index, span, tile):
+            rcv_ref[index, :, span:span + LANES] = tile
+
+        unpack_block(z, rcv_in, small, write)
+        for dev in range(z.n_dev):
+            flat[dev * ROWS:(dev + 1) * ROWS, :] = src_in[dev].astype(F32)
+        lane = lanes_of(width)
+        for first in range(0, ROWS, group):
+            tiles = [flat[pl.ds(first + j, z.n_dev, stride=ROWS), :] for j in range(group)]
+            turned = jnp.transpose(jnp.concatenate(tiles, 0))
+            for j in range(group):
+                for block in range(z.own // group):
+                    total = jnp.zeros((width, LANES), F32)
+                    for k in range(group):
+                        row = (block * group + k) * width
+                        tile = turned[row:row + width, :]
+                        shift = (k - j) * z.n_dev % LANES
+                        moved = pltpu.roll(tile, shift, 1) if shift else tile
+                        total = jnp.where((lane >= k * z.n_dev) & (lane < (k + 1) * z.n_dev), moved, total)
+                    rows = slice((first + j) * width, (first + j + 1) * width)
+                    table[rows, block * LANES:(block + 1) * LANES] = total.astype(BF16)
+        here = lax.broadcasted_iota(jnp.int32, (z.n_freq, z.n_freq), 0)
+        there = lax.broadcasted_iota(jnp.int32, (z.n_freq, z.n_freq), 1)
+        order = (there == here % z.n_dev * z.own + here // z.n_dev).astype(F32).astype(BF16)
+        for index in range(ROWS):
+            part, slow = divmod(index, n)
+            rows = table[index * width:(index + 1) * width, :]
+            src_ref[2 * slow + part] = jnp.dot(rows, order, preferred_element_type=F32)
+
+    return pl.pallas_call(
+        kernel,
+        grid=(1,),
+        in_specs=[
+            whole(z.own, ROWS, z.rcv_dev),
+            whole(z.n_dev, ROWS, LANES),
+            pl.BlockSpec(memory_space=pl.ANY),
+        ],
+        out_specs=[
+            pl.BlockSpec((ROWS, z.own, z.rcv_dev), lambda k: (0, lax.axis_index("rcv") ^ other, 0)),
+            whole(ROWS, width, z.n_freq),
+        ],
+        scratch_shapes=[
+            pltpu.VMEM((z.n_dev * ROWS, LANES), F32),
+            pltpu.VMEM((z.own * ROWS, LANES), F32),
+            pltpu.VMEM((ROWS * width, z.n_freq), BF16),
+        ],
+        out_shape=[
+            jax.ShapeDtypeStruct((ROWS, z.rcv_freq, z.rcv_dev), F32),
+            jax.ShapeDtypeStruct((ROWS, width, z.n_freq), F32),
+        ],
+        input_output_aliases={2: 0},
+        compiler_params=pltpu.CompilerParams(vmem_limit_bytes=VMEM),
+        cost_estimate=pl.CostEstimate(flops=10**6, bytes_accessed=2 * 10**6, transcendentals=0),
+        name="unpack_last",
+    )
+
+
+def swap(z, block, other):
+    if other == 0:
+        return block
+    return lax.ppermute(block, "rcv", [(j, j ^ other) for j in range(z.n_rcv)])
+
+
+def per_device(src_spec, rcv_spec, lag_table, src_pos, rcv_pos):
+    n_src, n_rcv = lax.axis_size("src"), lax.axis_size("rcv")
+    z = Sizes((src_spec.shape, rcv_spec.shape, lag_table.shape), n_src, n_rcv)
+    if not z.fits():
+        return per_device_general(src_spec, rcv_spec, lag_table, src_pos, rcv_pos)
+    src_rows = src_spec.reshape(ROWS, z.src_freq, z.src_dev)
+    rcv_rows = rcv_spec.reshape(ROWS, z.rcv_freq, z.rcv_dev)
+    spread = lax.all_to_all(pack_sources(z)(src_pos, src_rows, lag_table), "rcv", 0, 0, tiled=True)
+    packed = pack_receivers(z)(rcv_pos, rcv_rows, lag_table)
+    spread, packed = lax.optimization_barrier((spread, packed))
+    spread = spread.reshape(z.n_src, z.chunk + LAG_ROWS, LANES)
+    sources = lax.all_to_all(spread, "src", 0, 0, tiled=True)
+    blocks = {other: swap(z, packed[other], other) for others in CALLS for other in others}
+    done, carry = {}, ()
+    for n, others in enumerate(CALLS):
+        call = compute(z, len(others), n == 0, n == len(CALLS) - 1)
+        *panels, total = call(sources, *(blocks[other] for other in others), *carry)
+        done.update({other: swap(z, panel, other) for other, panel in zip(others, panels)})
+        carry = (total,)
+    late = CALLS[-1][0]
+    early = tuple(other for others in CALLS[:-1] for other in others)
+    total, arrived = lax.optimization_barrier((total, [done[other] for other in early]))
+    done.update(zip(early, arrived))
+    got_src = lax.all_to_all(total, ("src", "rcv"), 0, 0, tiled=True)
+    held = unpack_first(z, early)(*(done[other] for other in early))
+    panel_rcv, panel_src = unpack_last(z, late)(done[late], got_src, held)
+    return (
+        panel_src.reshape(z.n_slow, 2, z.src_part, z.n_freq),
+        panel_rcv.reshape(z.n_slow, 2, z.rcv_freq, z.rcv_dev),
+    )
+
+
 def solution(mesh):
     placed = (P(None, None, "rcv", "src"), P(None, None, "src", "rcv"), P(), P("src"), P("rcv"))
     return jax.shard_map(

time: 433 us -> 77.5 us (0.18)
  waiting for transfers between devices: 198 us -> 23.5 us
  other arithmetic: 109 us -> 0 us
  local copies, waits for them, and re-layouts: 68.7 us -> 0.68 us
  matrix products: 41.3 us -> 0 us
  Pallas kernels: 0 us -> 30.7 us
  starting transfers between devices: 0.15 us -> 21.5 us
  between operations: 13.8 us -> 0.69 us
    reduce_scatter x2 -> x0, waiting for transfers between devices: 118 us -> none  [the longest x1 74.9 us: per_device(): panel_rcv = lax.psum_scatter(other, 'src', scatter_dimension=2, tiled=True)]
    all_gather x2 -> x0, waiting for transfers between devices: 77.3 us -> none  [the longest x1 39.9 us: per_device(): src_full = lax.all_gather(src_spec, 'rcv', axis=2, tiled=True)]
    dot_general x64 -> x0, matrix products: 41.3 us -> none  [the longest x16 22 us: cross_block(): jnp.einsum('cgwfs,cgwfr->gfsr', swapped, rcv_five, preferred_element_type...]
    convert_element_type x48 -> x0, other arithmetic: 34.9 us -> none  [the longest x16 20.1 us: source_slant(): sin_b = rcv_sin.astype(jnp.bfloat16)]
    pallas_call x0 -> x7, Pallas kernels: none -> 30.7 us  [the longest x3 21.4 us: per_device(): *panels, total = call(sources, *(blocks[other] for other in others), *carry)]
    dynamic_slice x32 -> x0, local copies, waits for them, and re-layouts: 30.6 us -> none  [the longest x16 15.7 us: inner(): rcv_block = lax.dynamic_slice_in_dim(shard_piece, offset, block_width, 2)]
    neg x32 -> x0, other arithmetic: 26.1 us -> none  [the longest x16 17 us: source_slant(): bottom = jnp.concatenate([-sin_b, cos_b], axis=2)]
    another operation x16 -> x0, other arithmetic: 20.7 us -> none  [receiver_outer(): return jnp.transpose(jnp.stack([panel_re, panel_im]), (2, 0, 1, 3))]
  transfers between devices with their start and end apart: 4 -> 9, of which waited for: 4 -> 7; matrix products, arithmetic and copies ran while one was open for 2% -> 0% of each run, Pallas kernels for 0% -> 33%
where the time goes in v2:
time: 77.5 us; the launch traced here: 77.1 us
  Pallas kernels  30.7 us (40%)
  waiting for transfers between devices  23.5 us (30%)
  starting transfers between devices  21.5 us (28%)
    pallas_call x3, Pallas kernels, per_device(): *panels, total = call(sources, *(blocks[other] for other in others), *carry)  21.4 us
    ppermute x6, waiting for transfers between devices, swap(): return lax.ppermute(block, 'rcv', [(j, j ^ other) for j in range(z.n_rcv)])  14.1 us
    ppermute x6, starting transfers between devices, swap(): return lax.ppermute(block, 'rcv', [(j, j ^ other) for j in range(z.n_rcv)])  7.53 us
    all_to_all x1, starting transfers between devices, per_device(): lax.all_to_all(pack_sources(z)(src_pos, src_rows, lag_table), 'rcv', 0, 0...  6.45 us
    all_to_all x1, waiting for transfers between devices, per_device(): lax.all_to_all(pack_sources(z)(src_pos, src_rows, lag_table), 'rcv', 0, 0...  6.25 us
    all_to_all x1, starting transfers between devices, per_device(): got_src = lax.all_to_all(total, ('src', 'rcv'), 0, 0, tiled=True)  3.81 us
    all_to_all x1, starting transfers between devices, per_device(): sources = lax.all_to_all(spread, 'src', 0, 0, tiled=True)  3.72 us
    pallas_call x1, Pallas kernels, per_device(): pack_sources(z)(src_pos, src_rows, lag_table)  3.01 us
  transfers between devices with their start and end apart: 9, of which 7 were waited for; matrix products, arithmetic and copies ran while one was open for 0% of the time, Pallas kernels for 33%

profile of v2, /device:TPU:0, one launch (start us, length us, event | category | flops | bytes accessed | tf_op | source)
XLA Modules:
  0.0 77.1 jit_solution(16494893556558966147)
XLA Ops:
  0.6 0.0 copy-start.1
  0.6 3.0 %pack_sources.1 = bf16[4,2,144,128]{3,2,1,0:T(8,128)(2,1)} custom-call(s32[64]{0:T(128)} %pos_ref.2, bf16[32,64,64]{2,1,0:T(8,128)(2,1)} %bitcast.7, s32[16,8192]{1,0:T(8,128)} %lag_ref.3), custom_call_target="tpu_custom_call" | custom-call | flops 1000000 | bytes 2000000 | tf_op jit(solution)/shard_map/pack_sources/pallas_call | solution.py:533
  3.6 0.0 copy-start
  3.6 6.4 %all-to-all-start = ((bf16[4,2,144,128]{3,2,1,0:T(8,128)(2,1)}), bf16[4,2,144,128]{3,2,1,0:T(8,128)(2,1)}, u32[]{:S(2)}, u32[]{:S(2)}) async-start(bf16[4,2,144,128]{3,2,1,0:T(8,128)(2,1)} %pack_sources.1), calls=%async_computation | async-start | bytes 589824 | tf_op jit(solution)/shard_map/all_to_all | solution.py:533
  10.1 0.0 copy-start.2
  10.1 0.0 copy-done.1
  10.1 0.0 copy-done
  10.1 0.7 copy-done.2
  10.8 2.8 %pack_receivers.1 = (bf16[272,256]{1,0:T(8,128)(2,1)S(1)}, bf16[272,256]{1,0:T(8,128)(2,1)S(1)}, bf16[272,256]{1,0:T(8,128)(2,1)S(1)}, bf16[272,256]{1,0:T(8,128)(2,1)S(1)}) custom-call(s32[256]{0:T(256)S(1)} %copy-done.2, bf16[32,32,256]{2,1,0:T(8,128)(2,1)S(1)} %bitcast.5, s32[16,8192]{1,0:T(8,128)S(1)} %copy-done), custom_call_target="tpu_custom_call" | custom-call | flops 1000000 | bytes 2000000 | tf_op jit(solution)/shard_map/pack_receivers/pallas_call | solution.py:534
  13.6 6.3 %all-to-all-done = bf16[4,2,144,128]{3,2,1,0:T(8,128)(2,1)} async-done(((bf16[4,2,144,128]{3,2,1,0:T(8,128)(2,1)}), bf16[4,2,144,128]{3,2,1,0:T(8,128)(2,1)}, u32[]{:S(2)}, u32[]{:S(2)}) %all-to-all-start) | async-done | bytes 294944 | tf_op jit(solution)/shard_map/all_to_all | solution.py:533
  19.8 3.7 %all-to-all-start.1 = ((bf16[8,144,128]{2,1,0:T(8,128)(2,1)}), bf16[8,144,128]{2,1,0:T(8,128)(2,1)S(1)}, u32[]{:S(2)}, u32[]{:S(2)}) async-start(bf16[8,144,128]{2,1,0:T(8,128)(2,1)} %bitcast.2), calls=%async_computation.1 | async-start | bytes 589824 | tf_op jit(solution)/shard_map/all_to_all | solution.py:537
  23.5 1.4 %collective-permute-start.1 = (bf16[272,256]{1,0:T(8,128)(2,1)S(1)}, bf16[272,256]{1,0:T(8,128)(2,1)S(1)}, u32[]{:S(2)}, u32[]{:S(2)}) collective-permute-start(bf16[272,256]{1,0:T(8,128)(2,1)S(1)} %get-tuple-element.30), channel_id=1, source_target_pairs={{0,3},{1,2},{2,1},{3,0},{4,7},{5,6},{6,5},{7,4},{8,11},{9,10},{10,... | collective-permute-start | bytes 417800 | tf_op jit(solution)/shard_map/ppermute | solution.py:523
  25.0 0.0 collective-permute-start.2
  25.0 2.9 %collective-permute-start = (bf16[272,256]{1,0:T(8,128)(2,1)S(1)}, bf16[272,256]{1,0:T(8,128)(2,1)S(1)}, u32[]{:S(2)}, u32[]{:S(2)}) collective-permute-start(bf16[272,256]{1,0:T(8,128)(2,1)S(1)} %get-tuple-element.29), channel_id=1, source_target_pairs={{0,1},{1,0},{2,3},{3,2},{4,5},{5,4},{6,7},{7,6},{8,9},{9,8},{10,11... | collective-permute-start | bytes 417800 | tf_op jit(solution)/shard_map/ppermute | solution.py:523
  28.0 2.9 %all-to-all-done.1.src_ref = bf16[8,144,128]{2,1,0:T(8,128)(2,1)S(1)} async-done(((bf16[8,144,128]{2,1,0:T(8,128)(2,1)}), bf16[8,144,128]{2,1,0:T(8,128)(2,1)S(1)}, u32[]{:S(2)}, u32[]{:S(2)}) %all-to-all-start.1) | async-done | bytes 294944 | tf_op jit(solution)/shard_map/all_to_all | solution.py:537
  30.8 5.0 %compute_first.1 = (bf16[8,32,256]{2,1,0:T(8,128)(2,1)S(1)}, f32[8,32,512]{2,1,0:T(8,128)S(1)}) custom-call(bf16[8,144,128]{2,1,0:T(8,128)(2,1)S(1)} %all-to-all-done.1.src_ref, bf16[272,256]{1,0:T(8,128)(2,1)S(1)} %get-tuple-element.32.refs_0_), custom_call_target="tpu_custom_call" | custom-call | flops 1000000 | bytes 1000000 | tf_op jit(solution)/shard_map/compute_first/pallas_call | solution.py:542
  35.8 0.0 collective-permute-done.1.refs_0_
  35.8 2.2 %collective-permute-done.2.refs_1_ = bf16[272,256]{1,0:T(8,128)(2,1)S(1)} collective-permute-done((bf16[272,256]{1,0:T(8,128)(2,1)S(1)}, bf16[272,256]{1,0:T(8,128)(2,1)S(1)}, u32[]{:S(2)}, u32[]{:S(2)}) %collective-permute-start.2) | collective-permute-done | bytes 139296 | tf_op jit(solution)/shard_map/ppermute | solution.py:523
  38.0 10.5 %compute_next.1 = (bf16[8,32,256]{2,1,0:T(8,128)(2,1)S(1)}, bf16[8,32,256]{2,1,0:T(8,128)(2,1)S(1)}, f32[8,32,512]{2,1,0:T(8,128)S(1)}) custom-call(bf16[8,144,128]{2,1,0:T(8,128)(2,1)S(1)} %all-to-all-done.1.src_ref, bf16[272,256]{1,0:T(8,128)(2,1)S(1)} %collective-permute-done.1.refs_0_, bf16[272,256]{1,0:T(8,128)(2,1)S(1)} %collective-permute-done.2.refs_1_, ...), custom_call_target="tpu_custom_call" | custom-call | flops 2000000 | bytes 1000000 | tf_op jit(solution)/shard_map/compute_next/pallas_call | solution.py:542
  48.5 1.3 %collective-permute-start.4 = (bf16[8,32,256]{2,1,0:T(8,128)(2,1)S(1)}, bf16[8,32,256]{2,1,0:T(8,128)(2,1)S(1)}, u32[]{:S(2)}, u32[]{:S(2)}) collective-permute-start(bf16[8,32,256]{2,1,0:T(8,128)(2,1)S(1)} %get-tuple-element.38), channel_id=1, source_target_pairs={{0,3},{1,2},{2,1},{3,0},{4,7},{5,6},{6,5},{7,4},{8,11},{9,10},{10,... | collective-permute-start | bytes 393224 | tf_op jit(solution)/shard_map/ppermute | solution.py:523
  49.8 0.0 collective-permute-start.5
  49.8 0.0 collective-permute-done.refs_0_
  49.8 6.0 %compute_last.1 = (bf16[8,32,256]{2,1,0:T(8,128)(2,1)S(1)}, bf16[32,32,128]{2,1,0:T(8,128)(2,1)}) custom-call(bf16[8,144,128]{2,1,0:T(8,128)(2,1)S(1)} %all-to-all-done.1.src_ref, bf16[272,256]{1,0:T(8,128)(2,1)S(1)} %collective-permute-done.refs_0_, f32[8,32,512]{2,1,0:T(8,128)S(1)} %get-tuple-element.34.refs_1_), custom_call_target="tpu_custom_call" | custom-call | flops 1000000 | bytes 1000000 | tf_op jit(solution)/shard_map/compute_last/pallas_call | solution.py:542
  55.8 1.1 %collective-permute-done.4.refs_1_ = bf16[8,32,256]{2,1,0:T(8,128)(2,1)S(1)} collective-permute-done((bf16[8,32,256]{2,1,0:T(8,128)(2,1)S(1)}, bf16[8,32,256]{2,1,0:T(8,128)(2,1)S(1)}, u32[]{:S(2)}, u32[]{:S(2)}) %collective-permute-start.4) | collective-permute-done | bytes 131104 | tf_op jit(solution)/shard_map/ppermute | solution.py:523
  56.9 4.2 %collective-permute-done.5.refs_2_ = bf16[8,32,256]{2,1,0:T(8,128)(2,1)S(1)} collective-permute-done((bf16[8,32,256]{2,1,0:T(8,128)(2,1)S(1)}, bf16[8,32,256]{2,1,0:T(8,128)(2,1)S(1)}, u32[]{:S(2)}, u32[]{:S(2)}) %collective-permute-start.5) | collective-permute-done | bytes 131104 | tf_op jit(solution)/shard_map/ppermute | solution.py:523
  61.1 3.8 %all-to-all-start.2 = ((bf16[32,32,128]{2,1,0:T(8,128)(2,1)}), bf16[32,32,128]{2,1,0:T(8,128)(2,1)S(1)}, u32[]{:S(2)}, u32[]{:S(2)}) async-start(bf16[32,32,128]{2,1,0:T(8,128)(2,1)} %get-tuple-element.40), calls=%async_computation.2 | async-start | bytes 524288 | tf_op jit(solution)/shard_map/all_to_all | solution.py:549
  64.9 1.8 %collective-permute-start.3 = (bf16[8,32,256]{2,1,0:T(8,128)(2,1)S(1)}, bf16[8,32,256]{2,1,0:T(8,128)(2,1)S(1)}, u32[]{:S(2)}, u32[]{:S(2)}) collective-permute-start(bf16[8,32,256]{2,1,0:T(8,128)(2,1)S(1)} %get-tuple-element.35), channel_id=1, source_target_pairs={{0,1},{1,0},{2,3},{3,2},{4,5},{5,4},{6,7},{7,6},{8,9},{9,8},{10,11... | collective-permute-start | bytes 393224 | tf_op jit(solution)/shard_map/ppermute | solution.py:523
  66.8 1.5 %unpack_first.1.held_ref = f32[32,32,256]{2,1,0:T(8,128)} custom-call(bf16[8,32,256]{2,1,0:T(8,128)(2,1)S(1)} %get-tuple-element.41.refs_0_, bf16[8,32,256]{2,1,0:T(8,128)(2,1)S(1)} %collective-permute-done.4.refs_1_, bf16[8,32,256]{2,1,0:T(8,128)(2,1)S(1)} %collective-permute-done.5.refs_2_), custom_call_target="tpu_custom_call" | custom-call | flops 1000000 | bytes 1000000 | tf_op jit(solution)/shard_map/unpack_first/pallas_call | solution.py:550
  68.2 6.6 %collective-permute-done.3.rcv_in = bf16[8,32,256]{2,1,0:T(8,128)(2,1)S(1)} collective-permute-done((bf16[8,32,256]{2,1,0:T(8,128)(2,1)S(1)}, bf16[8,32,256]{2,1,0:T(8,128)(2,1)S(1)}, u32[]{:S(2)}, u32[]{:S(2)}) %collective-permute-start.3) | collective-permute-done | bytes 131104 | tf_op jit(solution)/shard_map/ppermute | solution.py:523
  74.8 0.3 all-to-all-done.2.src_in
  75.1 2.0 %unpack_last.1 = (f32[32,32,256]{2,1,0:T(8,128)}, f32[32,16,256]{2,1,0:T(8,128)}) custom-call(bf16[8,32,256]{2,1,0:T(8,128)(2,1)S(1)} %collective-permute-done.3.rcv_in, bf16[32,32,128]{2,1,0:T(8,128)(2,1)S(1)} %all-to-all-done.2.src_in, f32[32,32,256]{2,1,0:T(8,128)} %unpack_first.1.held_ref), custom_call_target="tpu_custom_call", output_to_operand_aliasing={{0}: (2, {})} | custom-call | flops 1000000 | bytes 2000000 | tf_op jit(solution)/shard_map/unpack_last/pallas_call | solution.py:551
Async XLA Ops:
  0.6 9.5 %copy-start.1 = (bf16[2,16,32,256]{3,2,1,0:T(8,128)(2,1)S(1)}, bf16[2,16,32,256]{3,2,1,0:T(8,128)(2,1)}, u32[]{:S(2)}) copy-start(bf16[2,16,32,256]{3,2,1,0:T(8,128)(2,1)} %param.6) | copy-start | bytes 1572868
  3.6 6.5 %copy-start = (s32[16,8192]{1,0:T(8,128)S(1)}, s32[16,8192]{1,0:T(8,128)}, u32[]{:S(2)}) copy-start(s32[16,8192]{1,0:T(8,128)} %lag_ref.3) | copy-start | bytes 1572868
  3.6 16.2 %all-to-all-start = ((bf16[4,2,144,128]{3,2,1,0:T(8,128)(2,1)}), bf16[4,2,144,128]{3,2,1,0:T(8,128)(2,1)}, u32[]{:S(2)}, u32[]{:S(2)}) async-start(bf16[4,2,144,128]{3,2,1,0:T(8,128)(2,1)} %pack_sources.1), calls=%async_computation | async-start | bytes 589824 | tf_op jit(solution)/shard_map/all_to_all | solution.py:533
  10.1 0.7 copy-start.2
  19.8 11.0 %all-to-all-start.1 = ((bf16[8,144,128]{2,1,0:T(8,128)(2,1)}), bf16[8,144,128]{2,1,0:T(8,128)(2,1)S(1)}, u32[]{:S(2)}, u32[]{:S(2)}) async-start(bf16[8,144,128]{2,1,0:T(8,128)(2,1)} %bitcast.2), calls=%async_computation.1 | async-start | bytes 589824 | tf_op jit(solution)/shard_map/all_to_all | solution.py:537
  23.5 12.3 %collective-permute-start.1 = (bf16[272,256]{1,0:T(8,128)(2,1)S(1)}, bf16[272,256]{1,0:T(8,128)(2,1)S(1)}, u32[]{:S(2)}, u32[]{:S(2)}) collective-permute-start(bf16[272,256]{1,0:T(8,128)(2,1)S(1)} %get-tuple-element.30), channel_id=1, source_target_pairs={{0,3},{1,2},{2,1},{3,0},{4,7},{5,6},{6,5},{7,4},{8,11},{9,10},{10,... | collective-permute-start | bytes 417800 | tf_op jit(solution)/shard_map/ppermute | solution.py:523
  25.0 13.0 %collective-permute-start.2 = (bf16[272,256]{1,0:T(8,128)(2,1)S(1)}, bf16[272,256]{1,0:T(8,128)(2,1)S(1)}, u32[]{:S(2)}, u32[]{:S(2)}) collective-permute-start(bf16[272,256]{1,0:T(8,128)(2,1)S(1)} %get-tuple-element.31), channel_id=1, source_target_pairs={{0,2},{1,3},{2,0},{3,1},{4,6},{5,7},{6,4},{7,5},{8,10},{9,11},{10,... | collective-permute-start | bytes 417800 | tf_op jit(solution)/shard_map/ppermute | solution.py:523
  25.0 24.8 %collective-permute-start = (bf16[272,256]{1,0:T(8,128)(2,1)S(1)}, bf16[272,256]{1,0:T(8,128)(2,1)S(1)}, u32[]{:S(2)}, u32[]{:S(2)}) collective-permute-start(bf16[272,256]{1,0:T(8,128)(2,1)S(1)} %get-tuple-element.29), channel_id=1, source_target_pairs={{0,1},{1,0},{2,3},{3,2},{4,5},{5,4},{6,7},{7,6},{8,9},{9,8},{10,11... | collective-permute-start | bytes 417800 | tf_op jit(solution)/shard_map/ppermute | solution.py:523
  48.5 8.4 %collective-permute-start.4 = (bf16[8,32,256]{2,1,0:T(8,128)(2,1)S(1)}, bf16[8,32,256]{2,1,0:T(8,128)(2,1)S(1)}, u32[]{:S(2)}, u32[]{:S(2)}) collective-permute-start(bf16[8,32,256]{2,1,0:T(8,128)(2,1)S(1)} %get-tuple-element.38), channel_id=1, source_target_pairs={{0,3},{1,2},{2,1},{3,0},{4,7},{5,6},{6,5},{7,4},{8,11},{9,10},{10,... | collective-permute-start | bytes 393224 | tf_op jit(solution)/shard_map/ppermute | solution.py:523
  49.8 11.3 %collective-permute-start.5 = (bf16[8,32,256]{2,1,0:T(8,128)(2,1)S(1)}, bf16[8,32,256]{2,1,0:T(8,128)(2,1)S(1)}, u32[]{:S(2)}, u32[]{:S(2)}) collective-permute-start(bf16[8,32,256]{2,1,0:T(8,128)(2,1)S(1)} %get-tuple-element.39), channel_id=1, source_target_pairs={{0,2},{1,3},{2,0},{3,1},{4,6},{5,7},{6,4},{7,5},{8,10},{9,11},{10,... | collective-permute-start | bytes 393224 | tf_op jit(solution)/shard_map/ppermute | solution.py:523
  61.1 14.0 %all-to-all-start.2 = ((bf16[32,32,128]{2,1,0:T(8,128)(2,1)}), bf16[32,32,128]{2,1,0:T(8,128)(2,1)S(1)}, u32[]{:S(2)}, u32[]{:S(2)}) async-start(bf16[32,32,128]{2,1,0:T(8,128)(2,1)} %get-tuple-element.40), calls=%async_computation.2 | async-start | bytes 524288 | tf_op jit(solution)/shard_map/all_to_all | solution.py:549
  64.9 9.9 %collective-permute-start.3 = (bf16[8,32,256]{2,1,0:T(8,128)(2,1)S(1)}, bf16[8,32,256]{2,1,0:T(8,128)(2,1)S(1)}, u32[]{:S(2)}, u32[]{:S(2)}) collective-permute-start(bf16[8,32,256]{2,1,0:T(8,128)(2,1)S(1)} %get-tuple-element.35), channel_id=1, source_target_pairs={{0,1},{1,0},{2,3},{3,2},{4,5},{5,4},{6,7},{7,6},{8,9},{9,8},{10,11... | collective-permute-start | bytes 393224 | tf_op jit(solution)/shard_map/ppermute | solution.py:523

commit v3 on v2

--- a/solution.py
+++ b/solution.py
@@ -117,7 +117,7 @@
 LANES = 128
 ROWS = 32
 LAG_ROWS = 16
-CALLS = ((0,), (3, 2), (1,))
+CALLS = ((0,), (3,), (2,), (1,))
 VMEM = 20 * 2**20
 FULL_VMEM = 56 * 2**20
 TILE_ROWS = 64
@@ -197,7 +197,7 @@
         base = pl.multiple_of((pos // LANES) * LANES, LANES)
         tile = lag_ref[:, pl.ds(base, LANES)]
         acc = jnp.where(lane == n, pltpu.roll(tile, (n - pos) & (LANES - 1), 1), acc)
-    return (acc - offset).astype(F32).astype(BF16)
+    return (acc - offset).astype(F32)
 
 
 def whole(*shape):
@@ -206,7 +206,8 @@
 
 def pack_sources(z):
     def kernel(pos_ref, src_ref, lag_ref, out_ref, flat):
-        lags = look_up(lag_ref, pos_ref, 0, z.src_dev, z.n_freq)
+        lags = look_up(lag_ref, pos_ref, 0, z.src_dev, z.n_freq)[:, :z.src_dev]
+        lags = jnp.concatenate([lags[:LAG_ROWS // 2], lags[LAG_ROWS // 2:]], 1).astype(BF16)
         for row in range(ROWS):
             flat[row * z.src_freq:(row + 1) * z.src_freq, :z.src_dev] = src_ref[row].astype(F32)
         half = z.own // 2
@@ -220,7 +221,7 @@
                     out_ref[rcv, low, m * ROWS:(m + 1) * ROWS, :] = both.astype(BF16)
                 out_ref[rcv, low, z.chunk:, :] = lags
 
-    shape = (z.n_rcv, z.low, z.chunk + LAG_ROWS, LANES)
+    shape = (z.n_rcv, z.low, z.chunk + LAG_ROWS // 2, LANES)
     return pl.pallas_call(
         kernel,
         grid=(1,),
@@ -242,7 +243,7 @@
     def kernel(pos_ref, rcv_ref, lag_ref, *refs):
         outs, flat = refs[:z.n_rcv], refs[z.n_rcv:]
         spans = range(0, z.rcv_dev, LANES)
-        lags = [look_up(lag_ref, pos_ref, span, LANES, z.n_freq) for span in spans]
+        lags = [look_up(lag_ref, pos_ref, span, LANES, z.n_freq).astype(BF16) for span in spans]
         for row in range(ROWS):
             here = rcv_ref[row].astype(F32)
             for n, span in enumerate(spans):
@@ -323,8 +324,11 @@
         out_refs, refs = refs[:count], refs[count:]
         sum_ref, src_lag, rcv_lag, left, right, stack = refs[:6]
         for src in range(z.n_src):
-            lags = src_ref[src, z.chunk:, :z.src_dev].astype(F32) + float(z.n_freq)
-            src_lag[:, src * z.src_dev:(src + 1) * z.src_dev] = lags
+            lags = src_ref[src, z.chunk:, :].astype(F32) + float(z.n_freq)
+            for part in range(2):
+                rows = slice(part * LAG_ROWS // 2, (part + 1) * LAG_ROWS // 2)
+                lanes = slice(part * z.src_dev, (part + 1) * z.src_dev)
+                src_lag[rows, src * z.src_dev:(src + 1) * z.src_dev] = lags[:, lanes]
         for block, ref in enumerate(rcv_refs):
             rcv_lag[:, block * z.rcv_dev:(block + 1) * z.rcv_dev] = ref[place_lag:, :].astype(F32) + float(z.n_freq)
         begin = lax.axis_index("src") * z.rcv_freq + lax.axis_index("rcv") * z.own
@@ -360,7 +364,15 @@
             over_re, over_im = over_rcv[:n], over_rcv[n:]
             panel_re = over_re * src_cos + over_im * src_sin
             panel_im = over_im * src_cos - over_re * src_sin
-            refs[6][turn] = jnp.concatenate([panel_re, panel_im], 0)
+            panel = jnp.concatenate([panel_re, panel_im], 0)
+            width, acc = z.src_part, refs[6]
+            lanes = slice(turn * width, (turn + 1) * width)
+            for dev in range(z.n_dev):
+                block, place = divmod(dev * width, LANES)
+                tile = panel[:, block * LANES:(block + 1) * LANES]
+                shift = (turn * width - place) % LANES
+                moved = pltpu.roll(tile, shift, 1) if shift else tile
+                acc[dev, :, lanes] = moved[:, lanes]
 
         cross(0, 0)
         for turn in range(1, z.own):
@@ -368,9 +380,9 @@
             slant(turn - 1, (turn - 1) % 2)
         slant(z.own - 1, (z.own - 1) % 2)
         if last:
-            send_sources(z, refs[6], sum_ref)
-
-    in_specs = [whole(z.n_src, z.chunk + LAG_ROWS, LANES)]
+            sum_ref[...] = refs[6][...].astype(BF16)
+
+    in_specs = [whole(z.n_src, z.chunk + LAG_ROWS // 2, LANES)]
     in_specs += [whole(z.own * ROWS + LAG_ROWS, z.rcv_dev)] * count
     out_specs = [whole(z.own, ROWS, z.rcv_dev)] * count
     out_shape = [jax.ShapeDtypeStruct((z.own, ROWS, z.rcv_dev), BF16)] * count
@@ -387,7 +399,7 @@
     if last:
         out_specs.append(whole(z.n_dev, ROWS, LANES))
         out_shape.append(jax.ShapeDtypeStruct((z.n_dev, ROWS, LANES), BF16))
-        scratch.append(pltpu.VMEM((z.own, ROWS, z.s_all), F32))
+        scratch.append(pltpu.VMEM((z.n_dev, ROWS, LANES), F32))
     else:
         out_specs.append(part_spec)
         out_shape.append(jax.ShapeDtypeStruct((z.own, ROWS, z.s_all), F32))
@@ -402,20 +414,6 @@
         cost_estimate=pl.CostEstimate(flops=COST * count, bytes_accessed=10**6, transcendentals=0),
         name="compute_first" if first else "compute_last" if last else "compute_next",
     )
-
-
-def send_sources(z, sums, out_ref):
-    lane = lanes_of(ROWS)
-    width = z.src_part
-    for dev in range(z.n_dev):
-        block, place = divmod(dev * width, LANES)
-        total = jnp.zeros((ROWS, LANES), F32)
-        for k in range(z.own):
-            tile = sums[k, :, block * LANES:(block + 1) * LANES]
-            shift = (k * width - place) % LANES
-            moved = pltpu.roll(tile, shift, 1) if shift else tile
-            total = jnp.where((lane >= k * width) & (lane < (k + 1) * width), moved, total)
-        out_ref[dev] = total.astype(BF16)
 
 
 def unpack_block(z, in_ref, flat, write):
@@ -523,6 +521,12 @@
     return lax.ppermute(block, "rcv", [(j, j ^ other) for j in range(z.n_rcv)])
 
 
+def arrive(done, others, values):
+    here, values = lax.optimization_barrier(([done[other] for other in others], values))
+    done.update(zip(others, here))
+    return values
+
+
 def per_device(src_spec, rcv_spec, lag_table, src_pos, rcv_pos):
     n_src, n_rcv = lax.axis_size("src"), lax.axis_size("rcv")
     z = Sizes((src_spec.shape, rcv_spec.shape, lag_table.shape), n_src, n_rcv)
@@ -533,20 +537,22 @@
     spread = lax.all_to_all(pack_sources(z)(src_pos, src_rows, lag_table), "rcv", 0, 0, tiled=True)
     packed = pack_receivers(z)(rcv_pos, rcv_rows, lag_table)
     spread, packed = lax.optimization_barrier((spread, packed))
-    spread = spread.reshape(z.n_src, z.chunk + LAG_ROWS, LANES)
+    spread = spread.reshape(z.n_src, z.chunk + LAG_ROWS // 2, LANES)
     sources = lax.all_to_all(spread, "src", 0, 0, tiled=True)
     blocks = {other: swap(z, packed[other], other) for others in CALLS for other in others}
     done, carry = {}, ()
     for n, others in enumerate(CALLS):
+        ready = [blocks[other] for other in others]
+        if n >= 2:
+            ready, carry = arrive(done, CALLS[n - 2], (ready, carry))
         call = compute(z, len(others), n == 0, n == len(CALLS) - 1)
-        *panels, total = call(sources, *(blocks[other] for other in others), *carry)
+        *panels, total = call(sources, *ready, *carry)
         done.update({other: swap(z, panel, other) for other, panel in zip(others, panels)})
         carry = (total,)
+    total = arrive(done, CALLS[-2], total)
+    got_src = lax.all_to_all(total, ("src", "rcv"), 0, 0, tiled=True)
     late = CALLS[-1][0]
-    early = tuple(other for others in CALLS[:-1] for other in others)
-    total, arrived = lax.optimization_barrier((total, [done[other] for other in early]))
-    done.update(zip(early, arrived))
-    got_src = lax.all_to_all(total, ("src", "rcv"), 0, 0, tiled=True)
+    early = tuple(other for other in done if other != late)
     held = unpack_first(z, early)(*(done[other] for other in early))
     panel_rcv, panel_src = unpack_last(z, late)(done[late], got_src, held)
     return (

time: 77.5 us -> 70 us (0.903)
  waiting for transfers between devices: 23.5 us -> 16.7 us
    ppermute x6, waiting for transfers between devices: 14.1 us -> 7.76 us  [swap(): return lax.ppermute(block, 'rcv', [(j, j ^ other) for j in range(z.n_rcv)])]
    all_to_all x1, starting transfers between devices: 3.81 us -> 2.63 us  [per_device(): got_src = lax.all_to_all(total, ('src', 'rcv'), 0, 0, tiled=True)]
    pallas_call x3 -> x4, Pallas kernels: 21.4 us -> 21.1 us  [per_device(): *panels, total = call(sources, *ready, *carry)]
  transfers between devices with their start and end apart: 9 -> 9, of which waited for: 7 -> 5; matrix products, arithmetic and copies ran while one was open for 0% -> 0% of each run, Pallas kernels for 33% -> 36%
where the time goes in v3:
time: 70 us; the launch traced here: 69.6 us
  Pallas kernels  30.4 us (43%)
  starting transfers between devices  21.1 us (30%)
  waiting for transfers between devices  16.7 us (24%)
    pallas_call x4, Pallas kernels, per_device(): *panels, total = call(sources, *ready, *carry)  21.1 us
    ppermute x6, starting transfers between devices, swap(): return lax.ppermute(block, 'rcv', [(j, j ^ other) for j in range(z.n_rcv)])  8.3 us
    ppermute x6, waiting for transfers between devices, swap(): return lax.ppermute(block, 'rcv', [(j, j ^ other) for j in range(z.n_rcv)])  7.76 us
    all_to_all x1, starting transfers between devices, per_device(): lax.all_to_all(pack_sources(z)(src_pos, src_rows, lag_table), 'rcv', 0, 0...  6.45 us
    all_to_all x1, waiting for transfers between devices, per_device(): lax.all_to_all(pack_sources(z)(src_pos, src_rows, lag_table), 'rcv', 0, 0...  5.9 us
    all_to_all x1, starting transfers between devices, per_device(): sources = lax.all_to_all(spread, 'src', 0, 0, tiled=True)  3.73 us
    pallas_call x1, Pallas kernels, per_device(): pack_sources(z)(src_pos, src_rows, lag_table)  3.03 us
    pallas_call x1, Pallas kernels, per_device(): packed = pack_receivers(z)(rcv_pos, rcv_rows, lag_table)  2.78 us
  transfers between devices with their start and end apart: 9, of which 5 were waited for; matrix products, arithmetic and copies ran while one was open for 0% of the time, Pallas kernels for 36%

profile of v3, /device:TPU:0, one launch (start us, length us, event | category | flops | bytes accessed | tf_op | source)
XLA Modules:
  0.0 69.6 jit_solution(13021724901111749618)
XLA Ops:
  0.6 0.0 copy-start.1
  0.6 3.0 %pack_sources.1 = bf16[4,2,136,128]{3,2,1,0:T(8,128)(2,1)} custom-call(s32[64]{0:T(128)} %pos_ref.2, bf16[32,64,64]{2,1,0:T(8,128)(2,1)} %bitcast.7, s32[16,8192]{1,0:T(8,128)} %lag_ref.3), custom_call_target="tpu_custom_call" | custom-call | flops 1000000 | bytes 2000000 | tf_op jit(solution)/shard_map/pack_sources/pallas_call | solution.py:537
  3.7 0.0 copy-start
  3.7 6.4 %all-to-all-start = ((bf16[4,2,136,128]{3,2,1,0:T(8,128)(2,1)}), bf16[4,2,136,128]{3,2,1,0:T(8,128)(2,1)}, u32[]{:S(2)}, u32[]{:S(2)}) async-start(bf16[4,2,136,128]{3,2,1,0:T(8,128)(2,1)} %pack_sources.1), calls=%async_computation | async-start | bytes 557056 | tf_op jit(solution)/shard_map/all_to_all | solution.py:537
  10.1 0.0 copy-start.2
  10.1 0.0 copy-done.1
  10.1 0.0 copy-done
  10.1 0.7 copy-done.2
  10.8 2.8 %pack_receivers.1 = (bf16[272,256]{1,0:T(8,128)(2,1)S(1)}, bf16[272,256]{1,0:T(8,128)(2,1)S(1)}, bf16[272,256]{1,0:T(8,128)(2,1)S(1)}, bf16[272,256]{1,0:T(8,128)(2,1)S(1)}) custom-call(s32[256]{0:T(256)S(1)} %copy-done.2, bf16[32,32,256]{2,1,0:T(8,128)(2,1)S(1)} %bitcast.5, s32[16,8192]{1,0:T(8,128)S(1)} %copy-done), custom_call_target="tpu_custom_call" | custom-call | flops 1000000 | bytes 2000000 | tf_op jit(solution)/shard_map/pack_receivers/pallas_call | solution.py:538
  13.6 5.9 %all-to-all-done = bf16[4,2,136,128]{3,2,1,0:T(8,128)(2,1)} async-done(((bf16[4,2,136,128]{3,2,1,0:T(8,128)(2,1)}), bf16[4,2,136,128]{3,2,1,0:T(8,128)(2,1)}, u32[]{:S(2)}, u32[]{:S(2)}) %all-to-all-start) | async-done | bytes 278560 | tf_op jit(solution)/shard_map/all_to_all | solution.py:537
  19.5 3.7 %all-to-all-start.1 = ((bf16[8,136,128]{2,1,0:T(8,128)(2,1)}), bf16[8,136,128]{2,1,0:T(8,128)(2,1)S(1)}, u32[]{:S(2)}, u32[]{:S(2)}) async-start(bf16[8,136,128]{2,1,0:T(8,128)(2,1)} %bitcast.2), calls=%async_computation.1 | async-start | bytes 557056 | tf_op jit(solution)/shard_map/all_to_all | solution.py:541
  23.2 1.4 %collective-permute-start = (bf16[272,256]{1,0:T(8,128)(2,1)S(1)}, bf16[272,256]{1,0:T(8,128)(2,1)S(1)}, u32[]{:S(2)}, u32[]{:S(2)}) collective-permute-start(bf16[272,256]{1,0:T(8,128)(2,1)S(1)} %get-tuple-element.34), channel_id=1, source_target_pairs={{0,3},{1,2},{2,1},{3,0},{4,7},{5,6},{6,5},{7,4},{8,11},{9,10},{10,... | collective-permute-start | bytes 417800 | tf_op jit(solution)/shard_map/ppermute | solution.py:521
  24.7 0.1 collective-permute-start.3
  24.8 2.9 %collective-permute-start.2 = (bf16[272,256]{1,0:T(8,128)(2,1)S(1)}, bf16[272,256]{1,0:T(8,128)(2,1)S(1)}, u32[]{:S(2)}, u32[]{:S(2)}) collective-permute-start(bf16[272,256]{1,0:T(8,128)(2,1)S(1)} %get-tuple-element.38), channel_id=1, source_target_pairs={{0,1},{1,0},{2,3},{3,2},{4,5},{5,4},{6,7},{7,6},{8,9},{9,8},{10,11... | collective-permute-start | bytes 417800 | tf_op jit(solution)/shard_map/ppermute | solution.py:521
  27.6 2.7 %all-to-all-done.1.src_ref = bf16[8,136,128]{2,1,0:T(8,128)(2,1)S(1)} async-done(((bf16[8,136,128]{2,1,0:T(8,128)(2,1)}), bf16[8,136,128]{2,1,0:T(8,128)(2,1)S(1)}, u32[]{:S(2)}, u32[]{:S(2)}) %all-to-all-start.1) | async-done | bytes 278560 | tf_op jit(solution)/shard_map/all_to_all | solution.py:541
  30.3 5.0 %compute_first.1 = (bf16[8,32,256]{2,1,0:T(8,128)(2,1)S(1)}, f32[8,32,512]{2,1,0:T(8,128)S(1)}) custom-call(bf16[8,136,128]{2,1,0:T(8,128)(2,1)S(1)} %all-to-all-done.1.src_ref, bf16[272,256]{1,0:T(8,128)(2,1)S(1)} %get-tuple-element.35.refs_0_), custom_call_target="tpu_custom_call" | custom-call | flops 1000000 | bytes 1000000 | tf_op jit(solution)/shard_map/compute_first/pallas_call | solution.py:549
  35.3 0.0 collective-permute-done.refs_0_
  35.3 5.0 %compute_next.2 = (bf16[8,32,256]{2,1,0:T(8,128)(2,1)S(1)}, f32[8,32,512]{2,1,0:T(8,128)S(1)}) custom-call(bf16[8,136,128]{2,1,0:T(8,128)(2,1)S(1)} %all-to-all-done.1.src_ref, bf16[272,256]{1,0:T(8,128)(2,1)S(1)} %collective-permute-done.refs_0_, f32[8,32,512]{2,1,0:T(8,128)S(1)} %get-tuple-element.36.refs_1_), custom_call_target="tpu_custom_call" | custom-call | flops 1000000 | bytes 1000000 | tf_op jit(solution)/shard_map/compute_next/pallas_call | solution.py:549
  40.3 1.5 %collective-permute-start.1 = (bf16[8,32,256]{2,1,0:T(8,128)(2,1)S(1)}, bf16[8,32,256]{2,1,0:T(8,128)(2,1)S(1)}, u32[]{:S(2)}, u32[]{:S(2)}) collective-permute-start(bf16[8,32,256]{2,1,0:T(8,128)(2,1)S(1)} %get-tuple-element.37), channel_id=1, source_target_pairs={{0,3},{1,2},{2,1},{3,0},{4,7},{5,6},{6,5},{7,4},{8,11},{9,10},{10,... | collective-permute-start | bytes 393224 | tf_op jit(solution)/shard_map/ppermute | solution.py:521
  41.8 0.0 collective-permute-done.3.refs_0_
  41.8 5.2 %compute_next.3 = (bf16[8,32,256]{2,1,0:T(8,128)(2,1)S(1)}, f32[8,32,512]{2,1,0:T(8,128)S(1)}) custom-call(bf16[8,136,128]{2,1,0:T(8,128)(2,1)S(1)} %all-to-all-done.1.src_ref, bf16[272,256]{1,0:T(8,128)(2,1)S(1)} %collective-permute-done.3.refs_0_, f32[8,32,512]{2,1,0:T(8,128)S(1)} %get-tuple-element.43.refs_1_), custom_call_target="tpu_custom_call" | custom-call | flops 1000000 | bytes 1000000 | tf_op jit(solution)/shard_map/compute_next/pallas_call | solution.py:549
  47.0 0.6 collective-permute-start.5
  47.5 0.0 collective-permute-done.2.refs_0_
  47.5 0.0 collective-permute-done.1.refs_1_
  47.6 6.0 %compute_last.1 = (bf16[8,32,256]{2,1,0:T(8,128)(2,1)S(1)}, bf16[32,32,128]{2,1,0:T(8,128)(2,1)}) custom-call(bf16[8,136,128]{2,1,0:T(8,128)(2,1)S(1)} %all-to-all-done.1.src_ref, bf16[272,256]{1,0:T(8,128)(2,1)S(1)} %collective-permute-done.2.refs_0_, f32[8,32,512]{2,1,0:T(8,128)S(1)} %get-tuple-element.46.refs_1_), custom_call_target="tpu_custom_call" | custom-call | flops 1000000 | bytes 1000000 | tf_op jit(solution)/shard_map/compute_last/pallas_call | solution.py:549
  53.5 1.2 %collective-permute-done.5.refs_2_ = bf16[8,32,256]{2,1,0:T(8,128)(2,1)S(1)} collective-permute-done((bf16[8,32,256]{2,1,0:T(8,128)(2,1)S(1)}, bf16[8,32,256]{2,1,0:T(8,128)(2,1)S(1)}, u32[]{:S(2)}, u32[]{:S(2)}) %collective-permute-start.5) | collective-permute-done | bytes 131104 | tf_op jit(solution)/shard_map/ppermute | solution.py:521
  54.7 2.6 %all-to-all-start.2 = ((bf16[32,32,128]{2,1,0:T(8,128)(2,1)}), bf16[32,32,128]{2,1,0:T(8,128)(2,1)S(1)}, u32[]{:S(2)}, u32[]{:S(2)}) async-start(bf16[32,32,128]{2,1,0:T(8,128)(2,1)} %get-tuple-element.50), calls=%async_computation.2 | async-start | bytes 524288 | tf_op jit(solution)/shard_map/all_to_all | solution.py:553
  57.4 1.8 %collective-permute-start.4 = (bf16[8,32,256]{2,1,0:T(8,128)(2,1)S(1)}, bf16[8,32,256]{2,1,0:T(8,128)(2,1)S(1)}, u32[]{:S(2)}, u32[]{:S(2)}) collective-permute-start(bf16[8,32,256]{2,1,0:T(8,128)(2,1)S(1)} %get-tuple-element.47), channel_id=1, source_target_pairs={{0,1},{1,0},{2,3},{3,2},{4,5},{5,4},{6,7},{7,6},{8,9},{9,8},{10,11... | collective-permute-start | bytes 393224 | tf_op jit(solution)/shard_map/ppermute | solution.py:521
  59.2 1.5 %unpack_first.1.held_ref = f32[32,32,256]{2,1,0:T(8,128)} custom-call(bf16[8,32,256]{2,1,0:T(8,128)(2,1)S(1)} %get-tuple-element.51.refs_0_, bf16[8,32,256]{2,1,0:T(8,128)(2,1)S(1)} %collective-permute-done.1.refs_1_, bf16[8,32,256]{2,1,0:T(8,128)(2,1)S(1)} %collective-permute-done.5.refs_2_), custom_call_target="tpu_custom_call" | custom-call | flops 1000000 | bytes 1000000 | tf_op jit(solution)/shard_map/unpack_first/pallas_call | solution.py:556
  60.7 6.6 %collective-permute-done.4.rcv_in = bf16[8,32,256]{2,1,0:T(8,128)(2,1)S(1)} collective-permute-done((bf16[8,32,256]{2,1,0:T(8,128)(2,1)S(1)}, bf16[8,32,256]{2,1,0:T(8,128)(2,1)S(1)}, u32[]{:S(2)}, u32[]{:S(2)}) %collective-permute-start.4) | collective-permute-done | bytes 131104 | tf_op jit(solution)/shard_map/ppermute | solution.py:521
  67.3 0.3 all-to-all-done.2.src_in
  67.6 2.0 %unpack_last.1 = (f32[32,32,256]{2,1,0:T(8,128)}, f32[32,16,256]{2,1,0:T(8,128)}) custom-call(bf16[8,32,256]{2,1,0:T(8,128)(2,1)S(1)} %collective-permute-done.4.rcv_in, bf16[32,32,128]{2,1,0:T(8,128)(2,1)S(1)} %all-to-all-done.2.src_in, f32[32,32,256]{2,1,0:T(8,128)} %unpack_first.1.held_ref), custom_call_target="tpu_custom_call", output_to_operand_aliasing={{0}: (2, {})} | custom-call | flops 1000000 | bytes 2000000 | tf_op jit(solution)/shard_map/unpack_last/pallas_call | solution.py:557
Async XLA Ops:
  0.6 9.5 %copy-start.1 = (bf16[2,16,32,256]{3,2,1,0:T(8,128)(2,1)S(1)}, bf16[2,16,32,256]{3,2,1,0:T(8,128)(2,1)}, u32[]{:S(2)}) copy-start(bf16[2,16,32,256]{3,2,1,0:T(8,128)(2,1)} %param.6) | copy-start | bytes 1572868
  3.7 6.5 %copy-start = (s32[16,8192]{1,0:T(8,128)S(1)}, s32[16,8192]{1,0:T(8,128)}, u32[]{:S(2)}) copy-start(s32[16,8192]{1,0:T(8,128)} %lag_ref.3) | copy-start | bytes 1572868
  3.7 15.8 %all-to-all-start = ((bf16[4,2,136,128]{3,2,1,0:T(8,128)(2,1)}), bf16[4,2,136,128]{3,2,1,0:T(8,128)(2,1)}, u32[]{:S(2)}, u32[]{:S(2)}) async-start(bf16[4,2,136,128]{3,2,1,0:T(8,128)(2,1)} %pack_sources.1), calls=%async_computation | async-start | bytes 557056 | tf_op jit(solution)/shard_map/all_to_all | solution.py:537
  10.1 0.7 copy-start.2
  19.5 10.8 %all-to-all-start.1 = ((bf16[8,136,128]{2,1,0:T(8,128)(2,1)}), bf16[8,136,128]{2,1,0:T(8,128)(2,1)S(1)}, u32[]{:S(2)}, u32[]{:S(2)}) async-start(bf16[8,136,128]{2,1,0:T(8,128)(2,1)} %bitcast.2), calls=%async_computation.1 | async-start | bytes 557056 | tf_op jit(solution)/shard_map/all_to_all | solution.py:541
  23.2 12.1 %collective-permute-start = (bf16[272,256]{1,0:T(8,128)(2,1)S(1)}, bf16[272,256]{1,0:T(8,128)(2,1)S(1)}, u32[]{:S(2)}, u32[]{:S(2)}) collective-permute-start(bf16[272,256]{1,0:T(8,128)(2,1)S(1)} %get-tuple-element.34), channel_id=1, source_target_pairs={{0,3},{1,2},{2,1},{3,0},{4,7},{5,6},{6,5},{7,4},{8,11},{9,10},{10,... | collective-permute-start | bytes 417800 | tf_op jit(solution)/shard_map/ppermute | solution.py:521
  24.7 17.1 %collective-permute-start.3 = (bf16[272,256]{1,0:T(8,128)(2,1)S(1)}, bf16[272,256]{1,0:T(8,128)(2,1)S(1)}, u32[]{:S(2)}, u32[]{:S(2)}) collective-permute-start(bf16[272,256]{1,0:T(8,128)(2,1)S(1)} %get-tuple-element.40), channel_id=1, source_target_pairs={{0,2},{1,3},{2,0},{3,1},{4,6},{5,7},{6,4},{7,5},{8,10},{9,11},{10,... | collective-permute-start | bytes 417800 | tf_op jit(solution)/shard_map/ppermute | solution.py:521
  24.8 22.8 %collective-permute-start.2 = (bf16[272,256]{1,0:T(8,128)(2,1)S(1)}, bf16[272,256]{1,0:T(8,128)(2,1)S(1)}, u32[]{:S(2)}, u32[]{:S(2)}) collective-permute-start(bf16[272,256]{1,0:T(8,128)(2,1)S(1)} %get-tuple-element.38), channel_id=1, source_target_pairs={{0,1},{1,0},{2,3},{3,2},{4,5},{5,4},{6,7},{7,6},{8,9},{9,8},{10,11... | collective-permute-start | bytes 417800 | tf_op jit(solution)/shard_map/ppermute | solution.py:521
  40.3 7.2 %collective-permute-start.1 = (bf16[8,32,256]{2,1,0:T(8,128)(2,1)S(1)}, bf16[8,32,256]{2,1,0:T(8,128)(2,1)S(1)}, u32[]{:S(2)}, u32[]{:S(2)}) collective-permute-start(bf16[8,32,256]{2,1,0:T(8,128)(2,1)S(1)} %get-tuple-element.37), channel_id=1, source_target_pairs={{0,3},{1,2},{2,1},{3,0},{4,7},{5,6},{6,5},{7,4},{8,11},{9,10},{10,... | collective-permute-start | bytes 393224 | tf_op jit(solution)/shard_map/ppermute | solution.py:521
  47.0 7.8 %collective-permute-start.5 = (bf16[8,32,256]{2,1,0:T(8,128)(2,1)S(1)}, bf16[8,32,256]{2,1,0:T(8,128)(2,1)S(1)}, u32[]{:S(2)}, u32[]{:S(2)}) collective-permute-start(bf16[8,32,256]{2,1,0:T(8,128)(2,1)S(1)} %get-tuple-element.48), channel_id=1, source_target_pairs={{0,2},{1,3},{2,0},{3,1},{4,6},{5,7},{6,4},{7,5},{8,10},{9,11},{10,... | collective-permute-start | bytes 393224 | tf_op jit(solution)/shard_map/ppermute | solution.py:521
  54.7 12.8 %all-to-all-start.2 = ((bf16[32,32,128]{2,1,0:T(8,128)(2,1)}), bf16[32,32,128]{2,1,0:T(8,128)(2,1)S(1)}, u32[]{:S(2)}, u32[]{:S(2)}) async-start(bf16[32,32,128]{2,1,0:T(8,128)(2,1)} %get-tuple-element.50), calls=%async_computation.2 | async-start | bytes 524288 | tf_op jit(solution)/shard_map/all_to_all | solution.py:553
  57.4 9.9 %collective-permute-start.4 = (bf16[8,32,256]{2,1,0:T(8,128)(2,1)S(1)}, bf16[8,32,256]{2,1,0:T(8,128)(2,1)S(1)}, u32[]{:S(2)}, u32[]{:S(2)}) collective-permute-start(bf16[8,32,256]{2,1,0:T(8,128)(2,1)S(1)} %get-tuple-element.47), channel_id=1, source_target_pairs={{0,1},{1,0},{2,3},{3,2},{4,5},{5,4},{6,7},{7,6},{8,9},{9,8},{10,11... | collective-permute-start | bytes 393224 | tf_op jit(solution)/shard_map/ppermute | solution.py:521

commit v4 on v3

--- a/solution.py
+++ b/solution.py
@@ -120,7 +120,7 @@
 CALLS = ((0,), (3,), (2,), (1,))
 VMEM = 20 * 2**20
 FULL_VMEM = 56 * 2**20
-TILE_ROWS = 64
+TILE_ROWS = 256
 COST = 10**6
 F32 = jnp.float32
 BF16 = jnp.bfloat16
@@ -177,6 +177,7 @@
             and self.n_win == WIN * SEGS
             and self.n_rcv == 4
             and self.own == 8
+            and self.own // 2 * ROWS == LANES
             and self.src_freq == self.low * self.n_rcv * self.own
             and self.rcv_freq == self.n_rcv * self.own
             and self.n_dev * self.own == self.n_freq == 2 * LANES
@@ -213,12 +214,11 @@
         half = z.own // 2
         for rcv in range(z.n_rcv):
             for low in range(z.low):
-                for m in range(half):
-                    freq = (low * z.n_rcv + rcv) * z.own + m
-                    one = flat[pl.ds(freq, ROWS, stride=z.src_freq), :]
-                    two = flat[pl.ds(freq + half, ROWS, stride=z.src_freq), :]
-                    both = jnp.concatenate([one[:, :z.src_dev], two[:, :z.src_dev]], 1)
-                    out_ref[rcv, low, m * ROWS:(m + 1) * ROWS, :] = both.astype(BF16)
+                for group in range(2):
+                    freq = (low * z.n_rcv + rcv) * z.own + group * half
+                    tiles = [flat[pl.ds(freq + m, ROWS, stride=z.src_freq), :] for m in range(half)]
+                    turned = jnp.transpose(jnp.concatenate(tiles, 0))[:z.src_dev]
+                    out_ref[rcv, low, group * z.src_dev:(group + 1) * z.src_dev, :] = turned.astype(BF16)
                 out_ref[rcv, low, z.chunk:, :] = lags
 
     shape = (z.n_rcv, z.low, z.chunk + LAG_ROWS // 2, LANES)
@@ -274,32 +274,25 @@
     )
 
 
-def cross_spectra(z, src_ref, rcv_refs, turn, left, right, stack):
+def cross_spectra(z, src_ref, rcv_refs, turn, right, stack):
     half = z.own // 2
-    begin = pl.multiple_of(turn % half * ROWS, ROWS)
-    odd = turn // half
-    lane = lanes_of(ROWS)
-    blocks = []
-    for block in range(z.s_all // LANES):
-        one = src_ref[2 * block, pl.ds(begin, ROWS), :].astype(F32)
-        two = src_ref[2 * block + 1, pl.ds(begin, ROWS), :].astype(F32)
-        one = jnp.where(odd == 0, one, pltpu.roll(one, z.src_dev, 1))
-        two = jnp.where(odd == 0, pltpu.roll(two, z.src_dev, 1), two)
-        blocks.append(jnp.where(lane < z.src_dev, one, two))
-    left[...] = jnp.transpose(jnp.concatenate(blocks, 1)).astype(BF16)
-    rows = pl.ds(pl.multiple_of(turn * ROWS, ROWS), ROWS)
+    group, place = divmod(turn, half)
+    begin = place * ROWS
+    rows = slice(turn * ROWS, (turn + 1) * ROWS)
     spec = jnp.concatenate([ref[rows, :] for ref in rcv_refs], 1).astype(F32)
     turned = jnp.concatenate([-spec[z.n_win:], spec[:z.n_win]], 0)
     window = lax.broadcasted_iota(jnp.int32, (ROWS, 1), 0) % z.n_win
     for seg in range(SEGS):
         here = window // WIN == seg
-        right[seg] = jnp.where(here, spec, 0.0).astype(BF16)
-        right[SEGS + seg] = jnp.where(here, turned, 0.0).astype(BF16)
+        right[seg, begin:begin + ROWS, :] = jnp.where(here, spec, 0.0).astype(BF16)
+        right[SEGS + seg, begin:begin + ROWS, :] = jnp.where(here, turned, 0.0).astype(BF16)
     width, height = 2 * LANES, TILE_ROWS
     r_now = spec.shape[1]
     for col in range(0, r_now, width):
         for row in range(0, z.s_all, height):
-            part = left[row:row + height, :]
+            senders = range(row // z.src_dev, (row + height) // z.src_dev)
+            lines = slice(group * z.src_dev, (group + 1) * z.src_dev)
+            part = jnp.concatenate([src_ref[sender, lines, :] for sender in senders], 0)
             total_re, total_im = 0.0, 0.0
             for seg in range(SEGS):
                 real = jnp.dot(part, right[seg, :, col:col + width], preferred_element_type=F32)
@@ -322,24 +315,32 @@
         if not first:
             before_ref, refs = refs[0], refs[1:]
         out_refs, refs = refs[:count], refs[count:]
-        sum_ref, src_lag, rcv_lag, left, right, stack = refs[:6]
+        sum_ref, lag, waves, right, stack = refs[:5]
+        right[...] = jnp.zeros_like(right)
         for src in range(z.n_src):
             lags = src_ref[src, z.chunk:, :].astype(F32) + float(z.n_freq)
             for part in range(2):
                 rows = slice(part * LAG_ROWS // 2, (part + 1) * LAG_ROWS // 2)
                 lanes = slice(part * z.src_dev, (part + 1) * z.src_dev)
-                src_lag[rows, src * z.src_dev:(src + 1) * z.src_dev] = lags[:, lanes]
+                lag[rows, src * z.src_dev:(src + 1) * z.src_dev] = lags[:, lanes]
         for block, ref in enumerate(rcv_refs):
-            rcv_lag[:, block * z.rcv_dev:(block + 1) * z.rcv_dev] = ref[place_lag:, :].astype(F32) + float(z.n_freq)
+            place = z.s_all + block * z.rcv_dev
+            lag[:, place:place + z.rcv_dev] = ref[place_lag:, :].astype(F32) + float(z.n_freq)
         begin = lax.axis_index("src") * z.rcv_freq + lax.axis_index("rcv") * z.own
+        waves[0], waves[1] = phases(lag[...], begin.astype(F32), 2.0 * z.n_freq)
+        waves[2], waves[3] = phases(lag[...], 1.0, 2.0 * z.n_freq)
+
+        def next_waves():
+            cos, sin = waves[0], waves[1]
+            step_cos, step_sin = waves[2], waves[3]
+            waves[0], waves[1] = cos * step_cos - sin * step_sin, sin * step_cos + cos * step_sin
+            return cos[:, :z.s_all], sin[:, :z.s_all], cos[:, z.s_all:], sin[:, z.s_all:]
 
         def cross(turn, slot):
-            cross_spectra(z, src_ref, rcv_refs, turn, left.at[slot], right.at[slot], stack.at[slot])
+            cross_spectra(z, src_ref, rcv_refs, turn, right.at[turn % (z.own // 2)], stack.at[slot])
 
         def slant(turn, slot):
-            freq = (begin + turn).astype(F32)
-            src_cos, src_sin = phases(src_lag[...], freq, 2.0 * z.n_freq)
-            rcv_cos, rcv_sin = phases(rcv_lag[...], freq, 2.0 * z.n_freq)
+            src_cos, src_sin, rcv_cos, rcv_sin = next_waves()
             upper = jnp.concatenate([src_cos, src_sin], 1)
             lower = jnp.concatenate([-src_sin, src_cos], 1)
             both = jnp.concatenate([upper, lower], 0).astype(BF16)
@@ -364,15 +365,7 @@
             over_re, over_im = over_rcv[:n], over_rcv[n:]
             panel_re = over_re * src_cos + over_im * src_sin
             panel_im = over_im * src_cos - over_re * src_sin
-            panel = jnp.concatenate([panel_re, panel_im], 0)
-            width, acc = z.src_part, refs[6]
-            lanes = slice(turn * width, (turn + 1) * width)
-            for dev in range(z.n_dev):
-                block, place = divmod(dev * width, LANES)
-                tile = panel[:, block * LANES:(block + 1) * LANES]
-                shift = (turn * width - place) % LANES
-                moved = pltpu.roll(tile, shift, 1) if shift else tile
-                acc[dev, :, lanes] = moved[:, lanes]
+            refs[5][turn] = jnp.concatenate([panel_re, panel_im], 0)
 
         cross(0, 0)
         for turn in range(1, z.own):
@@ -380,7 +373,7 @@
             slant(turn - 1, (turn - 1) % 2)
         slant(z.own - 1, (z.own - 1) % 2)
         if last:
-            sum_ref[...] = refs[6][...].astype(BF16)
+            send_sources(z, refs[5], sum_ref)
 
     in_specs = [whole(z.n_src, z.chunk + LAG_ROWS // 2, LANES)]
     in_specs += [whole(z.own * ROWS + LAG_ROWS, z.rcv_dev)] * count
@@ -388,10 +381,9 @@
     out_shape = [jax.ShapeDtypeStruct((z.own, ROWS, z.rcv_dev), BF16)] * count
     part_spec = whole(z.own, ROWS, z.s_all)
     scratch = [
-        pltpu.VMEM((n, z.s_all), F32),
-        pltpu.VMEM((n, r_now), F32),
-        pltpu.VMEM((2, z.s_all, ROWS), BF16),
-        pltpu.VMEM((2, 2 * SEGS, ROWS, r_now), BF16),
+        pltpu.VMEM((n, z.s_all + r_now), F32),
+        pltpu.VMEM((4, n, z.s_all + r_now), F32),
+        pltpu.VMEM((z.own // 2, 2 * SEGS, LANES, r_now), BF16),
         pltpu.VMEM((2, 2 * z.s_all, r_now), BF16),
     ]
     if not first:
@@ -399,7 +391,7 @@
     if last:
         out_specs.append(whole(z.n_dev, ROWS, LANES))
         out_shape.append(jax.ShapeDtypeStruct((z.n_dev, ROWS, LANES), BF16))
-        scratch.append(pltpu.VMEM((z.n_dev, ROWS, LANES), F32))
+        scratch.append(pltpu.VMEM((z.own, ROWS, z.s_all), F32))
     else:
         out_specs.append(part_spec)
         out_shape.append(jax.ShapeDtypeStruct((z.own, ROWS, z.s_all), F32))
@@ -414,6 +406,24 @@
         cost_estimate=pl.CostEstimate(flops=COST * count, bytes_accessed=10**6, transcendentals=0),
         name="compute_first" if first else "compute_last" if last else "compute_next",
     )
+
+
+def send_sources(z, sums, out_ref):
+    lane = lanes_of(ROWS)
+    for block in range(z.s_all // LANES):
+        tiles = [sums[k, :, block * LANES:(block + 1) * LANES] for k in range(z.own)]
+        bit = 1
+        while bit < z.own:
+            shift = bit * z.src_part
+            upper = lane & shift != 0
+            for k in range(z.own):
+                if not k & bit:
+                    one, two = tiles[k], tiles[k | bit]
+                    tiles[k] = jnp.where(upper, pltpu.roll(two, shift, 1), one)
+                    tiles[k | bit] = jnp.where(upper, two, pltpu.roll(one, LANES - shift, 1))
+            bit *= 2
+        for group in range(z.own):
+            out_ref[block * z.own + group] = tiles[group].astype(BF16)
 
 
 def unpack_block(z, in_ref, flat, write):

time: 70 us -> 67.8 us (0.969)
  Pallas kernels: 30.4 us -> 27.5 us
    pallas_call x4, Pallas kernels: 21.1 us -> 18.2 us  [per_device(): *panels, total = call(sources, *ready, *carry)]
    ppermute x6, starting transfers between devices: 8.3 us -> 9.02 us  [swap(): return lax.ppermute(block, 'rcv', [(j, j ^ other) for j in range(z.n_rcv)])]
  transfers between devices with their start and end apart: 9 -> 9, of which waited for: 5 -> 5; matrix products, arithmetic and copies ran while one was open for 0% -> 0% of each run, Pallas kernels for 36% -> 33%
where the time goes in v4:
time: 67.8 us; the launch traced here: 67.4 us
  Pallas kernels  27.5 us (41%)
  starting transfers between devices  21.8 us (32%)
  waiting for transfers between devices  16.7 us (25%)
  local copies, waits for them, and re-layouts  0.68 us (1%)
  between operations  0.68 us (1%)
    pallas_call x4, Pallas kernels, per_device(): *panels, total = call(sources, *ready, *carry)  18.2 us
    ppermute x6, starting transfers between devices, swap(): return lax.ppermute(block, 'rcv', [(j, j ^ other) for j in range(z.n_rcv)])  9.02 us
    ppermute x6, waiting for transfers between devices, swap(): return lax.ppermute(block, 'rcv', [(j, j ^ other) for j in range(z.n_rcv)])  7.75 us
    all_to_all x1, starting transfers between devices, per_device(): lax.all_to_all(pack_sources(z)(src_pos, src_rows, lag_table), 'rcv', 0, 0...  6.45 us
    all_to_all x1, waiting for transfers between devices, per_device(): lax.all_to_all(pack_sources(z)(src_pos, src_rows, lag_table), 'rcv', 0, 0...  5.9 us
    all_to_all x1, starting transfers between devices, per_device(): sources = lax.all_to_all(spread, 'src', 0, 0, tiled=True)  3.72 us
    pallas_call x1, Pallas kernels, per_device(): pack_sources(z)(src_pos, src_rows, lag_table)  3.03 us
    pallas_call x1, Pallas kernels, per_device(): packed = pack_receivers(z)(rcv_pos, rcv_rows, lag_table)  2.78 us
  transfers between devices with their start and end apart: 9, of which 5 were waited for; matrix products, arithmetic and copies ran while one was open for 0% of the time, Pallas kernels for 33%

profile of v4, /device:TPU:0, one launch (start us, length us, event | category | flops | bytes accessed | tf_op | source)
XLA Modules:
  0.0 67.4 jit_solution(12653660557199870067)
XLA Ops:
  0.6 0.0 copy-start.1
  0.6 3.0 %pack_sources.1 = bf16[4,2,136,128]{3,2,1,0:T(8,128)(2,1)} custom-call(s32[64]{0:T(128)} %pos_ref.2, bf16[32,64,64]{2,1,0:T(8,128)(2,1)} %bitcast.7, s32[16,8192]{1,0:T(8,128)} %lag_ref.3), custom_call_target="tpu_custom_call" | custom-call | flops 1000000 | bytes 2000000 | tf_op jit(solution)/shard_map/pack_sources/pallas_call | solution.py:547
  3.7 0.0 copy-start
  3.7 6.4 %all-to-all-start = ((bf16[4,2,136,128]{3,2,1,0:T(8,128)(2,1)}), bf16[4,2,136,128]{3,2,1,0:T(8,128)(2,1)}, u32[]{:S(2)}, u32[]{:S(2)}) async-start(bf16[4,2,136,128]{3,2,1,0:T(8,128)(2,1)} %pack_sources.1), calls=%async_computation | async-start | bytes 557056 | tf_op jit(solution)/shard_map/all_to_all | solution.py:547
  10.1 0.0 copy-start.2
  10.1 0.0 copy-done.1
  10.1 0.0 copy-done
  10.1 0.7 copy-done.2
  10.8 2.8 %pack_receivers.1 = (bf16[272,256]{1,0:T(8,128)(2,1)S(1)}, bf16[272,256]{1,0:T(8,128)(2,1)S(1)}, bf16[272,256]{1,0:T(8,128)(2,1)S(1)}, bf16[272,256]{1,0:T(8,128)(2,1)S(1)}) custom-call(s32[256]{0:T(256)S(1)} %copy-done.2, bf16[32,32,256]{2,1,0:T(8,128)(2,1)S(1)} %bitcast.5, s32[16,8192]{1,0:T(8,128)S(1)} %copy-done), custom_call_target="tpu_custom_call" | custom-call | flops 1000000 | bytes 2000000 | tf_op jit(solution)/shard_map/pack_receivers/pallas_call | solution.py:548
  13.6 5.9 %all-to-all-done = bf16[4,2,136,128]{3,2,1,0:T(8,128)(2,1)} async-done(((bf16[4,2,136,128]{3,2,1,0:T(8,128)(2,1)}), bf16[4,2,136,128]{3,2,1,0:T(8,128)(2,1)}, u32[]{:S(2)}, u32[]{:S(2)}) %all-to-all-start) | async-done | bytes 278560 | tf_op jit(solution)/shard_map/all_to_all | solution.py:547
  19.5 3.7 %all-to-all-start.1 = ((bf16[8,136,128]{2,1,0:T(8,128)(2,1)}), bf16[8,136,128]{2,1,0:T(8,128)(2,1)S(1)}, u32[]{:S(2)}, u32[]{:S(2)}) async-start(bf16[8,136,128]{2,1,0:T(8,128)(2,1)} %bitcast.2), calls=%async_computation.1 | async-start | bytes 557056 | tf_op jit(solution)/shard_map/all_to_all | solution.py:551
  23.2 1.4 %collective-permute-start = (bf16[272,256]{1,0:T(8,128)(2,1)S(1)}, bf16[272,256]{1,0:T(8,128)(2,1)S(1)}, u32[]{:S(2)}, u32[]{:S(2)}) collective-permute-start(bf16[272,256]{1,0:T(8,128)(2,1)S(1)} %get-tuple-element.34), channel_id=1, source_target_pairs={{0,3},{1,2},{2,1},{3,0},{4,7},{5,6},{6,5},{7,4},{8,11},{9,10},{10,... | collective-permute-start | bytes 417800 | tf_op jit(solution)/shard_map/ppermute | solution.py:531
  24.7 0.1 collective-permute-start.3
  24.8 2.9 %collective-permute-start.2 = (bf16[272,256]{1,0:T(8,128)(2,1)S(1)}, bf16[272,256]{1,0:T(8,128)(2,1)S(1)}, u32[]{:S(2)}, u32[]{:S(2)}) collective-permute-start(bf16[272,256]{1,0:T(8,128)(2,1)S(1)} %get-tuple-element.38), channel_id=1, source_target_pairs={{0,1},{1,0},{2,3},{3,2},{4,5},{5,4},{6,7},{7,6},{8,9},{9,8},{10,11... | collective-permute-start | bytes 417800 | tf_op jit(solution)/shard_map/ppermute | solution.py:531
  27.6 2.7 %all-to-all-done.1.src_ref = bf16[8,136,128]{2,1,0:T(8,128)(2,1)S(1)} async-done(((bf16[8,136,128]{2,1,0:T(8,128)(2,1)}), bf16[8,136,128]{2,1,0:T(8,128)(2,1)S(1)}, u32[]{:S(2)}, u32[]{:S(2)}) %all-to-all-start.1) | async-done | bytes 278560 | tf_op jit(solution)/shard_map/all_to_all | solution.py:551
  30.3 4.2 %compute_first.1 = (bf16[8,32,256]{2,1,0:T(8,128)(2,1)S(1)}, f32[8,32,512]{2,1,0:T(8,128)S(1)}) custom-call(bf16[8,136,128]{2,1,0:T(8,128)(2,1)S(1)} %all-to-all-done.1.src_ref, bf16[272,256]{1,0:T(8,128)(2,1)S(1)} %get-tuple-element.35.refs_0_), custom_call_target="tpu_custom_call" | custom-call | flops 1000000 | bytes 1000000 | tf_op jit(solution)/shard_map/compute_first/pallas_call | solution.py:559
  34.6 0.0 collective-permute-done.refs_0_
  34.6 4.3 %compute_next.2 = (bf16[8,32,256]{2,1,0:T(8,128)(2,1)S(1)}, f32[8,32,512]{2,1,0:T(8,128)S(1)}) custom-call(bf16[8,136,128]{2,1,0:T(8,128)(2,1)S(1)} %all-to-all-done.1.src_ref, bf16[272,256]{1,0:T(8,128)(2,1)S(1)} %collective-permute-done.refs_0_, f32[8,32,512]{2,1,0:T(8,128)S(1)} %get-tuple-element.36.refs_1_), custom_call_target="tpu_custom_call" | custom-call | flops 1000000 | bytes 1000000 | tf_op jit(solution)/shard_map/compute_next/pallas_call | solution.py:559
  38.8 1.5 %collective-permute-start.1 = (bf16[8,32,256]{2,1,0:T(8,128)(2,1)S(1)}, bf16[8,32,256]{2,1,0:T(8,128)(2,1)S(1)}, u32[]{:S(2)}, u32[]{:S(2)}) collective-permute-start(bf16[8,32,256]{2,1,0:T(8,128)(2,1)S(1)} %get-tuple-element.37), channel_id=1, source_target_pairs={{0,3},{1,2},{2,1},{3,0},{4,7},{5,6},{6,5},{7,4},{8,11},{9,10},{10,... | collective-permute-start | bytes 393224 | tf_op jit(solution)/shard_map/ppermute | solution.py:531
  40.3 0.0 collective-permute-done.3.refs_0_
  40.3 4.5 %compute_next.3 = (bf16[8,32,256]{2,1,0:T(8,128)(2,1)S(1)}, f32[8,32,512]{2,1,0:T(8,128)S(1)}) custom-call(bf16[8,136,128]{2,1,0:T(8,128)(2,1)S(1)} %all-to-all-done.1.src_ref, bf16[272,256]{1,0:T(8,128)(2,1)S(1)} %collective-permute-done.3.refs_0_, f32[8,32,512]{2,1,0:T(8,128)S(1)} %get-tuple-element.43.refs_1_), custom_call_target="tpu_custom_call" | custom-call | flops 1000000 | bytes 1000000 | tf_op jit(solution)/shard_map/compute_next/pallas_call | solution.py:559
  44.8 1.3 %collective-permute-start.5 = (bf16[8,32,256]{2,1,0:T(8,128)(2,1)S(1)}, bf16[8,32,256]{2,1,0:T(8,128)(2,1)S(1)}, u32[]{:S(2)}, u32[]{:S(2)}) collective-permute-start(bf16[8,32,256]{2,1,0:T(8,128)(2,1)S(1)} %get-tuple-element.48), channel_id=1, source_target_pairs={{0,2},{1,3},{2,0},{3,1},{4,6},{5,7},{6,4},{7,5},{8,10},{9,11},{10,... | collective-permute-start | bytes 393224 | tf_op jit(solution)/shard_map/ppermute | solution.py:531
  46.1 0.0 collective-permute-done.2.refs_0_
  46.1 0.0 collective-permute-done.1.refs_1_
  46.1 5.3 %compute_last.1 = (bf16[8,32,256]{2,1,0:T(8,128)(2,1)S(1)}, bf16[32,32,128]{2,1,0:T(8,128)(2,1)}) custom-call(bf16[8,136,128]{2,1,0:T(8,128)(2,1)S(1)} %all-to-all-done.1.src_ref, bf16[272,256]{1,0:T(8,128)(2,1)S(1)} %collective-permute-done.2.refs_0_, f32[8,32,512]{2,1,0:T(8,128)S(1)} %get-tuple-element.46.refs_1_), custom_call_target="tpu_custom_call" | custom-call | flops 1000000 | bytes 1000000 | tf_op jit(solution)/shard_map/compute_last/pallas_call | solution.py:559
  51.4 1.2 %collective-permute-done.5.refs_2_ = bf16[8,32,256]{2,1,0:T(8,128)(2,1)S(1)} collective-permute-done((bf16[8,32,256]{2,1,0:T(8,128)(2,1)S(1)}, bf16[8,32,256]{2,1,0:T(8,128)(2,1)S(1)}, u32[]{:S(2)}, u32[]{:S(2)}) %collective-permute-start.5) | collective-permute-done | bytes 131104 | tf_op jit(solution)/shard_map/ppermute | solution.py:531
  52.5 2.6 %all-to-all-start.2 = ((bf16[32,32,128]{2,1,0:T(8,128)(2,1)}), bf16[32,32,128]{2,1,0:T(8,128)(2,1)S(1)}, u32[]{:S(2)}, u32[]{:S(2)}) async-start(bf16[32,32,128]{2,1,0:T(8,128)(2,1)} %get-tuple-element.50), calls=%async_computation.2 | async-start | bytes 524288 | tf_op jit(solution)/shard_map/all_to_all | solution.py:563
  55.2 1.8 %collective-permute-start.4 = (bf16[8,32,256]{2,1,0:T(8,128)(2,1)S(1)}, bf16[8,32,256]{2,1,0:T(8,128)(2,1)S(1)}, u32[]{:S(2)}, u32[]{:S(2)}) collective-permute-start(bf16[8,32,256]{2,1,0:T(8,128)(2,1)S(1)} %get-tuple-element.47), channel_id=1, source_target_pairs={{0,1},{1,0},{2,3},{3,2},{4,5},{5,4},{6,7},{7,6},{8,9},{9,8},{10,11... | collective-permute-start | bytes 393224 | tf_op jit(solution)/shard_map/ppermute | solution.py:531
  57.0 1.5 %unpack_first.1.held_ref = f32[32,32,256]{2,1,0:T(8,128)} custom-call(bf16[8,32,256]{2,1,0:T(8,128)(2,1)S(1)} %get-tuple-element.51.refs_0_, bf16[8,32,256]{2,1,0:T(8,128)(2,1)S(1)} %collective-permute-done.1.refs_1_, bf16[8,32,256]{2,1,0:T(8,128)(2,1)S(1)} %collective-permute-done.5.refs_2_), custom_call_target="tpu_custom_call" | custom-call | flops 1000000 | bytes 1000000 | tf_op jit(solution)/shard_map/unpack_first/pallas_call | solution.py:566
  58.5 6.6 %collective-permute-done.4.rcv_in = bf16[8,32,256]{2,1,0:T(8,128)(2,1)S(1)} collective-permute-done((bf16[8,32,256]{2,1,0:T(8,128)(2,1)S(1)}, bf16[8,32,256]{2,1,0:T(8,128)(2,1)S(1)}, u32[]{:S(2)}, u32[]{:S(2)}) %collective-permute-start.4) | collective-permute-done | bytes 131104 | tf_op jit(solution)/shard_map/ppermute | solution.py:531
  65.1 0.3 all-to-all-done.2.src_in
  65.4 2.0 %unpack_last.1 = (f32[32,32,256]{2,1,0:T(8,128)}, f32[32,16,256]{2,1,0:T(8,128)}) custom-call(bf16[8,32,256]{2,1,0:T(8,128)(2,1)S(1)} %collective-permute-done.4.rcv_in, bf16[32,32,128]{2,1,0:T(8,128)(2,1)S(1)} %all-to-all-done.2.src_in, f32[32,32,256]{2,1,0:T(8,128)} %unpack_first.1.held_ref), custom_call_target="tpu_custom_call", output_to_operand_aliasing={{0}: (2, {})} | custom-call | flops 1000000 | bytes 2000000 | tf_op jit(solution)/shard_map/unpack_last/pallas_call | solution.py:567
Async XLA Ops:
  0.6 9.5 %copy-start.1 = (bf16[2,16,32,256]{3,2,1,0:T(8,128)(2,1)S(1)}, bf16[2,16,32,256]{3,2,1,0:T(8,128)(2,1)}, u32[]{:S(2)}) copy-start(bf16[2,16,32,256]{3,2,1,0:T(8,128)(2,1)} %param.6) | copy-start | bytes 1572868
  3.7 6.5 %copy-start = (s32[16,8192]{1,0:T(8,128)S(1)}, s32[16,8192]{1,0:T(8,128)}, u32[]{:S(2)}) copy-start(s32[16,8192]{1,0:T(8,128)} %lag_ref.3) | copy-start | bytes 1572868
  3.7 15.8 %all-to-all-start = ((bf16[4,2,136,128]{3,2,1,0:T(8,128)(2,1)}), bf16[4,2,136,128]{3,2,1,0:T(8,128)(2,1)}, u32[]{:S(2)}, u32[]{:S(2)}) async-start(bf16[4,2,136,128]{3,2,1,0:T(8,128)(2,1)} %pack_sources.1), calls=%async_computation | async-start | bytes 557056 | tf_op jit(solution)/shard_map/all_to_all | solution.py:547
  10.1 0.7 %copy-start.2 = (s32[256]{0:T(256)S(1)}, s32[256]{0:T(256)}, u32[]{:S(2)}) copy-start(s32[256]{0:T(256)} %pos_ref.3) | copy-start | bytes 3076
  19.5 10.8 %all-to-all-start.1 = ((bf16[8,136,128]{2,1,0:T(8,128)(2,1)}), bf16[8,136,128]{2,1,0:T(8,128)(2,1)S(1)}, u32[]{:S(2)}, u32[]{:S(2)}) async-start(bf16[8,136,128]{2,1,0:T(8,128)(2,1)} %bitcast.2), calls=%async_computation.1 | async-start | bytes 557056 | tf_op jit(solution)/shard_map/all_to_all | solution.py:551
  23.2 11.3 %collective-permute-start = (bf16[272,256]{1,0:T(8,128)(2,1)S(1)}, bf16[272,256]{1,0:T(8,128)(2,1)S(1)}, u32[]{:S(2)}, u32[]{:S(2)}) collective-permute-start(bf16[272,256]{1,0:T(8,128)(2,1)S(1)} %get-tuple-element.34), channel_id=1, source_target_pairs={{0,3},{1,2},{2,1},{3,0},{4,7},{5,6},{6,5},{7,4},{8,11},{9,10},{10,... | collective-permute-start | bytes 417800 | tf_op jit(solution)/shard_map/ppermute | solution.py:531
  24.7 15.7 %collective-permute-start.3 = (bf16[272,256]{1,0:T(8,128)(2,1)S(1)}, bf16[272,256]{1,0:T(8,128)(2,1)S(1)}, u32[]{:S(2)}, u32[]{:S(2)}) collective-permute-start(bf16[272,256]{1,0:T(8,128)(2,1)S(1)} %get-tuple-element.40), channel_id=1, source_target_pairs={{0,2},{1,3},{2,0},{3,1},{4,6},{5,7},{6,4},{7,5},{8,10},{9,11},{10,... | collective-permute-start | bytes 417800 | tf_op jit(solution)/shard_map/ppermute | solution.py:531
  24.8 21.3 %collective-permute-start.2 = (bf16[272,256]{1,0:T(8,128)(2,1)S(1)}, bf16[272,256]{1,0:T(8,128)(2,1)S(1)}, u32[]{:S(2)}, u32[]{:S(2)}) collective-permute-start(bf16[272,256]{1,0:T(8,128)(2,1)S(1)} %get-tuple-element.38), channel_id=1, source_target_pairs={{0,1},{1,0},{2,3},{3,2},{4,5},{5,4},{6,7},{7,6},{8,9},{9,8},{10,11... | collective-permute-start | bytes 417800 | tf_op jit(solution)/shard_map/ppermute | solution.py:531
  38.8 7.2 %collective-permute-start.1 = (bf16[8,32,256]{2,1,0:T(8,128)(2,1)S(1)}, bf16[8,32,256]{2,1,0:T(8,128)(2,1)S(1)}, u32[]{:S(2)}, u32[]{:S(2)}) collective-permute-start(bf16[8,32,256]{2,1,0:T(8,128)(2,1)S(1)} %get-tuple-element.37), channel_id=1, source_target_pairs={{0,3},{1,2},{2,1},{3,0},{4,7},{5,6},{6,5},{7,4},{8,11},{9,10},{10,... | collective-permute-start | bytes 393224 | tf_op jit(solution)/shard_map/ppermute | solution.py:531
  44.8 7.7 %collective-permute-start.5 = (bf16[8,32,256]{2,1,0:T(8,128)(2,1)S(1)}, bf16[8,32,256]{2,1,0:T(8,128)(2,1)S(1)}, u32[]{:S(2)}, u32[]{:S(2)}) collective-permute-start(bf16[8,32,256]{2,1,0:T(8,128)(2,1)S(1)} %get-tuple-element.48), channel_id=1, source_target_pairs={{0,2},{1,3},{2,0},{3,1},{4,6},{5,7},{6,4},{7,5},{8,10},{9,11},{10,... | collective-permute-start | bytes 393224 | tf_op jit(solution)/shard_map/ppermute | solution.py:531
  52.5 12.9 %all-to-all-start.2 = ((bf16[32,32,128]{2,1,0:T(8,128)(2,1)}), bf16[32,32,128]{2,1,0:T(8,128)(2,1)S(1)}, u32[]{:S(2)}, u32[]{:S(2)}) async-start(bf16[32,32,128]{2,1,0:T(8,128)(2,1)} %get-tuple-element.50), calls=%async_computation.2 | async-start | bytes 524288 | tf_op jit(solution)/shard_map/all_to_all | solution.py:563
  55.2 9.9 %collective-permute-start.4 = (bf16[8,32,256]{2,1,0:T(8,128)(2,1)S(1)}, bf16[8,32,256]{2,1,0:T(8,128)(2,1)S(1)}, u32[]{:S(2)}, u32[]{:S(2)}) collective-permute-start(bf16[8,32,256]{2,1,0:T(8,128)(2,1)S(1)} %get-tuple-element.47), channel_id=1, source_target_pairs={{0,1},{1,0},{2,3},{3,2},{4,5},{5,4},{6,7},{7,6},{8,9},{9,8},{10,11... | collective-permute-start | bytes 393224 | tf_op jit(solution)/shard_map/ppermute | solution.py:531

commit v5 on v4

--- a/solution.py
+++ b/solution.py
@@ -190,15 +190,15 @@
         )
 
 
-def look_up(lag_ref, pos_ref, begin, count, offset):
-    lane = lanes_of(LAG_ROWS)
-    acc = jnp.zeros((LAG_ROWS, LANES), jnp.int32)
-    for n in range(count):
-        pos = pos_ref[begin + n]
-        base = pl.multiple_of((pos // LANES) * LANES, LANES)
-        tile = lag_ref[:, pl.ds(base, LANES)]
-        acc = jnp.where(lane == n, pltpu.roll(tile, (n - pos) & (LANES - 1), 1), acc)
-    return (acc - offset).astype(F32)
+def look_up(z, table, pos_ref):
+    pos = pos_ref[...]
+    lane = lax.broadcasted_iota(jnp.int32, (LANES, pos.shape[1]), 0)
+    spot = (lane == pos % LANES).astype(F32).astype(BF16)
+    found = jnp.dot(table, spot, preferred_element_type=F32)
+    total = 0.0
+    for block in range(z.n_pos // LANES):
+        total += jnp.where(pos // LANES == block, found[block * z.n_slow:(block + 1) * z.n_slow], 0.0)
+    return total
 
 
 def whole(*shape):
@@ -206,32 +206,27 @@
 
 
 def pack_sources(z):
-    def kernel(pos_ref, src_ref, lag_ref, out_ref, flat):
-        lags = look_up(lag_ref, pos_ref, 0, z.src_dev, z.n_freq)[:, :z.src_dev]
-        lags = jnp.concatenate([lags[:LAG_ROWS // 2], lags[LAG_ROWS // 2:]], 1).astype(BF16)
+    def kernel(src_ref, *refs):
+        outs, flat = refs[:z.n_rcv], refs[z.n_rcv]
         for row in range(ROWS):
             flat[row * z.src_freq:(row + 1) * z.src_freq, :z.src_dev] = src_ref[row].astype(F32)
         half = z.own // 2
-        for rcv in range(z.n_rcv):
+        for other in range(z.n_rcv):
+            rcv = lax.axis_index("rcv") ^ other
             for low in range(z.low):
                 for group in range(2):
                     freq = (low * z.n_rcv + rcv) * z.own + group * half
                     tiles = [flat[pl.ds(freq + m, ROWS, stride=z.src_freq), :] for m in range(half)]
                     turned = jnp.transpose(jnp.concatenate(tiles, 0))[:z.src_dev]
-                    out_ref[rcv, low, group * z.src_dev:(group + 1) * z.src_dev, :] = turned.astype(BF16)
-                out_ref[rcv, low, z.chunk:, :] = lags
-
-    shape = (z.n_rcv, z.low, z.chunk + LAG_ROWS // 2, LANES)
+                    outs[other][low, group * z.src_dev:(group + 1) * z.src_dev, :] = turned.astype(BF16)
+
+    shape = (z.low, z.chunk, LANES)
     return pl.pallas_call(
         kernel,
         grid=(1,),
-        in_specs=[
-            pl.BlockSpec(memory_space=pltpu.SMEM),
-            whole(ROWS, z.src_freq, z.src_dev),
-            whole(z.n_slow, z.n_pos),
-        ],
-        out_specs=whole(*shape),
-        out_shape=jax.ShapeDtypeStruct(shape, BF16),
+        in_specs=[whole(ROWS, z.src_freq, z.src_dev)],
+        out_specs=[whole(*shape)] * z.n_rcv,
+        out_shape=[jax.ShapeDtypeStruct(shape, BF16)] * z.n_rcv,
         scratch_shapes=[pltpu.VMEM((ROWS * z.src_freq, LANES), F32)],
         compiler_params=pltpu.CompilerParams(vmem_limit_bytes=FULL_VMEM),
         cost_estimate=pl.CostEstimate(flops=10**6, bytes_accessed=2 * 10**6, transcendentals=0),
@@ -239,11 +234,37 @@
     )
 
 
+def order_sources(z):
+    def kernel(lag_ref, *refs):
+        out_ref = refs[-1]
+        for other in range(z.n_rcv):
+            place = lax.axis_index("rcv") ^ other
+            out_ref[pl.ds(place * z.low, z.low), :z.chunk, :] = refs[other][...]
+        for place in range(z.n_src):
+            out_ref[place, z.chunk:, :] = lag_ref[...]
+
+    shape = (z.chunk + LAG_ROWS // 2, LANES)
+    return pl.pallas_call(
+        kernel,
+        grid=(1,),
+        in_specs=[whole(LAG_ROWS // 2, LANES)] + [whole(z.low, z.chunk, LANES)] * z.n_rcv,
+        out_specs=whole(z.n_src, *shape),
+        out_shape=jax.ShapeDtypeStruct((z.n_src, *shape), BF16),
+        compiler_params=pltpu.CompilerParams(vmem_limit_bytes=VMEM),
+        cost_estimate=pl.CostEstimate(flops=10**6, bytes_accessed=10**6, transcendentals=0),
+        name="order_sources",
+    )
+
+
 def pack_receivers(z):
-    def kernel(pos_ref, rcv_ref, lag_ref, *refs):
-        outs, flat = refs[:z.n_rcv], refs[z.n_rcv:]
+    def kernel(pos_ref, src_pos_ref, rcv_ref, lag_ref, *refs):
+        outs, src_out, flat = refs[:z.n_rcv], refs[z.n_rcv], refs[z.n_rcv + 1:]
+        blocks = [lag_ref[:, place:place + LANES] for place in range(0, z.n_pos, LANES)]
+        table = (jnp.concatenate(blocks, 0) - z.n_freq).astype(F32).astype(BF16)
+        src_lags = look_up(z, table, src_pos_ref)
+        src_out[...] = jnp.concatenate([src_lags[:LAG_ROWS // 2], src_lags[LAG_ROWS // 2:]], 1).astype(BF16)
         spans = range(0, z.rcv_dev, LANES)
-        lags = [look_up(lag_ref, pos_ref, span, LANES, z.n_freq).astype(BF16) for span in spans]
+        lags = look_up(z, table, pos_ref).astype(BF16)
         for row in range(ROWS):
             here = rcv_ref[row].astype(F32)
             for n, span in enumerate(spans):
@@ -254,19 +275,21 @@
                 for k in range(z.own):
                     tile = flat[n][pl.ds(first + k, ROWS, stride=z.rcv_freq), :]
                     outs[other][k * ROWS:(k + 1) * ROWS, span:span + LANES] = tile.astype(BF16)
-                outs[other][z.own * ROWS:, span:span + LANES] = lags[n]
+                outs[other][z.own * ROWS:, span:span + LANES] = lags[:, span:span + LANES]
 
     shape = (z.own * ROWS + LAG_ROWS, z.rcv_dev)
     return pl.pallas_call(
         kernel,
         grid=(1,),
         in_specs=[
-            pl.BlockSpec(memory_space=pltpu.SMEM),
+            whole(1, z.rcv_dev),
+            whole(1, z.src_dev),
             whole(ROWS, z.rcv_freq, z.rcv_dev),
             whole(z.n_slow, z.n_pos),
         ],
-        out_specs=[whole(*shape)] * z.n_rcv,
-        out_shape=[jax.ShapeDtypeStruct(shape, BF16)] * z.n_rcv,
+        out_specs=[whole(*shape)] * z.n_rcv + [whole(LAG_ROWS // 2, LANES)],
+        out_shape=[jax.ShapeDtypeStruct(shape, BF16)] * z.n_rcv
+        + [jax.ShapeDtypeStruct((LAG_ROWS // 2, LANES), BF16)],
         scratch_shapes=[pltpu.VMEM((ROWS * z.rcv_freq, LANES), F32)] * (z.rcv_dev // LANES),
         compiler_params=pltpu.CompilerParams(vmem_limit_bytes=VMEM),
         cost_estimate=pl.CostEstimate(flops=10**6, bytes_accessed=2 * 10**6, transcendentals=0),
@@ -366,6 +389,7 @@
             panel_re = over_re * src_cos + over_im * src_sin
             panel_im = over_im * src_cos - over_re * src_sin
             refs[5][turn] = jnp.concatenate([panel_re, panel_im], 0)
+            regroup_after(z, refs[5], turn)
 
         cross(0, 0)
         for turn in range(1, z.own):
@@ -408,22 +432,30 @@
     )
 
 
+def regroup(z, sums, bit, first):
+    lane = lanes_of(ROWS)
+    shift = bit * z.src_part
+    upper = lane & shift != 0
+    for block in range(z.s_all // LANES):
+        lanes = slice(block * LANES, (block + 1) * LANES)
+        one, two = sums[first, :, lanes], sums[first + bit, :, lanes]
+        sums[first, :, lanes] = jnp.where(upper, pltpu.roll(two, shift, 1), one)
+        sums[first + bit, :, lanes] = jnp.where(upper, two, pltpu.roll(one, LANES - shift, 1))
+
+
+def regroup_after(z, sums, turn):
+    bit = 1
+    while bit < z.own and turn & bit:
+        base = turn & ~(2 * bit - 1)
+        for low in range(bit):
+            regroup(z, sums, bit, base + low)
+        bit *= 2
+
+
 def send_sources(z, sums, out_ref):
-    lane = lanes_of(ROWS)
     for block in range(z.s_all // LANES):
-        tiles = [sums[k, :, block * LANES:(block + 1) * LANES] for k in range(z.own)]
-        bit = 1
-        while bit < z.own:
-            shift = bit * z.src_part
-            upper = lane & shift != 0
-            for k in range(z.own):
-                if not k & bit:
-                    one, two = tiles[k], tiles[k | bit]
-                    tiles[k] = jnp.where(upper, pltpu.roll(two, shift, 1), one)
-                    tiles[k | bit] = jnp.where(upper, two, pltpu.roll(one, LANES - shift, 1))
-            bit *= 2
         for group in range(z.own):
-            out_ref[block * z.own + group] = tiles[group].astype(BF16)
+            out_ref[block * z.own + group] = sums[group, :, block * LANES:(block + 1) * LANES].astype(BF16)
 
 
 def unpack_block(z, in_ref, flat, write):
@@ -492,10 +524,10 @@
         here = lax.broadcasted_iota(jnp.int32, (z.n_freq, z.n_freq), 0)
         there = lax.broadcasted_iota(jnp.int32, (z.n_freq, z.n_freq), 1)
         order = (there == here % z.n_dev * z.own + here // z.n_dev).astype(F32).astype(BF16)
+        ordered = jnp.dot(table[...], order, preferred_element_type=F32)
         for index in range(ROWS):
             part, slow = divmod(index, n)
-            rows = table[index * width:(index + 1) * width, :]
-            src_ref[2 * slow + part] = jnp.dot(rows, order, preferred_element_type=F32)
+            src_ref[2 * slow + part] = ordered[index * width:(index + 1) * width, :]
 
     return pl.pallas_call(
         kernel,
@@ -544,10 +576,11 @@
         return per_device_general(src_spec, rcv_spec, lag_table, src_pos, rcv_pos)
     src_rows = src_spec.reshape(ROWS, z.src_freq, z.src_dev)
     rcv_rows = rcv_spec.reshape(ROWS, z.rcv_freq, z.rcv_dev)
-    spread = lax.all_to_all(pack_sources(z)(src_pos, src_rows, lag_table), "rcv", 0, 0, tiled=True)
-    packed = pack_receivers(z)(rcv_pos, rcv_rows, lag_table)
-    spread, packed = lax.optimization_barrier((spread, packed))
-    spread = spread.reshape(z.n_src, z.chunk + LAG_ROWS // 2, LANES)
+    parts = pack_sources(z)(src_rows)
+    moved = {other: swap(z, parts[other], other) for other in (3, 2, 1, 0)}
+    *packed, src_lags = pack_receivers(z)(rcv_pos[None], src_pos[None], rcv_rows, lag_table)
+    moved, packed, src_lags = lax.optimization_barrier((moved, packed, src_lags))
+    spread = order_sources(z)(src_lags, *(moved[other] for other in range(z.n_rcv)))
     sources = lax.all_to_all(spread, "src", 0, 0, tiled=True)
     blocks = {other: swap(z, packed[other], other) for others in CALLS for other in others}
     done, carry = {}, ()

time: 67.8 us -> 65.2 us (0.962)
  Pallas kernels: 27.5 us -> 25.2 us
  waiting for transfers between devices: 16.7 us -> 15 us
  local copies, waits for them, and re-layouts: 0.68 us -> 1.72 us
    all_to_all x1 -> x0, starting transfers between devices: 6.45 us -> none  [per_device(): lax.all_to_all(pack_sources(z)(src_pos, src_rows, lag_table), 'rcv', 0, 0...]
    all_to_all x1 -> x0, waiting for transfers between devices: 5.9 us -> none  [per_device(): lax.all_to_all(pack_sources(z)(src_pos, src_rows, lag_table), 'rcv', 0, 0...]
    ppermute x6 -> x9, starting transfers between devices: 9.02 us -> 14.9 us  [swap(): return lax.ppermute(block, 'rcv', [(j, j ^ other) for j in range(z.n_rcv)])]
    ppermute x6 -> x9, waiting for transfers between devices: 7.75 us -> 11.9 us  [swap(): return lax.ppermute(block, 'rcv', [(j, j ^ other) for j in range(z.n_rcv)])]
    pallas_call x2 -> x3, Pallas kernels: 5.81 us -> 4.27 us  [the longest x1 2.46 us: per_device(): parts = pack_sources(z)(src_rows)]
    unnamed x6 -> x10, local copies, waits for them, and re-layouts: 0.68 us -> 1.72 us
    all_to_all x1, starting transfers between devices: 2.65 us -> 3.69 us  [per_device(): got_src = lax.all_to_all(total, ('src', 'rcv'), 0, 0, tiled=True)]
  transfers between devices with their start and end apart: 9 -> 11, of which waited for: 5 -> 6; matrix products, arithmetic and copies ran while one was open for 0% -> 0% of each run, Pallas kernels for 33% -> 31%
where the time goes in v5:
time: 65.2 us; the launch traced here: 64.8 us
  Pallas kernels  25.2 us (39%)
  starting transfers between devices  22.3 us (34%)
  waiting for transfers between devices  15 us (23%)
  local copies, waits for them, and re-layouts  1.72 us (3%)
  between operations  0.69 us (1%)
    pallas_call x4, Pallas kernels, per_device(): *panels, total = call(sources, *ready, *carry)  17.8 us
    ppermute x9, starting transfers between devices, swap(): return lax.ppermute(block, 'rcv', [(j, j ^ other) for j in range(z.n_rcv)])  14.9 us
    ppermute x9, waiting for transfers between devices, swap(): return lax.ppermute(block, 'rcv', [(j, j ^ other) for j in range(z.n_rcv)])  11.9 us
    all_to_all x1, starting transfers between devices, per_device(): sources = lax.all_to_all(spread, 'src', 0, 0, tiled=True)  3.72 us
    all_to_all x1, starting transfers between devices, per_device(): got_src = lax.all_to_all(total, ('src', 'rcv'), 0, 0, tiled=True)  3.69 us
    all_to_all x1, waiting for transfers between devices, per_device(): sources = lax.all_to_all(spread, 'src', 0, 0, tiled=True)  2.69 us
    pallas_call x1, Pallas kernels, per_device(): parts = pack_sources(z)(src_rows)  2.46 us
    unnamed x10, local copies, waits for them, and re-layouts  1.72 us
  transfers between devices with their start and end apart: 11, of which 6 were waited for; matrix products, arithmetic and copies ran while one was open for 0% of the time, Pallas kernels for 31%

profile of v5, /device:TPU:0, one launch (start us, length us, event | category | flops | bytes accessed | tf_op | source)
XLA Modules:
  0.0 64.8 jit_solution(2128511915013732667)
XLA Ops:
  0.6 2.5 %pack_sources.1 = (bf16[2,128,128]{2,1,0:T(8,128)(2,1)}, bf16[2,128,128]{2,1,0:T(8,128)(2,1)}, bf16[2,128,128]{2,1,0:T(8,128)(2,1)}, bf16[2,128,128]{2,1,0:T(8,128)(2,1)}) custom-call(bf16[32,64,64]{2,1,0:T(8,128)(2,1)} %bitcast.10), custom_call_target="tpu_custom_call" | custom-call | flops 1000000 | bytes 2000000 | tf_op jit(solution)/shard_map/pack_sources/pallas_call | solution.py:579
  3.1 3.0 %collective-permute-start = (bf16[2,128,128]{2,1,0:T(8,128)(2,1)}, bf16[2,128,128]{2,1,0:T(8,128)(2,1)S(1)}, u32[]{:S(2)}, u32[]{:S(2)}) collective-permute-start(bf16[2,128,128]{2,1,0:T(8,128)(2,1)} %get-tuple-element.39), channel_id=1, source_target_pairs={{0,1},{1,0},{2,3},{3,2},{4,5},{5,4},{6,7},{7,6},{8,9},{9,8},{10,11... | collective-permute-start | bytes 196616 | tf_op jit(solution)/shard_map/ppermute | solution.py:563
  6.1 2.6 %collective-permute-start.1 = (bf16[2,128,128]{2,1,0:T(8,128)(2,1)}, bf16[2,128,128]{2,1,0:T(8,128)(2,1)S(1)}, u32[]{:S(2)}, u32[]{:S(2)}) collective-permute-start(bf16[2,128,128]{2,1,0:T(8,128)(2,1)} %get-tuple-element.40), channel_id=1, source_target_pairs={{0,2},{1,3},{2,0},{3,1},{4,6},{5,7},{6,4},{7,5},{8,10},{9,11},{10,... | collective-permute-start | bytes 196616 | tf_op jit(solution)/shard_map/ppermute | solution.py:563
  8.7 0.0 collective-permute-start.2
  8.7 0.7 %copy-done.3 = s32[256]{0:T(256)S(1)} copy-done((s32[256]{0:T(256)S(1)}, s32[256]{0:T(256)}, u32[]{:S(2)}) %copy-start.3) | copy-done | bytes 1048
  9.4 1.0 %copy-done.1 = s32[16,8192]{1,0:T(8,128)S(1)} copy-done((s32[16,8192]{1,0:T(8,128)S(1)}, s32[16,8192]{1,0:T(8,128)}, u32[]{:S(2)}) %copy-start.1) | copy-done | bytes 524312
  10.4 1.1 %pack_receivers.1 = (bf16[272,256]{1,0:T(8,128)(2,1)S(1)}, bf16[272,256]{1,0:T(8,128)(2,1)S(1)}, bf16[272,256]{1,0:T(8,128)(2,1)S(1)}, bf16[272,256]{1,0:T(8,128)(2,1)S(1)}, bf16[8,128]{1,0:T(8,128)(2,1)S(1)}) custom-call(s32[1,256]{1,0:T(1,128)S(1)} %bitcast.7, s32[1,64]{1,0:T(1,128)S(1)} %bitcast.8, bf16[32,32,256]{2,1,0:T(8,128)(2,1)S(1)} %bitcast.6, ...), custom_call_target="tpu_custom_call" | custom-call | flops 1000000 | bytes 2000000 | tf_op jit(solution)/shard_map/pack_receivers/pallas_call | solution.py:581
  11.5 0.0 collective-permute-done.refs_1_
  11.5 2.1 %collective-permute-done.1.refs_2_ = bf16[2,128,128]{2,1,0:T(8,128)(2,1)S(1)} collective-permute-done((bf16[2,128,128]{2,1,0:T(8,128)(2,1)}, bf16[2,128,128]{2,1,0:T(8,128)(2,1)S(1)}, u32[]{:S(2)}, u32[]{:S(2)}) %collective-permute-start.1) | collective-permute-done | bytes 65568 | tf_op jit(solution)/shard_map/ppermute | solution.py:563
  13.6 1.4 %collective-permute-done.2.refs_3_ = bf16[2,128,128]{2,1,0:T(8,128)(2,1)S(1)} collective-permute-done((bf16[2,128,128]{2,1,0:T(8,128)(2,1)}, bf16[2,128,128]{2,1,0:T(8,128)(2,1)S(1)}, u32[]{:S(2)}, u32[]{:S(2)}) %collective-permute-start.2) | collective-permute-done | bytes 65568 | tf_op jit(solution)/shard_map/ppermute | solution.py:563
  15.0 0.7 %order_sources.1 = bf16[8,136,128]{2,1,0:T(8,128)(2,1)} custom-call(bf16[8,128]{1,0:T(8,128)(2,1)S(1)} %get-tuple-element.47.lag_ref, bf16[2,128,128]{2,1,0:T(8,128)(2,1)S(1)} %copy-done.2, bf16[2,128,128]{2,1,0:T(8,128)(2,1)S(1)} %collective-permute-done.refs_1_, bf16[2,128,128]{2,1,0:T(8,128)(2,1)S(1)} %collective-permute-done.1.refs_2_, ...), custom_call_target="tpu_custom_call" | custom-call | flops 1000000 | bytes 1000000 | tf_op jit(solution)/shard_map/order_sources/pallas_call | solution.py:583
  15.7 3.7 %all-to-all-start = ((bf16[8,136,128]{2,1,0:T(8,128)(2,1)}), bf16[8,136,128]{2,1,0:T(8,128)(2,1)S(1)}, u32[]{:S(2)}, u32[]{:S(2)}) async-start(bf16[8,136,128]{2,1,0:T(8,128)(2,1)} %order_sources.1), calls=%async_computation | async-start | bytes 557056 | tf_op jit(solution)/shard_map/all_to_all | solution.py:584
  19.5 1.8 %collective-permute-start.3 = (bf16[272,256]{1,0:T(8,128)(2,1)S(1)}, bf16[272,256]{1,0:T(8,128)(2,1)S(1)}, u32[]{:S(2)}, u32[]{:S(2)}) collective-permute-start(bf16[272,256]{1,0:T(8,128)(2,1)S(1)} %get-tuple-element.52), channel_id=1, source_target_pairs={{0,3},{1,2},{2,1},{3,0},{4,7},{5,6},{6,5},{7,4},{8,11},{9,10},{10,... | collective-permute-start | bytes 417800 | tf_op jit(solution)/shard_map/ppermute | solution.py:563
  21.3 0.0 collective-permute-start.6
  21.3 2.6 %collective-permute-start.5 = (bf16[272,256]{1,0:T(8,128)(2,1)S(1)}, bf16[272,256]{1,0:T(8,128)(2,1)S(1)}, u32[]{:S(2)}, u32[]{:S(2)}) collective-permute-start(bf16[272,256]{1,0:T(8,128)(2,1)S(1)} %get-tuple-element.56), channel_id=1, source_target_pairs={{0,1},{1,0},{2,3},{3,2},{4,5},{5,4},{6,7},{7,6},{8,9},{9,8},{10,11... | collective-permute-start | bytes 417800 | tf_op jit(solution)/shard_map/ppermute | solution.py:563
  23.9 2.7 %all-to-all-done.src_ref = bf16[8,136,128]{2,1,0:T(8,128)(2,1)S(1)} async-done(((bf16[8,136,128]{2,1,0:T(8,128)(2,1)}), bf16[8,136,128]{2,1,0:T(8,128)(2,1)S(1)}, u32[]{:S(2)}, u32[]{:S(2)}) %all-to-all-start) | async-done | bytes 278560 | tf_op jit(solution)/shard_map/all_to_all | solution.py:584
  26.6 4.1 %compute_first.1 = (bf16[8,32,256]{2,1,0:T(8,128)(2,1)S(1)}, f32[8,32,512]{2,1,0:T(8,128)S(1)}) custom-call(bf16[8,136,128]{2,1,0:T(8,128)(2,1)S(1)} %all-to-all-done.src_ref, bf16[272,256]{1,0:T(8,128)(2,1)S(1)} %get-tuple-element.53.refs_0_), custom_call_target="tpu_custom_call" | custom-call | flops 1000000 | bytes 1000000 | tf_op jit(solution)/shard_map/compute_first/pallas_call | solution.py:592
  30.7 4.1 %compute_next.2 = (bf16[8,32,256]{2,1,0:T(8,128)(2,1)S(1)}, f32[8,32,512]{2,1,0:T(8,128)S(1)}) custom-call(bf16[8,136,128]{2,1,0:T(8,128)(2,1)S(1)} %all-to-all-done.src_ref, bf16[272,256]{1,0:T(8,128)(2,1)S(1)} %collective-permute-done.3.refs_0_, f32[8,32,512]{2,1,0:T(8,128)S(1)} %get-tuple-element.54.refs_1_), custom_call_target="tpu_custom_call" | custom-call | flops 1000000 | bytes 1000000 | tf_op jit(solution)/shard_map/compute_next/pallas_call | solution.py:592
  34.8 1.8 %collective-permute-start.4 = (bf16[8,32,256]{2,1,0:T(8,128)(2,1)S(1)}, bf16[8,32,256]{2,1,0:T(8,128)(2,1)S(1)}, u32[]{:S(2)}, u32[]{:S(2)}) collective-permute-start(bf16[8,32,256]{2,1,0:T(8,128)(2,1)S(1)} %get-tuple-element.55), channel_id=1, source_target_pairs={{0,3},{1,2},{2,1},{3,0},{4,7},{5,6},{6,5},{7,4},{8,11},{9,10},{10,... | collective-permute-start | bytes 393224 | tf_op jit(solution)/shard_map/ppermute | solution.py:563
  36.7 0.0 collective-permute-done.6.refs_0_
  36.7 4.3 %compute_next.3 = (bf16[8,32,256]{2,1,0:T(8,128)(2,1)S(1)}, f32[8,32,512]{2,1,0:T(8,128)S(1)}) custom-call(bf16[8,136,128]{2,1,0:T(8,128)(2,1)S(1)} %all-to-all-done.src_ref, bf16[272,256]{1,0:T(8,128)(2,1)S(1)} %collective-permute-done.6.refs_0_, f32[8,32,512]{2,1,0:T(8,128)S(1)} %get-tuple-element.61.refs_1_), custom_call_target="tpu_custom_call" | custom-call | flops 1000000 | bytes 1000000 | tf_op jit(solution)/shard_map/compute_next/pallas_call | solution.py:592
  41.0 1.1 %collective-permute-start.8 = (bf16[8,32,256]{2,1,0:T(8,128)(2,1)S(1)}, bf16[8,32,256]{2,1,0:T(8,128)(2,1)S(1)}, u32[]{:S(2)}, u32[]{:S(2)}) collective-permute-start(bf16[8,32,256]{2,1,0:T(8,128)(2,1)S(1)} %get-tuple-element.66), channel_id=1, source_target_pairs={{0,2},{1,3},{2,0},{3,1},{4,6},{5,7},{6,4},{7,5},{8,10},{9,11},{10,... | collective-permute-start | bytes 393224 | tf_op jit(solution)/shard_map/ppermute | solution.py:563
  42.2 0.0 collective-permute-done.5.refs_0_
  42.2 0.0 collective-permute-done.4.refs_1_
  42.2 5.2 %compute_last.1 = (bf16[8,32,256]{2,1,0:T(8,128)(2,1)S(1)}, bf16[32,32,128]{2,1,0:T(8,128)(2,1)}) custom-call(bf16[8,136,128]{2,1,0:T(8,128)(2,1)S(1)} %all-to-all-done.src_ref, bf16[272,256]{1,0:T(8,128)(2,1)S(1)} %collective-permute-done.5.refs_0_, f32[8,32,512]{2,1,0:T(8,128)S(1)} %get-tuple-element.64.refs_1_), custom_call_target="tpu_custom_call" | custom-call | flops 1000000 | bytes 1000000 | tf_op jit(solution)/shard_map/compute_last/pallas_call | solution.py:592
  47.4 1.9 %collective-permute-done.8.refs_2_ = bf16[8,32,256]{2,1,0:T(8,128)(2,1)S(1)} collective-permute-done((bf16[8,32,256]{2,1,0:T(8,128)(2,1)S(1)}, bf16[8,32,256]{2,1,0:T(8,128)(2,1)S(1)}, u32[]{:S(2)}, u32[]{:S(2)}) %collective-permute-start.8) | collective-permute-done | bytes 131104 | tf_op jit(solution)/shard_map/ppermute | solution.py:563
  49.3 3.7 %all-to-all-start.1 = ((bf16[32,32,128]{2,1,0:T(8,128)(2,1)}), bf16[32,32,128]{2,1,0:T(8,128)(2,1)S(1)}, u32[]{:S(2)}, u32[]{:S(2)}) async-start(bf16[32,32,128]{2,1,0:T(8,128)(2,1)} %get-tuple-element.68), calls=%async_computation.1 | async-start | bytes 524288 | tf_op jit(solution)/shard_map/all_to_all | solution.py:596
  53.0 1.8 %collective-permute-start.7 = (bf16[8,32,256]{2,1,0:T(8,128)(2,1)S(1)}, bf16[8,32,256]{2,1,0:T(8,128)(2,1)S(1)}, u32[]{:S(2)}, u32[]{:S(2)}) collective-permute-start(bf16[8,32,256]{2,1,0:T(8,128)(2,1)S(1)} %get-tuple-element.65), channel_id=1, source_target_pairs={{0,1},{1,0},{2,3},{3,2},{4,5},{5,4},{6,7},{7,6},{8,9},{9,8},{10,11... | collective-permute-start | bytes 393224 | tf_op jit(solution)/shard_map/ppermute | solution.py:563
  54.8 1.5 %unpack_first.1.held_ref = f32[32,32,256]{2,1,0:T(8,128)} custom-call(bf16[8,32,256]{2,1,0:T(8,128)(2,1)S(1)} %get-tuple-element.69.refs_0_, bf16[8,32,256]{2,1,0:T(8,128)(2,1)S(1)} %collective-permute-done.4.refs_1_, bf16[8,32,256]{2,1,0:T(8,128)(2,1)S(1)} %collective-permute-done.8.refs_2_), custom_call_target="tpu_custom_call" | custom-call | flops 1000000 | bytes 1000000 | tf_op jit(solution)/shard_map/unpack_first/pallas_call | solution.py:599
  56.3 6.6 %collective-permute-done.7.rcv_in = bf16[8,32,256]{2,1,0:T(8,128)(2,1)S(1)} collective-permute-done((bf16[8,32,256]{2,1,0:T(8,128)(2,1)S(1)}, bf16[8,32,256]{2,1,0:T(8,128)(2,1)S(1)}, u32[]{:S(2)}, u32[]{:S(2)}) %collective-permute-start.7) | collective-permute-done | bytes 131104 | tf_op jit(solution)/shard_map/ppermute | solution.py:563
  62.8 0.3 all-to-all-done.1.src_in
  63.2 1.7 %unpack_last.1 = (f32[32,32,256]{2,1,0:T(8,128)}, f32[32,16,256]{2,1,0:T(8,128)}) custom-call(bf16[8,32,256]{2,1,0:T(8,128)(2,1)S(1)} %collective-permute-done.7.rcv_in, bf16[32,32,128]{2,1,0:T(8,128)(2,1)S(1)} %all-to-all-done.1.src_in, f32[32,32,256]{2,1,0:T(8,128)} %unpack_first.1.held_ref), custom_call_target="tpu_custom_call", output_to_operand_aliasing={{0}: (2, {})} | custom-call | flops 1000000 | bytes 2000000 | tf_op jit(solution)/shard_map/unpack_last/pallas_call | solution.py:600
  (9 shorter events, 0.0 us)
Async XLA Ops:
  0.6 8.1 %copy-start = (bf16[2,16,32,256]{3,2,1,0:T(8,128)(2,1)S(1)}, bf16[2,16,32,256]{3,2,1,0:T(8,128)(2,1)}, u32[]{:S(2)}) copy-start(bf16[2,16,32,256]{3,2,1,0:T(8,128)(2,1)} %param.6) | copy-start | bytes 1572868
  3.1 8.4 %collective-permute-start = (bf16[2,128,128]{2,1,0:T(8,128)(2,1)}, bf16[2,128,128]{2,1,0:T(8,128)(2,1)S(1)}, u32[]{:S(2)}, u32[]{:S(2)}) collective-permute-start(bf16[2,128,128]{2,1,0:T(8,128)(2,1)} %get-tuple-element.39), channel_id=1, source_target_pairs={{0,1},{1,0},{2,3},{3,2},{4,5},{5,4},{6,7},{7,6},{8,9},{9,8},{10,11... | collective-permute-start | bytes 196616 | tf_op jit(solution)/shard_map/ppermute | solution.py:563
  6.1 7.5 %collective-permute-start.1 = (bf16[2,128,128]{2,1,0:T(8,128)(2,1)}, bf16[2,128,128]{2,1,0:T(8,128)(2,1)S(1)}, u32[]{:S(2)}, u32[]{:S(2)}) collective-permute-start(bf16[2,128,128]{2,1,0:T(8,128)(2,1)} %get-tuple-element.40), channel_id=1, source_target_pairs={{0,2},{1,3},{2,0},{3,1},{4,6},{5,7},{6,4},{7,5},{8,10},{9,11},{10,... | collective-permute-start | bytes 196616 | tf_op jit(solution)/shard_map/ppermute | solution.py:563
  8.7 6.3 %collective-permute-start.2 = (bf16[2,128,128]{2,1,0:T(8,128)(2,1)}, bf16[2,128,128]{2,1,0:T(8,128)(2,1)S(1)}, u32[]{:S(2)}, u32[]{:S(2)}) collective-permute-start(bf16[2,128,128]{2,1,0:T(8,128)(2,1)} %get-tuple-element.41), channel_id=1, source_target_pairs={{0,3},{1,2},{2,1},{3,0},{4,7},{5,6},{6,5},{7,4},{8,11},{9,10},{10,... | collective-permute-start | bytes 196616 | tf_op jit(solution)/shard_map/ppermute | solution.py:563
  8.7 0.7 %copy-start.3 = (s32[256]{0:T(256)S(1)}, s32[256]{0:T(256)}, u32[]{:S(2)}) copy-start(s32[256]{0:T(256)} %param.9) | copy-start | bytes 3076
  8.7 0.7 %copy-start.4 = (s32[64]{0:T(128)S(1)}, s32[64]{0:T(128)}, u32[]{:S(2)}) copy-start(s32[64]{0:T(128)} %param.8) | copy-start | bytes 772
  9.4 1.0 %copy-start.1 = (s32[16,8192]{1,0:T(8,128)S(1)}, s32[16,8192]{1,0:T(8,128)}, u32[]{:S(2)}) copy-start(s32[16,8192]{1,0:T(8,128)} %lag_ref.1) | copy-start | bytes 1572868
  10.4 4.6 %copy-start.2 = (bf16[2,128,128]{2,1,0:T(8,128)(2,1)S(1)}, bf16[2,128,128]{2,1,0:T(8,128)(2,1)}, u32[]{:S(2)}) copy-start(bf16[2,128,128]{2,1,0:T(8,128)(2,1)} %get-tuple-element.48.refs_0_) | copy-start | bytes 196612
  15.7 10.8 %all-to-all-start = ((bf16[8,136,128]{2,1,0:T(8,128)(2,1)}), bf16[8,136,128]{2,1,0:T(8,128)(2,1)S(1)}, u32[]{:S(2)}, u32[]{:S(2)}) async-start(bf16[8,136,128]{2,1,0:T(8,128)(2,1)} %order_sources.1), calls=%async_computation | async-start | bytes 557056 | tf_op jit(solution)/shard_map/all_to_all | solution.py:584
  19.5 11.2 %collective-permute-start.3 = (bf16[272,256]{1,0:T(8,128)(2,1)S(1)}, bf16[272,256]{1,0:T(8,128)(2,1)S(1)}, u32[]{:S(2)}, u32[]{:S(2)}) collective-permute-start(bf16[272,256]{1,0:T(8,128)(2,1)S(1)} %get-tuple-element.52), channel_id=1, source_target_pairs={{0,3},{1,2},{2,1},{3,0},{4,7},{5,6},{6,5},{7,4},{8,11},{9,10},{10,... | collective-permute-start | bytes 417800 | tf_op jit(solution)/shard_map/ppermute | solution.py:563
  21.3 15.4 %collective-permute-start.6 = (bf16[272,256]{1,0:T(8,128)(2,1)S(1)}, bf16[272,256]{1,0:T(8,128)(2,1)S(1)}, u32[]{:S(2)}, u32[]{:S(2)}) collective-permute-start(bf16[272,256]{1,0:T(8,128)(2,1)S(1)} %get-tuple-element.58), channel_id=1, source_target_pairs={{0,2},{1,3},{2,0},{3,1},{4,6},{5,7},{6,4},{7,5},{8,10},{9,11},{10,... | collective-permute-start | bytes 417800 | tf_op jit(solution)/shard_map/ppermute | solution.py:563
  21.3 20.9 %collective-permute-start.5 = (bf16[272,256]{1,0:T(8,128)(2,1)S(1)}, bf16[272,256]{1,0:T(8,128)(2,1)S(1)}, u32[]{:S(2)}, u32[]{:S(2)}) collective-permute-start(bf16[272,256]{1,0:T(8,128)(2,1)S(1)} %get-tuple-element.56), channel_id=1, source_target_pairs={{0,1},{1,0},{2,3},{3,2},{4,5},{5,4},{6,7},{7,6},{8,9},{9,8},{10,11... | collective-permute-start | bytes 417800 | tf_op jit(solution)/shard_map/ppermute | solution.py:563
  34.8 7.4 %collective-permute-start.4 = (bf16[8,32,256]{2,1,0:T(8,128)(2,1)S(1)}, bf16[8,32,256]{2,1,0:T(8,128)(2,1)S(1)}, u32[]{:S(2)}, u32[]{:S(2)}) collective-permute-start(bf16[8,32,256]{2,1,0:T(8,128)(2,1)S(1)} %get-tuple-element.55), channel_id=1, source_target_pairs={{0,3},{1,2},{2,1},{3,0},{4,7},{5,6},{6,5},{7,4},{8,11},{9,10},{10,... | collective-permute-start | bytes 393224 | tf_op jit(solution)/shard_map/ppermute | solution.py:563
  41.0 8.2 %collective-permute-start.8 = (bf16[8,32,256]{2,1,0:T(8,128)(2,1)S(1)}, bf16[8,32,256]{2,1,0:T(8,128)(2,1)S(1)}, u32[]{:S(2)}, u32[]{:S(2)}) collective-permute-start(bf16[8,32,256]{2,1,0:T(8,128)(2,1)S(1)} %get-tuple-element.66), channel_id=1, source_target_pairs={{0,2},{1,3},{2,0},{3,1},{4,6},{5,7},{6,4},{7,5},{8,10},{9,11},{10,... | collective-permute-start | bytes 393224 | tf_op jit(solution)/shard_map/ppermute | solution.py:563
  49.3 13.9 %all-to-all-start.1 = ((bf16[32,32,128]{2,1,0:T(8,128)(2,1)}), bf16[32,32,128]{2,1,0:T(8,128)(2,1)S(1)}, u32[]{:S(2)}, u32[]{:S(2)}) async-start(bf16[32,32,128]{2,1,0:T(8,128)(2,1)} %get-tuple-element.68), calls=%async_computation.1 | async-start | bytes 524288 | tf_op jit(solution)/shard_map/all_to_all | solution.py:596
  53.0 9.9 %collective-permute-start.7 = (bf16[8,32,256]{2,1,0:T(8,128)(2,1)S(1)}, bf16[8,32,256]{2,1,0:T(8,128)(2,1)S(1)}, u32[]{:S(2)}, u32[]{:S(2)}) collective-permute-start(bf16[8,32,256]{2,1,0:T(8,128)(2,1)S(1)} %get-tuple-element.65), channel_id=1, source_target_pairs={{0,1},{1,0},{2,3},{3,2},{4,5},{5,4},{6,7},{7,6},{8,9},{9,8},{10,11... | collective-permute-start | bytes 393224 | tf_op jit(solution)/shard_map/ppermute | solution.py:563

commit v6 on v5

--- a/solution.py
+++ b/solution.py
@@ -227,7 +227,7 @@
         in_specs=[whole(ROWS, z.src_freq, z.src_dev)],
         out_specs=[whole(*shape)] * z.n_rcv,
         out_shape=[jax.ShapeDtypeStruct(shape, BF16)] * z.n_rcv,
-        scratch_shapes=[pltpu.VMEM((ROWS * z.src_freq, LANES), F32)],
+        scratch_shapes=[pltpu.VMEM(((ROWS + 1) * z.src_freq, LANES), F32)],
         compiler_params=pltpu.CompilerParams(vmem_limit_bytes=FULL_VMEM),
         cost_estimate=pl.CostEstimate(flops=10**6, bytes_accessed=2 * 10**6, transcendentals=0),
         name="pack_sources",
@@ -290,7 +290,7 @@
         out_specs=[whole(*shape)] * z.n_rcv + [whole(LAG_ROWS // 2, LANES)],
         out_shape=[jax.ShapeDtypeStruct(shape, BF16)] * z.n_rcv
         + [jax.ShapeDtypeStruct((LAG_ROWS // 2, LANES), BF16)],
-        scratch_shapes=[pltpu.VMEM((ROWS * z.rcv_freq, LANES), F32)] * (z.rcv_dev // LANES),
+        scratch_shapes=[pltpu.VMEM(((ROWS + 1) * z.rcv_freq, LANES), F32)] * (z.rcv_dev // LANES),
         compiler_params=pltpu.CompilerParams(vmem_limit_bytes=VMEM),
         cost_estimate=pl.CostEstimate(flops=10**6, bytes_accessed=2 * 10**6, transcendentals=0),
         name="pack_receivers",
@@ -485,7 +485,7 @@
         in_specs=[whole(z.own, ROWS, z.rcv_dev)] * len(others),
         out_specs=whole(ROWS, z.rcv_freq, z.rcv_dev),
         out_shape=jax.ShapeDtypeStruct((ROWS, z.rcv_freq, z.rcv_dev), F32),
-        scratch_shapes=[pltpu.VMEM((z.own * ROWS, LANES), F32)],
+        scratch_shapes=[pltpu.VMEM(((z.own + 1) * ROWS, LANES), F32)],
         compiler_params=pltpu.CompilerParams(vmem_limit_bytes=VMEM),
         cost_estimate=pl.CostEstimate(flops=10**6, bytes_accessed=10**6, transcendentals=0),
         name="unpack_first",
@@ -542,8 +542,8 @@
             whole(ROWS, width, z.n_freq),
         ],
         scratch_shapes=[
-            pltpu.VMEM((z.n_dev * ROWS, LANES), F32),
-            pltpu.VMEM((z.own * ROWS, LANES), F32),
+            pltpu.VMEM(((z.n_dev + 1) * ROWS, LANES), F32),
+            pltpu.VMEM(((z.own + 1) * ROWS, LANES), F32),
             pltpu.VMEM((ROWS * width, z.n_freq), BF16),
         ],
         out_shape=[
@@ -579,7 +579,6 @@
     parts = pack_sources(z)(src_rows)
     moved = {other: swap(z, parts[other], other) for other in (3, 2, 1, 0)}
     *packed, src_lags = pack_receivers(z)(rcv_pos[None], src_pos[None], rcv_rows, lag_table)
-    moved, packed, src_lags = lax.optimization_barrier((moved, packed, src_lags))
     spread = order_sources(z)(src_lags, *(moved[other] for other in range(z.n_rcv)))
     sources = lax.all_to_all(spread, "src", 0, 0, tiled=True)
     blocks = {other: swap(z, packed[other], other) for others in CALLS for other in others}

time: 65.2 us -> 65.2 us (level)
  no operation moved by 1% of the time
where the time goes in v6:
time: 65.2 us; the launch traced here: 64.8 us
  Pallas kernels  25.2 us (39%)
  starting transfers between devices  22.3 us (34%)
  waiting for transfers between devices  15 us (23%)
  local copies, waits for them, and re-layouts  1.72 us (3%)
  between operations  0.69 us (1%)
    pallas_call x4, Pallas kernels, per_device(): *panels, total = call(sources, *ready, *carry)  17.8 us
    ppermute x9, starting transfers between devices, swap(): return lax.ppermute(block, 'rcv', [(j, j ^ other) for j in range(z.n_rcv)])  14.9 us
    ppermute x9, waiting for transfers between devices, swap(): return lax.ppermute(block, 'rcv', [(j, j ^ other) for j in range(z.n_rcv)])  12 us
    all_to_all x1, starting transfers between devices, per_device(): sources = lax.all_to_all(spread, 'src', 0, 0, tiled=True)  3.72 us
    all_to_all x1, starting transfers between devices, per_device(): got_src = lax.all_to_all(total, ('src', 'rcv'), 0, 0, tiled=True)  3.69 us
    all_to_all x1, waiting for transfers between devices, per_device(): sources = lax.all_to_all(spread, 'src', 0, 0, tiled=True)  2.69 us
    pallas_call x1, Pallas kernels, per_device(): parts = pack_sources(z)(src_rows)  2.46 us
    unnamed x10, local copies, waits for them, and re-layouts  1.72 us
  transfers between devices with their start and end apart: 11, of which 6 were waited for; matrix products, arithmetic and copies ran while one was open for 0% of the time, Pallas kernels for 31%

profile of v6, /device:TPU:0, one launch (start us, length us, event | category | flops | bytes accessed | tf_op | source)
XLA Modules:
  0.0 64.8 jit_solution(6680167973477459788)
XLA Ops:
  0.6 2.5 %pack_sources.1 = (bf16[2,128,128]{2,1,0:T(8,128)(2,1)}, bf16[2,128,128]{2,1,0:T(8,128)(2,1)}, bf16[2,128,128]{2,1,0:T(8,128)(2,1)}, bf16[2,128,128]{2,1,0:T(8,128)(2,1)}) custom-call(bf16[32,64,64]{2,1,0:T(8,128)(2,1)} %bitcast.10), custom_call_target="tpu_custom_call" | custom-call | flops 1000000 | bytes 2000000 | tf_op jit(solution)/shard_map/pack_sources/pallas_call | solution.py:579
  3.1 3.0 %collective-permute-start = (bf16[2,128,128]{2,1,0:T(8,128)(2,1)}, bf16[2,128,128]{2,1,0:T(8,128)(2,1)S(1)}, u32[]{:S(2)}, u32[]{:S(2)}) collective-permute-start(bf16[2,128,128]{2,1,0:T(8,128)(2,1)} %get-tuple-element.31), channel_id=1, source_target_pairs={{0,1},{1,0},{2,3},{3,2},{4,5},{5,4},{6,7},{7,6},{8,9},{9,8},{10,11... | collective-permute-start | bytes 196616 | tf_op jit(solution)/shard_map/ppermute | solution.py:563
  6.1 2.6 %collective-permute-start.1 = (bf16[2,128,128]{2,1,0:T(8,128)(2,1)}, bf16[2,128,128]{2,1,0:T(8,128)(2,1)S(1)}, u32[]{:S(2)}, u32[]{:S(2)}) collective-permute-start(bf16[2,128,128]{2,1,0:T(8,128)(2,1)} %get-tuple-element.32), channel_id=1, source_target_pairs={{0,2},{1,3},{2,0},{3,1},{4,6},{5,7},{6,4},{7,5},{8,10},{9,11},{10,... | collective-permute-start | bytes 196616 | tf_op jit(solution)/shard_map/ppermute | solution.py:563
  8.7 0.0 collective-permute-start.2
  8.7 0.7 %copy-done.3 = s32[256]{0:T(256)S(1)} copy-done((s32[256]{0:T(256)S(1)}, s32[256]{0:T(256)}, u32[]{:S(2)}) %copy-start.3) | copy-done | bytes 1048
  9.4 1.0 %copy-done.1 = s32[16,8192]{1,0:T(8,128)S(1)} copy-done((s32[16,8192]{1,0:T(8,128)S(1)}, s32[16,8192]{1,0:T(8,128)}, u32[]{:S(2)}) %copy-start.1) | copy-done | bytes 524312
  10.4 1.1 %pack_receivers.1 = (bf16[272,256]{1,0:T(8,128)(2,1)S(1)}, bf16[272,256]{1,0:T(8,128)(2,1)S(1)}, bf16[272,256]{1,0:T(8,128)(2,1)S(1)}, bf16[272,256]{1,0:T(8,128)(2,1)S(1)}, bf16[8,128]{1,0:T(8,128)(2,1)S(1)}) custom-call(s32[1,256]{1,0:T(1,128)S(1)} %bitcast.7, s32[1,64]{1,0:T(1,128)S(1)} %bitcast.8, bf16[32,32,256]{2,1,0:T(8,128)(2,1)S(1)} %bitcast.6, ...), custom_call_target="tpu_custom_call" | custom-call | flops 1000000 | bytes 2000000 | tf_op jit(solution)/shard_map/pack_receivers/pallas_call | solution.py:581
  11.5 0.0 collective-permute-done.refs_1_
  11.5 2.1 %collective-permute-done.1.refs_2_ = bf16[2,128,128]{2,1,0:T(8,128)(2,1)S(1)} collective-permute-done((bf16[2,128,128]{2,1,0:T(8,128)(2,1)}, bf16[2,128,128]{2,1,0:T(8,128)(2,1)S(1)}, u32[]{:S(2)}, u32[]{:S(2)}) %collective-permute-start.1) | collective-permute-done | bytes 65568 | tf_op jit(solution)/shard_map/ppermute | solution.py:563
  13.6 1.4 %collective-permute-done.2.refs_3_ = bf16[2,128,128]{2,1,0:T(8,128)(2,1)S(1)} collective-permute-done((bf16[2,128,128]{2,1,0:T(8,128)(2,1)}, bf16[2,128,128]{2,1,0:T(8,128)(2,1)S(1)}, u32[]{:S(2)}, u32[]{:S(2)}) %collective-permute-start.2) | collective-permute-done | bytes 65568 | tf_op jit(solution)/shard_map/ppermute | solution.py:563
  15.0 0.7 %order_sources.1 = bf16[8,136,128]{2,1,0:T(8,128)(2,1)} custom-call(bf16[8,128]{1,0:T(8,128)(2,1)S(1)} %get-tuple-element.29.lag_ref, bf16[2,128,128]{2,1,0:T(8,128)(2,1)S(1)} %copy-done.2, bf16[2,128,128]{2,1,0:T(8,128)(2,1)S(1)} %collective-permute-done.refs_1_, bf16[2,128,128]{2,1,0:T(8,128)(2,1)S(1)} %collective-permute-done.1.refs_2_, ...), custom_call_target="tpu_custom_call" | custom-call | flops 1000000 | bytes 1000000 | tf_op jit(solution)/shard_map/order_sources/pallas_call | solution.py:582
  15.7 3.7 %all-to-all-start = ((bf16[8,136,128]{2,1,0:T(8,128)(2,1)}), bf16[8,136,128]{2,1,0:T(8,128)(2,1)S(1)}, u32[]{:S(2)}, u32[]{:S(2)}) async-start(bf16[8,136,128]{2,1,0:T(8,128)(2,1)} %order_sources.1), calls=%async_computation | async-start | bytes 557056 | tf_op jit(solution)/shard_map/all_to_all | solution.py:583
  19.5 1.8 %collective-permute-start.3 = (bf16[272,256]{1,0:T(8,128)(2,1)S(1)}, bf16[272,256]{1,0:T(8,128)(2,1)S(1)}, u32[]{:S(2)}, u32[]{:S(2)}) collective-permute-start(bf16[272,256]{1,0:T(8,128)(2,1)S(1)} %get-tuple-element.34), channel_id=1, source_target_pairs={{0,3},{1,2},{2,1},{3,0},{4,7},{5,6},{6,5},{7,4},{8,11},{9,10},{10,... | collective-permute-start | bytes 417800 | tf_op jit(solution)/shard_map/ppermute | solution.py:563
  21.3 0.0 collective-permute-start.6
  21.3 2.6 %collective-permute-start.5 = (bf16[272,256]{1,0:T(8,128)(2,1)S(1)}, bf16[272,256]{1,0:T(8,128)(2,1)S(1)}, u32[]{:S(2)}, u32[]{:S(2)}) collective-permute-start(bf16[272,256]{1,0:T(8,128)(2,1)S(1)} %get-tuple-element.38), channel_id=1, source_target_pairs={{0,1},{1,0},{2,3},{3,2},{4,5},{5,4},{6,7},{7,6},{8,9},{9,8},{10,11... | collective-permute-start | bytes 417800 | tf_op jit(solution)/shard_map/ppermute | solution.py:563
  23.9 2.7 %all-to-all-done.src_ref = bf16[8,136,128]{2,1,0:T(8,128)(2,1)S(1)} async-done(((bf16[8,136,128]{2,1,0:T(8,128)(2,1)}), bf16[8,136,128]{2,1,0:T(8,128)(2,1)S(1)}, u32[]{:S(2)}, u32[]{:S(2)}) %all-to-all-start) | async-done | bytes 278560 | tf_op jit(solution)/shard_map/all_to_all | solution.py:583
  26.6 4.1 %compute_first.1 = (bf16[8,32,256]{2,1,0:T(8,128)(2,1)S(1)}, f32[8,32,512]{2,1,0:T(8,128)S(1)}) custom-call(bf16[8,136,128]{2,1,0:T(8,128)(2,1)S(1)} %all-to-all-done.src_ref, bf16[272,256]{1,0:T(8,128)(2,1)S(1)} %get-tuple-element.35.refs_0_), custom_call_target="tpu_custom_call" | custom-call | flops 1000000 | bytes 1000000 | tf_op jit(solution)/shard_map/compute_first/pallas_call | solution.py:591
  30.7 4.1 %compute_next.2 = (bf16[8,32,256]{2,1,0:T(8,128)(2,1)S(1)}, f32[8,32,512]{2,1,0:T(8,128)S(1)}) custom-call(bf16[8,136,128]{2,1,0:T(8,128)(2,1)S(1)} %all-to-all-done.src_ref, bf16[272,256]{1,0:T(8,128)(2,1)S(1)} %collective-permute-done.3.refs_0_, f32[8,32,512]{2,1,0:T(8,128)S(1)} %get-tuple-element.36.refs_1_), custom_call_target="tpu_custom_call" | custom-call | flops 1000000 | bytes 1000000 | tf_op jit(solution)/shard_map/compute_next/pallas_call | solution.py:591
  34.8 1.8 %collective-permute-start.4 = (bf16[8,32,256]{2,1,0:T(8,128)(2,1)S(1)}, bf16[8,32,256]{2,1,0:T(8,128)(2,1)S(1)}, u32[]{:S(2)}, u32[]{:S(2)}) collective-permute-start(bf16[8,32,256]{2,1,0:T(8,128)(2,1)S(1)} %get-tuple-element.37), channel_id=1, source_target_pairs={{0,3},{1,2},{2,1},{3,0},{4,7},{5,6},{6,5},{7,4},{8,11},{9,10},{10,... | collective-permute-start | bytes 393224 | tf_op jit(solution)/shard_map/ppermute | solution.py:563
  36.7 0.0 collective-permute-done.6.refs_0_
  36.7 4.3 %compute_next.3 = (bf16[8,32,256]{2,1,0:T(8,128)(2,1)S(1)}, f32[8,32,512]{2,1,0:T(8,128)S(1)}) custom-call(bf16[8,136,128]{2,1,0:T(8,128)(2,1)S(1)} %all-to-all-done.src_ref, bf16[272,256]{1,0:T(8,128)(2,1)S(1)} %collective-permute-done.6.refs_0_, f32[8,32,512]{2,1,0:T(8,128)S(1)} %get-tuple-element.43.refs_1_), custom_call_target="tpu_custom_call" | custom-call | flops 1000000 | bytes 1000000 | tf_op jit(solution)/shard_map/compute_next/pallas_call | solution.py:591
  41.0 1.1 %collective-permute-start.8 = (bf16[8,32,256]{2,1,0:T(8,128)(2,1)S(1)}, bf16[8,32,256]{2,1,0:T(8,128)(2,1)S(1)}, u32[]{:S(2)}, u32[]{:S(2)}) collective-permute-start(bf16[8,32,256]{2,1,0:T(8,128)(2,1)S(1)} %get-tuple-element.48), channel_id=1, source_target_pairs={{0,2},{1,3},{2,0},{3,1},{4,6},{5,7},{6,4},{7,5},{8,10},{9,11},{10,... | collective-permute-start | bytes 393224 | tf_op jit(solution)/shard_map/ppermute | solution.py:563
  42.2 0.0 collective-permute-done.5.refs_0_
  42.2 0.0 collective-permute-done.4.refs_1_
  42.2 5.2 %compute_last.1 = (bf16[8,32,256]{2,1,0:T(8,128)(2,1)S(1)}, bf16[32,32,128]{2,1,0:T(8,128)(2,1)}) custom-call(bf16[8,136,128]{2,1,0:T(8,128)(2,1)S(1)} %all-to-all-done.src_ref, bf16[272,256]{1,0:T(8,128)(2,1)S(1)} %collective-permute-done.5.refs_0_, f32[8,32,512]{2,1,0:T(8,128)S(1)} %get-tuple-element.46.refs_1_), custom_call_target="tpu_custom_call" | custom-call | flops 1000000 | bytes 1000000 | tf_op jit(solution)/shard_map/compute_last/pallas_call | solution.py:591
  47.4 1.9 %collective-permute-done.8.refs_2_ = bf16[8,32,256]{2,1,0:T(8,128)(2,1)S(1)} collective-permute-done((bf16[8,32,256]{2,1,0:T(8,128)(2,1)S(1)}, bf16[8,32,256]{2,1,0:T(8,128)(2,1)S(1)}, u32[]{:S(2)}, u32[]{:S(2)}) %collective-permute-start.8) | collective-permute-done | bytes 131104 | tf_op jit(solution)/shard_map/ppermute | solution.py:563
  49.3 3.7 %all-to-all-start.1 = ((bf16[32,32,128]{2,1,0:T(8,128)(2,1)}), bf16[32,32,128]{2,1,0:T(8,128)(2,1)S(1)}, u32[]{:S(2)}, u32[]{:S(2)}) async-start(bf16[32,32,128]{2,1,0:T(8,128)(2,1)} %get-tuple-element.50), calls=%async_computation.1 | async-start | bytes 524288 | tf_op jit(solution)/shard_map/all_to_all | solution.py:595
  53.0 1.8 %collective-permute-start.7 = (bf16[8,32,256]{2,1,0:T(8,128)(2,1)S(1)}, bf16[8,32,256]{2,1,0:T(8,128)(2,1)S(1)}, u32[]{:S(2)}, u32[]{:S(2)}) collective-permute-start(bf16[8,32,256]{2,1,0:T(8,128)(2,1)S(1)} %get-tuple-element.47), channel_id=1, source_target_pairs={{0,1},{1,0},{2,3},{3,2},{4,5},{5,4},{6,7},{7,6},{8,9},{9,8},{10,11... | collective-permute-start | bytes 393224 | tf_op jit(solution)/shard_map/ppermute | solution.py:563
  54.8 1.5 %unpack_first.1.held_ref = f32[32,32,256]{2,1,0:T(8,128)} custom-call(bf16[8,32,256]{2,1,0:T(8,128)(2,1)S(1)} %get-tuple-element.51.refs_0_, bf16[8,32,256]{2,1,0:T(8,128)(2,1)S(1)} %collective-permute-done.4.refs_1_, bf16[8,32,256]{2,1,0:T(8,128)(2,1)S(1)} %collective-permute-done.8.refs_2_), custom_call_target="tpu_custom_call" | custom-call | flops 1000000 | bytes 1000000 | tf_op jit(solution)/shard_map/unpack_first/pallas_call | solution.py:598
  56.3 6.6 %collective-permute-done.7.rcv_in = bf16[8,32,256]{2,1,0:T(8,128)(2,1)S(1)} collective-permute-done((bf16[8,32,256]{2,1,0:T(8,128)(2,1)S(1)}, bf16[8,32,256]{2,1,0:T(8,128)(2,1)S(1)}, u32[]{:S(2)}, u32[]{:S(2)}) %collective-permute-start.7) | collective-permute-done | bytes 131104 | tf_op jit(solution)/shard_map/ppermute | solution.py:563
  62.8 0.3 all-to-all-done.1.src_in
  63.2 1.7 %unpack_last.1 = (f32[32,32,256]{2,1,0:T(8,128)}, f32[32,16,256]{2,1,0:T(8,128)}) custom-call(bf16[8,32,256]{2,1,0:T(8,128)(2,1)S(1)} %collective-permute-done.7.rcv_in, bf16[32,32,128]{2,1,0:T(8,128)(2,1)S(1)} %all-to-all-done.1.src_in, f32[32,32,256]{2,1,0:T(8,128)} %unpack_first.1.held_ref), custom_call_target="tpu_custom_call", output_to_operand_aliasing={{0}: (2, {})} | custom-call | flops 1000000 | bytes 2000000 | tf_op jit(solution)/shard_map/unpack_last/pallas_call | solution.py:599
  (9 shorter events, 0.0 us)
Async XLA Ops:
  0.6 8.1 %copy-start = (bf16[2,16,32,256]{3,2,1,0:T(8,128)(2,1)S(1)}, bf16[2,16,32,256]{3,2,1,0:T(8,128)(2,1)}, u32[]{:S(2)}) copy-start(bf16[2,16,32,256]{3,2,1,0:T(8,128)(2,1)} %param.6) | copy-start | bytes 1572868
  3.1 8.4 %collective-permute-start = (bf16[2,128,128]{2,1,0:T(8,128)(2,1)}, bf16[2,128,128]{2,1,0:T(8,128)(2,1)S(1)}, u32[]{:S(2)}, u32[]{:S(2)}) collective-permute-start(bf16[2,128,128]{2,1,0:T(8,128)(2,1)} %get-tuple-element.31), channel_id=1, source_target_pairs={{0,1},{1,0},{2,3},{3,2},{4,5},{5,4},{6,7},{7,6},{8,9},{9,8},{10,11... | collective-permute-start | bytes 196616 | tf_op jit(solution)/shard_map/ppermute | solution.py:563
  6.1 7.5 %collective-permute-start.1 = (bf16[2,128,128]{2,1,0:T(8,128)(2,1)}, bf16[2,128,128]{2,1,0:T(8,128)(2,1)S(1)}, u32[]{:S(2)}, u32[]{:S(2)}) collective-permute-start(bf16[2,128,128]{2,1,0:T(8,128)(2,1)} %get-tuple-element.32), channel_id=1, source_target_pairs={{0,2},{1,3},{2,0},{3,1},{4,6},{5,7},{6,4},{7,5},{8,10},{9,11},{10,... | collective-permute-start | bytes 196616 | tf_op jit(solution)/shard_map/ppermute | solution.py:563
  8.7 6.3 %collective-permute-start.2 = (bf16[2,128,128]{2,1,0:T(8,128)(2,1)}, bf16[2,128,128]{2,1,0:T(8,128)(2,1)S(1)}, u32[]{:S(2)}, u32[]{:S(2)}) collective-permute-start(bf16[2,128,128]{2,1,0:T(8,128)(2,1)} %get-tuple-element.33), channel_id=1, source_target_pairs={{0,3},{1,2},{2,1},{3,0},{4,7},{5,6},{6,5},{7,4},{8,11},{9,10},{10,... | collective-permute-start | bytes 196616 | tf_op jit(solution)/shard_map/ppermute | solution.py:563
  8.7 0.7 %copy-start.3 = (s32[256]{0:T(256)S(1)}, s32[256]{0:T(256)}, u32[]{:S(2)}) copy-start(s32[256]{0:T(256)} %param.9) | copy-start | bytes 3076
  8.7 0.7 %copy-start.4 = (s32[64]{0:T(128)S(1)}, s32[64]{0:T(128)}, u32[]{:S(2)}) copy-start(s32[64]{0:T(128)} %param.8) | copy-start | bytes 772
  9.4 1.0 %copy-start.1 = (s32[16,8192]{1,0:T(8,128)S(1)}, s32[16,8192]{1,0:T(8,128)}, u32[]{:S(2)}) copy-start(s32[16,8192]{1,0:T(8,128)} %lag_ref.1) | copy-start | bytes 1572868
  10.4 4.6 %copy-start.2 = (bf16[2,128,128]{2,1,0:T(8,128)(2,1)S(1)}, bf16[2,128,128]{2,1,0:T(8,128)(2,1)}, u32[]{:S(2)}) copy-start(bf16[2,128,128]{2,1,0:T(8,128)(2,1)} %get-tuple-element.30.refs_0_) | copy-start | bytes 196612
  15.7 10.8 %all-to-all-start = ((bf16[8,136,128]{2,1,0:T(8,128)(2,1)}), bf16[8,136,128]{2,1,0:T(8,128)(2,1)S(1)}, u32[]{:S(2)}, u32[]{:S(2)}) async-start(bf16[8,136,128]{2,1,0:T(8,128)(2,1)} %order_sources.1), calls=%async_computation | async-start | bytes 557056 | tf_op jit(solution)/shard_map/all_to_all | solution.py:583
  19.5 11.2 %collective-permute-start.3 = (bf16[272,256]{1,0:T(8,128)(2,1)S(1)}, bf16[272,256]{1,0:T(8,128)(2,1)S(1)}, u32[]{:S(2)}, u32[]{:S(2)}) collective-permute-start(bf16[272,256]{1,0:T(8,128)(2,1)S(1)} %get-tuple-element.34), channel_id=1, source_target_pairs={{0,3},{1,2},{2,1},{3,0},{4,7},{5,6},{6,5},{7,4},{8,11},{9,10},{10,... | collective-permute-start | bytes 417800 | tf_op jit(solution)/shard_map/ppermute | solution.py:563
  21.3 15.4 %collective-permute-start.6 = (bf16[272,256]{1,0:T(8,128)(2,1)S(1)}, bf16[272,256]{1,0:T(8,128)(2,1)S(1)}, u32[]{:S(2)}, u32[]{:S(2)}) collective-permute-start(bf16[272,256]{1,0:T(8,128)(2,1)S(1)} %get-tuple-element.40), channel_id=1, source_target_pairs={{0,2},{1,3},{2,0},{3,1},{4,6},{5,7},{6,4},{7,5},{8,10},{9,11},{10,... | collective-permute-start | bytes 417800 | tf_op jit(solution)/shard_map/ppermute | solution.py:563
  21.3 20.9 %collective-permute-start.5 = (bf16[272,256]{1,0:T(8,128)(2,1)S(1)}, bf16[272,256]{1,0:T(8,128)(2,1)S(1)}, u32[]{:S(2)}, u32[]{:S(2)}) collective-permute-start(bf16[272,256]{1,0:T(8,128)(2,1)S(1)} %get-tuple-element.38), channel_id=1, source_target_pairs={{0,1},{1,0},{2,3},{3,2},{4,5},{5,4},{6,7},{7,6},{8,9},{9,8},{10,11... | collective-permute-start | bytes 417800 | tf_op jit(solution)/shard_map/ppermute | solution.py:563
  34.8 7.4 %collective-permute-start.4 = (bf16[8,32,256]{2,1,0:T(8,128)(2,1)S(1)}, bf16[8,32,256]{2,1,0:T(8,128)(2,1)S(1)}, u32[]{:S(2)}, u32[]{:S(2)}) collective-permute-start(bf16[8,32,256]{2,1,0:T(8,128)(2,1)S(1)} %get-tuple-element.37), channel_id=1, source_target_pairs={{0,3},{1,2},{2,1},{3,0},{4,7},{5,6},{6,5},{7,4},{8,11},{9,10},{10,... | collective-permute-start | bytes 393224 | tf_op jit(solution)/shard_map/ppermute | solution.py:563
  41.0 8.2 %collective-permute-start.8 = (bf16[8,32,256]{2,1,0:T(8,128)(2,1)S(1)}, bf16[8,32,256]{2,1,0:T(8,128)(2,1)S(1)}, u32[]{:S(2)}, u32[]{:S(2)}) collective-permute-start(bf16[8,32,256]{2,1,0:T(8,128)(2,1)S(1)} %get-tuple-element.48), channel_id=1, source_target_pairs={{0,2},{1,3},{2,0},{3,1},{4,6},{5,7},{6,4},{7,5},{8,10},{9,11},{10,... | collective-permute-start | bytes 393224 | tf_op jit(solution)/shard_map/ppermute | solution.py:563
  49.3 13.9 %all-to-all-start.1 = ((bf16[32,32,128]{2,1,0:T(8,128)(2,1)}), bf16[32,32,128]{2,1,0:T(8,128)(2,1)S(1)}, u32[]{:S(2)}, u32[]{:S(2)}) async-start(bf16[32,32,128]{2,1,0:T(8,128)(2,1)} %get-tuple-element.50), calls=%async_computation.1 | async-start | bytes 524288 | tf_op jit(solution)/shard_map/all_to_all | solution.py:595
  53.0 9.9 %collective-permute-start.7 = (bf16[8,32,256]{2,1,0:T(8,128)(2,1)S(1)}, bf16[8,32,256]{2,1,0:T(8,128)(2,1)S(1)}, u32[]{:S(2)}, u32[]{:S(2)}) collective-permute-start(bf16[8,32,256]{2,1,0:T(8,128)(2,1)S(1)} %get-tuple-element.47), channel_id=1, source_target_pairs={{0,1},{1,0},{2,3},{3,2},{4,5},{5,4},{6,7},{7,6},{8,9},{9,8},{10,11... | collective-permute-start | bytes 393224 | tf_op jit(solution)/shard_map/ppermute | solution.py:563

commit v7 on v6

--- a/solution.py
+++ b/solution.py
@@ -117,6 +117,7 @@
 LANES = 128
 ROWS = 32
 LAG_ROWS = 16
+FAR_FIRST = (3, 2, 1, 0)
 CALLS = ((0,), (3,), (2,), (1,))
 VMEM = 20 * 2**20
 FULL_VMEM = 56 * 2**20
@@ -237,9 +238,9 @@
 def order_sources(z):
     def kernel(lag_ref, *refs):
         out_ref = refs[-1]
-        for other in range(z.n_rcv):
+        for other, ref in zip(FAR_FIRST, refs):
             place = lax.axis_index("rcv") ^ other
-            out_ref[pl.ds(place * z.low, z.low), :z.chunk, :] = refs[other][...]
+            out_ref[pl.ds(place * z.low, z.low), :z.chunk, :] = ref[...]
         for place in range(z.n_src):
             out_ref[place, z.chunk:, :] = lag_ref[...]
 
@@ -577,9 +578,9 @@
     src_rows = src_spec.reshape(ROWS, z.src_freq, z.src_dev)
     rcv_rows = rcv_spec.reshape(ROWS, z.rcv_freq, z.rcv_dev)
     parts = pack_sources(z)(src_rows)
-    moved = {other: swap(z, parts[other], other) for other in (3, 2, 1, 0)}
+    moved = {other: swap(z, parts[other], other) for other in FAR_FIRST}
     *packed, src_lags = pack_receivers(z)(rcv_pos[None], src_pos[None], rcv_rows, lag_table)
-    spread = order_sources(z)(src_lags, *(moved[other] for other in range(z.n_rcv)))
+    spread = order_sources(z)(src_lags, *(moved[other] for other in FAR_FIRST))
     sources = lax.all_to_all(spread, "src", 0, 0, tiled=True)
     blocks = {other: swap(z, packed[other], other) for others in CALLS for other in others}
     done, carry = {}, ()

time: 65.2 us -> 64.3 us (0.986)
  waiting for transfers between devices: 15 us -> 13.7 us
    ppermute x9, waiting for transfers between devices: 12 us -> 10.7 us  [swap(): return lax.ppermute(block, 'rcv', [(j, j ^ other) for j in range(z.n_rcv)])]
    ppermute x9, starting transfers between devices: 14.9 us -> 15.8 us  [swap(): return lax.ppermute(block, 'rcv', [(j, j ^ other) for j in range(z.n_rcv)])]
  transfers between devices with their start and end apart: 11 -> 11, of which waited for: 6 -> 5; matrix products, arithmetic and copies ran while one was open for 0% -> 0% of each run, Pallas kernels for 31% -> 32%
where the time goes in v7:
time: 64.3 us; the launch traced here: 63.9 us
  Pallas kernels  25.2 us (39%)
  starting transfers between devices  22.6 us (35%)
  waiting for transfers between devices  13.7 us (21%)
  local copies, waits for them, and re-layouts  1.73 us (3%)
  between operations  0.69 us (1%)
    pallas_call x4, Pallas kernels, per_device(): *panels, total = call(sources, *ready, *carry)  17.8 us
    ppermute x9, starting transfers between devices, swap(): return lax.ppermute(block, 'rcv', [(j, j ^ other) for j in range(z.n_rcv)])  15.8 us
    ppermute x9, waiting for transfers between devices, swap(): return lax.ppermute(block, 'rcv', [(j, j ^ other) for j in range(z.n_rcv)])  10.7 us
    all_to_all x1, starting transfers between devices, per_device(): sources = lax.all_to_all(spread, 'src', 0, 0, tiled=True)  3.72 us
    all_to_all x1, starting transfers between devices, per_device(): got_src = lax.all_to_all(total, ('src', 'rcv'), 0, 0, tiled=True)  3.16 us
    all_to_all x1, waiting for transfers between devices, per_device(): sources = lax.all_to_all(spread, 'src', 0, 0, tiled=True)  2.69 us
    pallas_call x1, Pallas kernels, per_device(): parts = pack_sources(z)(src_rows)  2.46 us
    unnamed x10, local copies, waits for them, and re-layouts  1.73 us
  transfers between devices with their start and end apart: 11, of which 5 were waited for; matrix products, arithmetic and copies ran while one was open for 0% of the time, Pallas kernels for 32%

profile of v7, /device:TPU:0, one launch (start us, length us, event | category | flops | bytes accessed | tf_op | source)
XLA Modules:
  0.0 63.9 jit_solution(7387839495429933920)
XLA Ops:
  0.6 2.5 %pack_sources.1 = (bf16[2,128,128]{2,1,0:T(8,128)(2,1)}, bf16[2,128,128]{2,1,0:T(8,128)(2,1)}, bf16[2,128,128]{2,1,0:T(8,128)(2,1)}, bf16[2,128,128]{2,1,0:T(8,128)(2,1)}) custom-call(bf16[32,64,64]{2,1,0:T(8,128)(2,1)} %bitcast.10), custom_call_target="tpu_custom_call" | custom-call | flops 1000000 | bytes 2000000 | tf_op jit(solution)/shard_map/pack_sources/pallas_call | solution.py:580
  3.1 5.0 %collective-permute-start = (bf16[2,128,128]{2,1,0:T(8,128)(2,1)}, bf16[2,128,128]{2,1,0:T(8,128)(2,1)S(1)}, u32[]{:S(2)}, u32[]{:S(2)}) collective-permute-start(bf16[2,128,128]{2,1,0:T(8,128)(2,1)} %get-tuple-element.30), channel_id=1, source_target_pairs={{0,3},{1,2},{2,1},{3,0},{4,7},{5,6},{6,5},{7,4},{8,11},{9,10},{10,... | collective-permute-start | bytes 196616 | tf_op jit(solution)/shard_map/ppermute | solution.py:564
  8.2 0.0 collective-permute-start.1
  8.2 0.6 collective-permute-start.2
  8.7 0.7 %copy-done.3 = s32[256]{0:T(256)S(1)} copy-done((s32[256]{0:T(256)S(1)}, s32[256]{0:T(256)}, u32[]{:S(2)}) %copy-start.3) | copy-done | bytes 1048
  9.4 1.0 %copy-done.1 = s32[16,8192]{1,0:T(8,128)S(1)} copy-done((s32[16,8192]{1,0:T(8,128)S(1)}, s32[16,8192]{1,0:T(8,128)}, u32[]{:S(2)}) %copy-start.1) | copy-done | bytes 524312
  10.4 1.1 %pack_receivers.1 = (bf16[272,256]{1,0:T(8,128)(2,1)S(1)}, bf16[272,256]{1,0:T(8,128)(2,1)S(1)}, bf16[272,256]{1,0:T(8,128)(2,1)S(1)}, bf16[272,256]{1,0:T(8,128)(2,1)S(1)}, bf16[8,128]{1,0:T(8,128)(2,1)S(1)}) custom-call(s32[1,256]{1,0:T(1,128)S(1)} %bitcast.7, s32[1,64]{1,0:T(1,128)S(1)} %bitcast.8, bf16[32,32,256]{2,1,0:T(8,128)(2,1)S(1)} %bitcast.6, ...), custom_call_target="tpu_custom_call" | custom-call | flops 1000000 | bytes 2000000 | tf_op jit(solution)/shard_map/pack_receivers/pallas_call | solution.py:582
  11.5 0.0 collective-permute-done.refs_0_
  11.5 2.4 %collective-permute-done.1.refs_1_ = bf16[2,128,128]{2,1,0:T(8,128)(2,1)S(1)} collective-permute-done((bf16[2,128,128]{2,1,0:T(8,128)(2,1)}, bf16[2,128,128]{2,1,0:T(8,128)(2,1)S(1)}, u32[]{:S(2)}, u32[]{:S(2)}) %collective-permute-start.1) | collective-permute-done | bytes 65568 | tf_op jit(solution)/shard_map/ppermute | solution.py:564
  14.0 0.0 collective-permute-done.2.refs_2_
  14.0 0.7 %order_sources.1 = bf16[8,136,128]{2,1,0:T(8,128)(2,1)} custom-call(bf16[8,128]{1,0:T(8,128)(2,1)S(1)} %get-tuple-element.29.lag_ref, bf16[2,128,128]{2,1,0:T(8,128)(2,1)S(1)} %collective-permute-done.refs_0_, bf16[2,128,128]{2,1,0:T(8,128)(2,1)S(1)} %collective-permute-done.1.refs_1_, bf16[2,128,128]{2,1,0:T(8,128)(2,1)S(1)} %collective-permute-done.2.refs_2_, ...), custom_call_target="tpu_custom_call" | custom-call | flops 1000000 | bytes 1000000 | tf_op jit(solution)/shard_map/order_sources/pallas_call | solution.py:583
  14.7 3.7 %all-to-all-start = ((bf16[8,136,128]{2,1,0:T(8,128)(2,1)}), bf16[8,136,128]{2,1,0:T(8,128)(2,1)S(1)}, u32[]{:S(2)}, u32[]{:S(2)}) async-start(bf16[8,136,128]{2,1,0:T(8,128)(2,1)} %order_sources.1), calls=%async_computation | async-start | bytes 557056 | tf_op jit(solution)/shard_map/all_to_all | solution.py:584
  18.4 2.7 %collective-permute-start.3 = (bf16[272,256]{1,0:T(8,128)(2,1)S(1)}, bf16[272,256]{1,0:T(8,128)(2,1)S(1)}, u32[]{:S(2)}, u32[]{:S(2)}) collective-permute-start(bf16[272,256]{1,0:T(8,128)(2,1)S(1)} %get-tuple-element.34), channel_id=1, source_target_pairs={{0,3},{1,2},{2,1},{3,0},{4,7},{5,6},{6,5},{7,4},{8,11},{9,10},{10,... | collective-permute-start | bytes 417800 | tf_op jit(solution)/shard_map/ppermute | solution.py:564
  21.1 0.0 collective-permute-start.6
  21.1 1.7 %collective-permute-start.5 = (bf16[272,256]{1,0:T(8,128)(2,1)S(1)}, bf16[272,256]{1,0:T(8,128)(2,1)S(1)}, u32[]{:S(2)}, u32[]{:S(2)}) collective-permute-start(bf16[272,256]{1,0:T(8,128)(2,1)S(1)} %get-tuple-element.38), channel_id=1, source_target_pairs={{0,1},{1,0},{2,3},{3,2},{4,5},{5,4},{6,7},{7,6},{8,9},{9,8},{10,11... | collective-permute-start | bytes 417800 | tf_op jit(solution)/shard_map/ppermute | solution.py:564
  22.9 2.7 %all-to-all-done.src_ref = bf16[8,136,128]{2,1,0:T(8,128)(2,1)S(1)} async-done(((bf16[8,136,128]{2,1,0:T(8,128)(2,1)}), bf16[8,136,128]{2,1,0:T(8,128)(2,1)S(1)}, u32[]{:S(2)}, u32[]{:S(2)}) %all-to-all-start) | async-done | bytes 278560 | tf_op jit(solution)/shard_map/all_to_all | solution.py:584
  25.5 4.1 %compute_first.1 = (bf16[8,32,256]{2,1,0:T(8,128)(2,1)S(1)}, f32[8,32,512]{2,1,0:T(8,128)S(1)}) custom-call(bf16[8,136,128]{2,1,0:T(8,128)(2,1)S(1)} %all-to-all-done.src_ref, bf16[272,256]{1,0:T(8,128)(2,1)S(1)} %get-tuple-element.35.refs_0_), custom_call_target="tpu_custom_call" | custom-call | flops 1000000 | bytes 1000000 | tf_op jit(solution)/shard_map/compute_first/pallas_call | solution.py:592
  29.7 0.0 collective-permute-done.3.refs_0_
  29.7 4.1 %compute_next.2 = (bf16[8,32,256]{2,1,0:T(8,128)(2,1)S(1)}, f32[8,32,512]{2,1,0:T(8,128)S(1)}) custom-call(bf16[8,136,128]{2,1,0:T(8,128)(2,1)S(1)} %all-to-all-done.src_ref, bf16[272,256]{1,0:T(8,128)(2,1)S(1)} %collective-permute-done.3.refs_0_, f32[8,32,512]{2,1,0:T(8,128)S(1)} %get-tuple-element.36.refs_1_), custom_call_target="tpu_custom_call" | custom-call | flops 1000000 | bytes 1000000 | tf_op jit(solution)/shard_map/compute_next/pallas_call | solution.py:592
  33.8 2.7 %collective-permute-start.4 = (bf16[8,32,256]{2,1,0:T(8,128)(2,1)S(1)}, bf16[8,32,256]{2,1,0:T(8,128)(2,1)S(1)}, u32[]{:S(2)}, u32[]{:S(2)}) collective-permute-start(bf16[8,32,256]{2,1,0:T(8,128)(2,1)S(1)} %get-tuple-element.37), channel_id=1, source_target_pairs={{0,3},{1,2},{2,1},{3,0},{4,7},{5,6},{6,5},{7,4},{8,11},{9,10},{10,... | collective-permute-start | bytes 393224 | tf_op jit(solution)/shard_map/ppermute | solution.py:564
  36.5 0.0 collective-permute-done.6.refs_0_
  36.5 4.3 %compute_next.3 = (bf16[8,32,256]{2,1,0:T(8,128)(2,1)S(1)}, f32[8,32,512]{2,1,0:T(8,128)S(1)}) custom-call(bf16[8,136,128]{2,1,0:T(8,128)(2,1)S(1)} %all-to-all-done.src_ref, bf16[272,256]{1,0:T(8,128)(2,1)S(1)} %collective-permute-done.6.refs_0_, f32[8,32,512]{2,1,0:T(8,128)S(1)} %get-tuple-element.43.refs_1_), custom_call_target="tpu_custom_call" | custom-call | flops 1000000 | bytes 1000000 | tf_op jit(solution)/shard_map/compute_next/pallas_call | solution.py:592
  40.9 1.2 %collective-permute-start.8 = (bf16[8,32,256]{2,1,0:T(8,128)(2,1)S(1)}, bf16[8,32,256]{2,1,0:T(8,128)(2,1)S(1)}, u32[]{:S(2)}, u32[]{:S(2)}) collective-permute-start(bf16[8,32,256]{2,1,0:T(8,128)(2,1)S(1)} %get-tuple-element.48), channel_id=1, source_target_pairs={{0,2},{1,3},{2,0},{3,1},{4,6},{5,7},{6,4},{7,5},{8,10},{9,11},{10,... | collective-permute-start | bytes 393224 | tf_op jit(solution)/shard_map/ppermute | solution.py:564
  42.1 0.0 collective-permute-done.4.refs_1_
  42.1 5.2 %compute_last.1 = (bf16[8,32,256]{2,1,0:T(8,128)(2,1)S(1)}, bf16[32,32,128]{2,1,0:T(8,128)(2,1)}) custom-call(bf16[8,136,128]{2,1,0:T(8,128)(2,1)S(1)} %all-to-all-done.src_ref, bf16[272,256]{1,0:T(8,128)(2,1)S(1)} %collective-permute-done.5.refs_0_, f32[8,32,512]{2,1,0:T(8,128)S(1)} %get-tuple-element.46.refs_1_), custom_call_target="tpu_custom_call" | custom-call | flops 1000000 | bytes 1000000 | tf_op jit(solution)/shard_map/compute_last/pallas_call | solution.py:592
  47.2 1.6 %collective-permute-done.8.refs_2_ = bf16[8,32,256]{2,1,0:T(8,128)(2,1)S(1)} collective-permute-done((bf16[8,32,256]{2,1,0:T(8,128)(2,1)S(1)}, bf16[8,32,256]{2,1,0:T(8,128)(2,1)S(1)}, u32[]{:S(2)}, u32[]{:S(2)}) %collective-permute-start.8) | collective-permute-done | bytes 131104 | tf_op jit(solution)/shard_map/ppermute | solution.py:564
  48.9 3.2 %all-to-all-start.1 = ((bf16[32,32,128]{2,1,0:T(8,128)(2,1)}), bf16[32,32,128]{2,1,0:T(8,128)(2,1)S(1)}, u32[]{:S(2)}, u32[]{:S(2)}) async-start(bf16[32,32,128]{2,1,0:T(8,128)(2,1)} %get-tuple-element.50), calls=%async_computation.1 | async-start | bytes 524288 | tf_op jit(solution)/shard_map/all_to_all | solution.py:596
  52.0 1.8 %collective-permute-start.7 = (bf16[8,32,256]{2,1,0:T(8,128)(2,1)S(1)}, bf16[8,32,256]{2,1,0:T(8,128)(2,1)S(1)}, u32[]{:S(2)}, u32[]{:S(2)}) collective-permute-start(bf16[8,32,256]{2,1,0:T(8,128)(2,1)S(1)} %get-tuple-element.47), channel_id=1, source_target_pairs={{0,1},{1,0},{2,3},{3,2},{4,5},{5,4},{6,7},{7,6},{8,9},{9,8},{10,11... | collective-permute-start | bytes 393224 | tf_op jit(solution)/shard_map/ppermute | solution.py:564
  53.9 1.5 %unpack_first.1.held_ref = f32[32,32,256]{2,1,0:T(8,128)} custom-call(bf16[8,32,256]{2,1,0:T(8,128)(2,1)S(1)} %get-tuple-element.51.refs_0_, bf16[8,32,256]{2,1,0:T(8,128)(2,1)S(1)} %collective-permute-done.4.refs_1_, bf16[8,32,256]{2,1,0:T(8,128)(2,1)S(1)} %collective-permute-done.8.refs_2_), custom_call_target="tpu_custom_call" | custom-call | flops 1000000 | bytes 1000000 | tf_op jit(solution)/shard_map/unpack_first/pallas_call | solution.py:599
  55.3 6.6 %collective-permute-done.7.rcv_in = bf16[8,32,256]{2,1,0:T(8,128)(2,1)S(1)} collective-permute-done((bf16[8,32,256]{2,1,0:T(8,128)(2,1)S(1)}, bf16[8,32,256]{2,1,0:T(8,128)(2,1)S(1)}, u32[]{:S(2)}, u32[]{:S(2)}) %collective-permute-start.7) | collective-permute-done | bytes 131104 | tf_op jit(solution)/shard_map/ppermute | solution.py:564
  61.9 0.3 all-to-all-done.1.src_in
  62.2 1.7 %unpack_last.1 = (f32[32,32,256]{2,1,0:T(8,128)}, f32[32,16,256]{2,1,0:T(8,128)}) custom-call(bf16[8,32,256]{2,1,0:T(8,128)(2,1)S(1)} %collective-permute-done.7.rcv_in, bf16[32,32,128]{2,1,0:T(8,128)(2,1)S(1)} %all-to-all-done.1.src_in, f32[32,32,256]{2,1,0:T(8,128)} %unpack_first.1.held_ref), custom_call_target="tpu_custom_call", output_to_operand_aliasing={{0}: (2, {})} | custom-call | flops 1000000 | bytes 2000000 | tf_op jit(solution)/shard_map/unpack_last/pallas_call | solution.py:600
  (9 shorter events, 0.0 us)
Async XLA Ops:
  0.6 8.1 %copy-start = (bf16[2,16,32,256]{3,2,1,0:T(8,128)(2,1)S(1)}, bf16[2,16,32,256]{3,2,1,0:T(8,128)(2,1)}, u32[]{:S(2)}) copy-start(bf16[2,16,32,256]{3,2,1,0:T(8,128)(2,1)} %param.6) | copy-start | bytes 1572868
  3.1 8.4 %collective-permute-start = (bf16[2,128,128]{2,1,0:T(8,128)(2,1)}, bf16[2,128,128]{2,1,0:T(8,128)(2,1)S(1)}, u32[]{:S(2)}, u32[]{:S(2)}) collective-permute-start(bf16[2,128,128]{2,1,0:T(8,128)(2,1)} %get-tuple-element.30), channel_id=1, source_target_pairs={{0,3},{1,2},{2,1},{3,0},{4,7},{5,6},{6,5},{7,4},{8,11},{9,10},{10,... | collective-permute-start | bytes 196616 | tf_op jit(solution)/shard_map/ppermute | solution.py:564
  8.2 5.8 %collective-permute-start.1 = (bf16[2,128,128]{2,1,0:T(8,128)(2,1)}, bf16[2,128,128]{2,1,0:T(8,128)(2,1)S(1)}, u32[]{:S(2)}, u32[]{:S(2)}) collective-permute-start(bf16[2,128,128]{2,1,0:T(8,128)(2,1)} %get-tuple-element.31), channel_id=1, source_target_pairs={{0,2},{1,3},{2,0},{3,1},{4,6},{5,7},{6,4},{7,5},{8,10},{9,11},{10,... | collective-permute-start | bytes 196616 | tf_op jit(solution)/shard_map/ppermute | solution.py:564
  8.2 5.8 %collective-permute-start.2 = (bf16[2,128,128]{2,1,0:T(8,128)(2,1)}, bf16[2,128,128]{2,1,0:T(8,128)(2,1)S(1)}, u32[]{:S(2)}, u32[]{:S(2)}) collective-permute-start(bf16[2,128,128]{2,1,0:T(8,128)(2,1)} %get-tuple-element.32), channel_id=1, source_target_pairs={{0,1},{1,0},{2,3},{3,2},{4,5},{5,4},{6,7},{7,6},{8,9},{9,8},{10,11... | collective-permute-start | bytes 196616 | tf_op jit(solution)/shard_map/ppermute | solution.py:564
  8.7 0.7 %copy-start.3 = (s32[256]{0:T(256)S(1)}, s32[256]{0:T(256)}, u32[]{:S(2)}) copy-start(s32[256]{0:T(256)} %param.9) | copy-start | bytes 3076
  8.7 0.7 %copy-start.4 = (s32[64]{0:T(128)S(1)}, s32[64]{0:T(128)}, u32[]{:S(2)}) copy-start(s32[64]{0:T(128)} %param.8) | copy-start | bytes 772
  9.4 1.0 %copy-start.1 = (s32[16,8192]{1,0:T(8,128)S(1)}, s32[16,8192]{1,0:T(8,128)}, u32[]{:S(2)}) copy-start(s32[16,8192]{1,0:T(8,128)} %lag_ref.1) | copy-start | bytes 1572868
  10.4 3.5 %copy-start.2 = (bf16[2,128,128]{2,1,0:T(8,128)(2,1)S(1)}, bf16[2,128,128]{2,1,0:T(8,128)(2,1)}, u32[]{:S(2)}) copy-start(bf16[2,128,128]{2,1,0:T(8,128)(2,1)} %get-tuple-element.33.refs_3_) | copy-start | bytes 196612
  14.7 10.8 %all-to-all-start = ((bf16[8,136,128]{2,1,0:T(8,128)(2,1)}), bf16[8,136,128]{2,1,0:T(8,128)(2,1)S(1)}, u32[]{:S(2)}, u32[]{:S(2)}) async-start(bf16[8,136,128]{2,1,0:T(8,128)(2,1)} %order_sources.1), calls=%async_computation | async-start | bytes 557056 | tf_op jit(solution)/shard_map/all_to_all | solution.py:584
  18.4 11.2 %collective-permute-start.3 = (bf16[272,256]{1,0:T(8,128)(2,1)S(1)}, bf16[272,256]{1,0:T(8,128)(2,1)S(1)}, u32[]{:S(2)}, u32[]{:S(2)}) collective-permute-start(bf16[272,256]{1,0:T(8,128)(2,1)S(1)} %get-tuple-element.34), channel_id=1, source_target_pairs={{0,3},{1,2},{2,1},{3,0},{4,7},{5,6},{6,5},{7,4},{8,11},{9,10},{10,... | collective-permute-start | bytes 417800 | tf_op jit(solution)/shard_map/ppermute | solution.py:564
  21.1 15.4 %collective-permute-start.6 = (bf16[272,256]{1,0:T(8,128)(2,1)S(1)}, bf16[272,256]{1,0:T(8,128)(2,1)S(1)}, u32[]{:S(2)}, u32[]{:S(2)}) collective-permute-start(bf16[272,256]{1,0:T(8,128)(2,1)S(1)} %get-tuple-element.40), channel_id=1, source_target_pairs={{0,2},{1,3},{2,0},{3,1},{4,6},{5,7},{6,4},{7,5},{8,10},{9,11},{10,... | collective-permute-start | bytes 417800 | tf_op jit(solution)/shard_map/ppermute | solution.py:564
  21.1 20.9 %collective-permute-start.5 = (bf16[272,256]{1,0:T(8,128)(2,1)S(1)}, bf16[272,256]{1,0:T(8,128)(2,1)S(1)}, u32[]{:S(2)}, u32[]{:S(2)}) collective-permute-start(bf16[272,256]{1,0:T(8,128)(2,1)S(1)} %get-tuple-element.38), channel_id=1, source_target_pairs={{0,1},{1,0},{2,3},{3,2},{4,5},{5,4},{6,7},{7,6},{8,9},{9,8},{10,11... | collective-permute-start | bytes 417800 | tf_op jit(solution)/shard_map/ppermute | solution.py:564
  33.8 8.2 %collective-permute-start.4 = (bf16[8,32,256]{2,1,0:T(8,128)(2,1)S(1)}, bf16[8,32,256]{2,1,0:T(8,128)(2,1)S(1)}, u32[]{:S(2)}, u32[]{:S(2)}) collective-permute-start(bf16[8,32,256]{2,1,0:T(8,128)(2,1)S(1)} %get-tuple-element.37), channel_id=1, source_target_pairs={{0,3},{1,2},{2,1},{3,0},{4,7},{5,6},{6,5},{7,4},{8,11},{9,10},{10,... | collective-permute-start | bytes 393224 | tf_op jit(solution)/shard_map/ppermute | solution.py:564
  40.9 8.0 %collective-permute-start.8 = (bf16[8,32,256]{2,1,0:T(8,128)(2,1)S(1)}, bf16[8,32,256]{2,1,0:T(8,128)(2,1)S(1)}, u32[]{:S(2)}, u32[]{:S(2)}) collective-permute-start(bf16[8,32,256]{2,1,0:T(8,128)(2,1)S(1)} %get-tuple-element.48), channel_id=1, source_target_pairs={{0,2},{1,3},{2,0},{3,1},{4,6},{5,7},{6,4},{7,5},{8,10},{9,11},{10,... | collective-permute-start | bytes 393224 | tf_op jit(solution)/shard_map/ppermute | solution.py:564
  48.9 13.4 %all-to-all-start.1 = ((bf16[32,32,128]{2,1,0:T(8,128)(2,1)}), bf16[32,32,128]{2,1,0:T(8,128)(2,1)S(1)}, u32[]{:S(2)}, u32[]{:S(2)}) async-start(bf16[32,32,128]{2,1,0:T(8,128)(2,1)} %get-tuple-element.50), calls=%async_computation.1 | async-start | bytes 524288 | tf_op jit(solution)/shard_map/all_to_all | solution.py:596
  52.0 9.9 %collective-permute-start.7 = (bf16[8,32,256]{2,1,0:T(8,128)(2,1)S(1)}, bf16[8,32,256]{2,1,0:T(8,128)(2,1)S(1)}, u32[]{:S(2)}, u32[]{:S(2)}) collective-permute-start(bf16[8,32,256]{2,1,0:T(8,128)(2,1)S(1)} %get-tuple-element.47), channel_id=1, source_target_pairs={{0,1},{1,0},{2,3},{3,2},{4,5},{5,4},{6,7},{7,6},{8,9},{9,8},{10,11... | collective-permute-start | bytes 393224 | tf_op jit(solution)/shard_map/ppermute | solution.py:564
